TPU v7x, 256 devices: a whole 4x4x8 slice. The times are simulated.
256 devices in a mesh: band: 8 (over x_lo, y), slab: 32 (over x_hi, z, core).
Axes of the slice: x: 4 (x_hi: 2, x_lo: 2; x = x_hi * 2 + x_lo), y: 4, z: 8, core: 2. Of those that a mesh axis runs over, the one named last changes fastest.
Arguments:
- resident: float32 [8, 192, 192, 192], P('band', 'slab'), may hold values from -6 to 6
- owned: float32 [8, 4, 192, 192, 192], P('band', None, 'slab'), may hold values from -6 to 6
- owner: int32 [2], replicated, may hold values from 0 to 7, as said below
Outputs:
- exchange: float32 [8, 192, 192, 192], P('band', 'slab')
Inputs may be any that keep to these rules, and one draw needn't show every extreme that they name: The owner groups of the 2 rounds are distinct, and group 7 owns one of the rounds.
All inputs are finite; a program needn't handle non-finite values.
Results may differ from a plain program's by a relative error of at most 0.0001.
Values sent between devices are 32-bit elements; how exact they have to be, the bound alone decides.
No kernel may reach another device: no remote copies, remote signals or barrier semaphores. Data moves between devices by JAX's collectives and lax.ppermute only.
A program may use at most 128 MiB of HBM per device.

v0:
```python
import math

import jax
import jax.numpy as jnp
from jax import lax
from jax.sharding import PartitionSpec as P

NB = 4
ROUNDS = 2


highest = lax.Precision.HIGHEST


def from_root(array, axis, root):
    mine = lax.axis_index(axis) == root
    return lax.psum(jnp.where(mine, array, jnp.zeros_like(array)), axis)


def cas_matrix(size):
    index = jnp.arange(size, dtype=jnp.int32)
    products = index[:, None] * index[None, :] % size
    phases = products.astype(jnp.float32) * (2.0 * math.pi / size)
    return jnp.cos(phases) + jnp.sin(phases)


def wavenumber(index, size):
    folded = jnp.minimum(index, size - index)
    return folded.astype(jnp.float32) * (2.0 * math.pi / size)


def forward_planes(field, cas):
    field = jnp.einsum("pabc,cz->pabz", field, cas, precision=highest)
    return jnp.einsum("pabc,by->payc", field, cas, precision=highest)


def inverse_planes(field, cas):
    field = jnp.einsum("pabc,by->payc", field, cas, precision=highest)
    return jnp.einsum("pabc,cz->pabz", field, cas, precision=highest)


def shards(resident, owned, owner):
    size = resident.shape[-1]
    slab_count = lax.axis_size("slab")
    col_count = size // slab_count
    cas = cas_matrix(size)
    orbital = resident[0]
    prefactor = -1.0 / math.sqrt(size * ROUNDS * NB)
    full_index = jnp.arange(size, dtype=jnp.int32)
    local_index = lax.axis_index("slab") * col_count + jnp.arange(col_count, dtype=jnp.int32)
    wave_full = wavenumber(full_index, size)
    wave_local = wavenumber(local_index, size)
    squared = (
        wave_full[:, None, None] ** 2
        + wave_local[None, :, None] ** 2
        + wave_full[None, None, :] ** 2
    )
    screen = (4.0 * math.pi / size) ** 2
    coulomb = 4.0 * math.pi / (squared + screen) / float(size) ** 3
    accumulated = jnp.zeros(orbital.shape, jnp.float32)
    for turn_index in range(ROUNDS):
        shared_bands = from_root(owned[0], "band", owner[turn_index])
        spectral = forward_planes(orbital[None] * shared_bands, cas)
        columns = lax.all_to_all(spectral, "slab", split_axis=2, concat_axis=1, tiled=True)
        columns = jnp.einsum("pabc,ax->pxbc", columns, cas, precision=highest)
        columns = columns * coulomb[None]
        columns = jnp.einsum("pabc,ax->pxbc", columns, cas, precision=highest)
        filtered = lax.all_to_all(columns, "slab", split_axis=1, concat_axis=2, tiled=True)
        weight = float(turn_index + 1)
        accumulated = accumulated + weight * jnp.sum(
            shared_bands * inverse_planes(filtered, cas), axis=0
        )
    return (accumulated * prefactor)[None]


def solution(mesh):
    placed = (P("band", "slab", None, None), P("band", None, "slab", None, None), P())
    return jax.shard_map(
        shards, mesh=mesh, in_specs=placed, out_specs=P("band", "slab", None, None), check_vma=False
    )
```

profile of v0, /device:TPU:1, one launch (start us, length us, event | category | flops | bytes accessed | tf_op | source)
XLA Modules:
  0.0 732.6 jit_solution(2043705897409326932)
XLA Ops:
  6.5 0.0 all-reduce.3.cloned.1.call-start
  6.5 1.3 fusion.95
  9.1 7.1 select_bitcast_fusion
  16.2 0.0 copy-start
  16.2 0.0 all-reduce.3.cloned.1.call-update
  16.3 213.6 %all-reduce.3.cloned.1.call-done = (f32[4,6,192,192]{3,2,1,0:T(8,128)}, f32[4,6,192,192]{3,2,1,0:T(8,128)}) async-done(((f32[4,6,192,192]{3,2,1,0:T(8,128)}, f32[4,6,192,192]{3,2,1,0:T(8,128)}), (f32[4,6,192,192]{3,2,1,0:T(8,128)}, f32[4,6,192,192]{3,2,1,0:T(8,128)})) %all-reduce.3.cloned.1.call-update) | async-done | bytes 7077904 | tf_op jit(solution)/shard_map/psum | solution.py:17
  229.8 0.0 copy-done
  229.8 7.0 fusion.20
  236.8 5.4 convolution_bitcast_fusion.1
  242.3 5.4 copy.45
  247.7 10.0 %all-to-all-start = ((f32[4,6,192,192]{3,0,1,2:T(4,128)}), f32[4,6,192,192]{3,0,1,2:T(4,128)}, u32[]{:S(2)}, u32[]{:S(2)}) async-start(f32[4,6,192,192]{3,0,1,2:T(4,128)} %copy.45), calls=%async_computation | async-start | bytes 9437184 | tf_op jit(solution)/shard_map/all_to_all | solution.py:64
  257.7 7.0 fusion.17
  264.7 5.4 convolution_bitcast_fusion
  270.1 15.1 %copy.56 = f32[4,6,192,192]{3,0,1,2:T(4,128)} copy(f32[4,6,192,192]{3,2,1,0:T(8,128)S(1)} %convolution_bitcast_fusion) | data formatting | bytes 7077888 | tf_op jit(solution)/shard_map/pabc,by->payc/transpose | solution.py:34
  285.2 79.8 %all-to-all-done = f32[4,6,192,192]{3,0,1,2:T(4,128)} async-done(((f32[4,6,192,192]{3,0,1,2:T(4,128)}), f32[4,6,192,192]{3,0,1,2:T(4,128)}, u32[]{:S(2)}, u32[]{:S(2)}) %all-to-all-start) | async-done | bytes 3538976 | tf_op jit(solution)/shard_map/all_to_all | solution.py:64
  365.1 7.6 %all-to-all-start.2 = ((f32[4,6,192,192]{3,0,1,2:T(4,128)}), f32[4,6,192,192]{3,0,1,2:T(4,128)}, u32[]{:S(2)}, u32[]{:S(2)}) async-start(f32[4,6,192,192]{3,0,1,2:T(4,128)} %copy.56), calls=%async_computation.2 | async-start | bytes 9437184 | tf_op jit(solution)/shard_map/all_to_all | solution.py:64
  372.7 0.1 broadcast_add_fusion
  372.8 0.3 divide_multiply_fusion
  373.1 3.1 copy.47
  376.2 6.1 fusion.14
  382.4 5.7 fusion.26
  388.1 5.2 copy.51
  393.4 86.7 %all-to-all-done.2 = f32[4,6,192,192]{3,0,1,2:T(4,128)} async-done(((f32[4,6,192,192]{3,0,1,2:T(4,128)}), f32[4,6,192,192]{3,0,1,2:T(4,128)}, u32[]{:S(2)}, u32[]{:S(2)}) %all-to-all-start.2) | async-done | bytes 3538976 | tf_op jit(solution)/shard_map/all_to_all | solution.py:64
  480.1 7.6 %all-to-all-start.1 = ((f32[4,192,6,192]{3,0,2,1:T(4,128)}), f32[4,192,6,192]{3,0,2,1:T(4,128)}, u32[]{:S(2)}, u32[]{:S(2)}) async-start(f32[4,192,6,192]{3,0,2,1:T(4,128)} %copy.51), calls=%async_computation.1 | async-start | bytes 9437184 | tf_op jit(solution)/shard_map/all_to_all | solution.py:68
  487.7 3.1 copy.58
  490.9 6.1 fusion.10
  497.0 5.5 fusion.31
  502.5 5.2 copy.62
  507.7 87.4 %all-to-all-done.1 = f32[4,192,6,192]{3,0,2,1:T(4,128)} async-done(((f32[4,192,6,192]{3,0,2,1:T(4,128)}), f32[4,192,6,192]{3,0,2,1:T(4,128)}, u32[]{:S(2)}, u32[]{:S(2)}) %all-to-all-start.1) | async-done | bytes 3538976 | tf_op jit(solution)/shard_map/all_to_all | solution.py:68
  595.1 7.6 %all-to-all-start.3 = ((f32[4,192,6,192]{3,0,2,1:T(4,128)}), f32[4,192,6,192]{3,0,2,1:T(4,128)}, u32[]{:S(2)}, u32[]{:S(2)}) async-start(f32[4,192,6,192]{3,0,2,1:T(4,128)} %copy.62), calls=%async_computation.3 | async-start | bytes 9437184 | tf_op jit(solution)/shard_map/all_to_all | solution.py:68
  602.7 0.0 slice-start.2
  602.7 3.4 copy.52
  606.1 0.0 slice-start.3
  606.1 5.7 fusion.12
  611.8 0.0 slice-done.2
  611.8 0.0 slice-done.3
  611.8 4.8 multiply_reduce_fusion.1
  616.7 93.4 %all-to-all-done.3 = f32[4,192,6,192]{3,0,2,1:T(4,128)} async-done(((f32[4,192,6,192]{3,0,2,1:T(4,128)}), f32[4,192,6,192]{3,0,2,1:T(4,128)}, u32[]{:S(2)}, u32[]{:S(2)}) %all-to-all-start.3) | async-done | bytes 3538976 | tf_op jit(solution)/shard_map/all_to_all | solution.py:68
  710.1 0.0 slice-start
  710.1 3.4 copy.63
  713.7 0.0 slice-start.1
  713.7 5.7 fusion.8
  719.4 0.0 slice-done
  719.4 0.0 slice-done.1
  719.4 4.8 multiply_reduce_fusion
  724.2 1.2 multiply_bitcast_fusion
  (4 shorter events, 0.0 us)
Async XLA Ops:
  6.5 223.3 %all-reduce.3.cloned.1.call-start = ((), (), s32[]{:S(2)}) async-start(), calls=%async_computation.4 | async-start | bytes 18874368 | tf_op jit(solution)/shard_map/psum | solution.py:17
  16.2 213.6 %copy-start = (f32[1,6,192,192]{3,2,1,0:T(8,128)S(1)}, f32[1,6,192,192]{3,2,1,0:T(8,128)}, u32[]{:S(2)}) copy-start(f32[1,6,192,192]{3,2,1,0:T(8,128)} %param.3) | copy-start | bytes 2654212
  247.7 117.4 %all-to-all-start = ((f32[4,6,192,192]{3,0,1,2:T(4,128)}), f32[4,6,192,192]{3,0,1,2:T(4,128)}, u32[]{:S(2)}, u32[]{:S(2)}) async-start(f32[4,6,192,192]{3,0,1,2:T(4,128)} %copy.45), calls=%async_computation | async-start | bytes 9437184 | tf_op jit(solution)/shard_map/all_to_all | solution.py:64
  365.1 115.0 %all-to-all-start.2 = ((f32[4,6,192,192]{3,0,1,2:T(4,128)}), f32[4,6,192,192]{3,0,1,2:T(4,128)}, u32[]{:S(2)}, u32[]{:S(2)}) async-start(f32[4,6,192,192]{3,0,1,2:T(4,128)} %copy.56), calls=%async_computation.2 | async-start | bytes 9437184 | tf_op jit(solution)/shard_map/all_to_all | solution.py:64
  480.1 115.0 %all-to-all-start.1 = ((f32[4,192,6,192]{3,0,2,1:T(4,128)}), f32[4,192,6,192]{3,0,2,1:T(4,128)}, u32[]{:S(2)}, u32[]{:S(2)}) async-start(f32[4,192,6,192]{3,0,2,1:T(4,128)} %copy.51), calls=%async_computation.1 | async-start | bytes 9437184 | tf_op jit(solution)/shard_map/all_to_all | solution.py:68
  595.1 115.0 %all-to-all-start.3 = ((f32[4,192,6,192]{3,0,2,1:T(4,128)}), f32[4,192,6,192]{3,0,2,1:T(4,128)}, u32[]{:S(2)}, u32[]{:S(2)}) async-start(f32[4,192,6,192]{3,0,2,1:T(4,128)} %copy.62), calls=%async_computation.3 | async-start | bytes 9437184 | tf_op jit(solution)/shard_map/all_to_all | solution.py:68
  602.7 9.1 %slice-start.2 = ((s8[4718592]{0:T(1024)(128)(4,1)}), s8[4194304]{0:T(1024)(128)(4,1)S(1)}, s32[]{:S(2)}) async-start(s8[4718592]{0:T(1024)(128)(4,1)} %bitcast.96), calls=%async_computation.7 | async-start | bytes 8388608
  606.1 5.7 slice-start.3
  710.1 9.3 %slice-start = ((s8[4718592]{0:T(1024)(128)(4,1)}), s8[4194304]{0:T(1024)(128)(4,1)S(1)}, s32[]{:S(2)}) async-start(s8[4718592]{0:T(1024)(128)(4,1)} %bitcast.94), calls=%async_computation.5 | async-start | bytes 8388608
  713.7 5.7 slice-start.1
Sparse Core Ops, SparseCore 0:
  16.4 213.3 all-reduce.2
where the time goes:
time: 742 us; the launch traced here: 733 us
  waiting for transfers between devices  561 us (76%)
  matrix products  69.4 us (9%)
  local copies, waits for them, and re-layouts  45.3 us (6%)
  starting transfers between devices  32.9 us (4%)
  between operations  15.5 us (2%)
  other arithmetic  8.66 us (1%)
    psum x1, waiting for transfers between devices, from_root(): return lax.psum(jnp.where(mine, array, jnp.zeros_like(array)), axis)  214 us
    all_to_all x2, waiting for transfers between devices, shards(): lax.all_to_all(columns, 'slab', split_axis=1, concat_axis=2, tiled=True)  181 us
    all_to_all x2, waiting for transfers between devices, shards(): lax.all_to_all(spectral, 'slab', split_axis=2, concat_axis=1, tiled=True)  167 us
    dot_general x4, matrix products, shards(): columns = jnp.einsum('pabc,ax->pxbc', columns, cas, precision=highest)  23.5 us
    transpose x2, local copies, waits for them, and re-layouts, forward_planes(): return jnp.einsum('pabc,by->payc', field, cas, precision=highest)  20.5 us
    all_to_all x2, starting transfers between devices, shards(): lax.all_to_all(spectral, 'slab', split_axis=2, concat_axis=1, tiled=True)  17.6 us
    all_to_all x2, starting transfers between devices, shards(): lax.all_to_all(columns, 'slab', split_axis=1, concat_axis=2, tiled=True)  15.3 us
  transfers between devices with their start and end apart: 5, of which 5 were waited for; matrix products, arithmetic and copies ran while one was open for 11% of the time, Pallas kernels for 0%

commit v1 on v0

v1 whole, which is shorter than its diff:
```python
import math

import jax
import jax.numpy as jnp
import numpy as np
from jax import lax
from jax.sharding import Mesh, PartitionSpec as P

N = 192
PLANE = ("x_lo", "y", "x_hi", "core")
high = lax.Precision.HIGH


def cas_matrix(size):
    index = np.arange(size)
    phases = (index[:, None] * index[None, :] % size) * (2.0 * math.pi / size)
    return (np.cos(phases) + np.sin(phases)).astype(np.float32)


def coulomb_grid(size):
    index = np.arange(size)
    wave = np.minimum(index, size - index) * (2.0 * math.pi / size)
    squared = wave[:, None, None] ** 2 + wave[None, :, None] ** 2 + wave[None, None, :] ** 2
    return squared


def held_order():
    z, x_hi, core, row = np.meshgrid(np.arange(8), np.arange(2), np.arange(2), np.arange(6), indexing="ij")
    return (6 * (x_hi * 16 + z * 2 + core) + row).reshape(-1)


def wavenumber(index):
    folded = jnp.minimum(index, N - index)
    return folded.astype(jnp.float32) * (2.0 * math.pi / N)


def exchange_plane(blocks):
    return lax.all_to_all(blocks, PLANE, 0, 0, tiled=True)


def exchange_z(blocks):
    return lax.all_to_all(blocks, "z", 0, 0, tiled=True)


def to_blocks(planes):
    count = planes.shape[0]
    blocks = planes.reshape(count, 6, 32, 6, N).transpose(2, 0, 1, 3, 4)
    return blocks.reshape(32, count * 54, 128)


def shards(resident, owned, owner):
    cas = jnp.asarray(cas_matrix(N))
    cas_held = jnp.asarray(cas_matrix(N)[:, held_order()])
    place = lax.axis_index(PLANE)
    pair_wave = wavenumber((place % 8) * 24 + jnp.arange(24, dtype=jnp.int32))
    wave = wavenumber(jnp.arange(N, dtype=jnp.int32))
    squared = pair_wave[:, None, None] ** 2 + wave[None, :, None] ** 2 + wave[None, None, :] ** 2
    screen = (4.0 * math.pi / N) ** 2
    coulomb = 4.0 * math.pi / (squared + screen) / float(N) ** 3

    orbital = exchange_z(exchange_plane(to_blocks(resident)).reshape(8, 216, 128))
    orbital = orbital.reshape(N, 6, N)
    accumulated = jnp.zeros((N, 6, N), jnp.float32)
    weights = -1.0 / math.sqrt(N * 8) * jnp.array([1.0, 1.0, 2.0, 2.0], jnp.float32)
    halves = []
    for half in range(2):
        part = owned[0, 2 * half : 2 * half + 2]
        spread = exchange_plane(to_blocks(part)).reshape(8, 4, 2, 6, 6 * N)
        chosen = jnp.take(spread, owner, axis=0, mode="clip")
        chosen = chosen.transpose(0, 2, 1, 3, 4).reshape(4, 24, 6 * N)
        bands = lax.all_gather(chosen, "z", axis=0, tiled=False)
        halves.append(bands.transpose(1, 0, 2, 3).reshape(4, N, 6, N))
    spectra = []
    for bands in halves:
        pairs = orbital[None] * bands
        pairs = jnp.einsum("paic,ck->paik", pairs, cas, precision=high)
        pairs = jnp.einsum("paic,ka->pkic", pairs, cas_held, precision=high)
        spectra.append(exchange_plane(pairs.reshape(32, 24, 6 * N)))
    filtered = []
    for columns in spectra:
        columns = columns.reshape(32, 24, 6, N)
        matrix = cas.reshape(32, 6, N)
        columns = jnp.einsum("sakc,skb->abc", columns, matrix, precision=high)
        columns = columns * coulomb
        columns = jnp.einsum("abc,skb->sakc", columns, matrix, precision=high)
        filtered.append(exchange_plane(columns.reshape(32, 24, 6 * N)))
    for bands, potential in zip(halves, filtered):
        potential = potential.reshape(4, N, 6, N)
        potential = jnp.einsum("pkic,ka->paic", potential, cas_held, precision=high)
        potential = jnp.einsum("paic,ck->paik", potential, cas, precision=high)
        accumulated = accumulated + jnp.sum(weights[:, None, None, None] * bands * potential, axis=0)
    back = exchange_z(accumulated.reshape(8, 216, 128))
    back = exchange_plane(back.reshape(32, 54, 128))
    return back.reshape(32, 6, 6, N).transpose(1, 0, 2, 3).reshape(1, 6, N, N)


def solution(mesh):
    fine = Mesh(mesh.devices.reshape(2, 4, 2, 8, 2), ("x_lo", "y", "x_hi", "z", "core"))
    band, slab = ("x_lo", "y"), ("x_hi", "z", "core")
    return jax.shard_map(
        shards,
        mesh=fine,
        in_specs=(P(band, slab), P(band, None, slab), P()),
        out_specs=P(band, slab),
        check_vma=False,
    )
```

time: 742 us -> 537 us (0.72)
  waiting for transfers between devices: 561 us -> 117 us
  blocking collectives: 0 us -> 143 us
  local copies, waits for them, and re-layouts: 45.3 us -> 127 us
  matrix products: 69.4 us -> 79.2 us
    all_to_all x4 -> x5, waiting for transfers between devices: 347 us -> 110 us  [exchange_plane(): return lax.all_to_all(blocks, PLANE, 0, 0, tiled=True)]
    psum x1 -> x0, waiting for transfers between devices: 214 us -> none  [from_root(): return lax.psum(jnp.where(mine, array, jnp.zeros_like(array)), axis)]
    all_to_all x0 -> x5, blocking collectives: none -> 143 us  [the longest x3 73.9 us: exchange_plane(): return lax.all_to_all(blocks, PLANE, 0, 0, tiled=True)]
    reshape x0 -> x20, local copies, waits for them, and re-layouts: none -> 75.1 us  [the longest x2 13.3 us: shards(): potential = potential.reshape(4, N, 6, N)]
    all_to_all x4 -> x0, local copies, waits for them, and re-layouts: 13 us -> none  [the longest x2 6.71 us: shards(): lax.all_to_all(columns, 'slab', split_axis=1, concat_axis=2, tiled=True)]
    dot_general x12, matrix products: 69.4 us -> 79.2 us  [the longest x2 18.1 us: shards(): columns = jnp.einsum('sakc,skb->abc', columns, matrix, precision=high)]
    mul x1, other arithmetic: 1.17 us -> 10.8 us  [shards(): pairs = orbital[None] * bands]
    all_to_all x4 -> x5, starting transfers between devices: 32.9 us -> 35.2 us  [exchange_plane(): return lax.all_to_all(blocks, PLANE, 0, 0, tiled=True)]
  transfers between devices with their start and end apart: 5 -> 7, of which waited for: 5 -> 6; matrix products, arithmetic and copies ran while one was open for 11% -> 22% of each run, Pallas kernels for 0% -> 0%
where the time goes in v1:
time: 537 us; the launch traced here: 527 us
  blocking collectives  143 us (27%)
  local copies, waits for them, and re-layouts  127 us (24%)
  waiting for transfers between devices  117 us (22%)
  matrix products  79.2 us (15%)
  starting transfers between devices  35.3 us (7%)
  between operations  14.3 us (3%)
  other arithmetic  11.7 us (2%)
    all_to_all x5, waiting for transfers between devices, exchange_plane(): return lax.all_to_all(blocks, PLANE, 0, 0, tiled=True)  110 us
    all_to_all x3, blocking collectives, exchange_plane(): return lax.all_to_all(blocks, PLANE, 0, 0, tiled=True)  73.9 us
    all_to_all x2, blocking collectives, exchange_z(): return lax.all_to_all(blocks, 'z', 0, 0, tiled=True)  69.6 us
    all_to_all x5, starting transfers between devices, exchange_plane(): return lax.all_to_all(blocks, PLANE, 0, 0, tiled=True)  35.2 us
    dot_general x2, matrix products, shards(): columns = jnp.einsum('sakc,skb->abc', columns, matrix, precision=high)  18.1 us
    dot_general x2, matrix products, shards(): potential = jnp.einsum('pkic,ka->paic', potential, cas_held, precision=high)  17.7 us
    dot_general x2, matrix products, shards(): potential = jnp.einsum('paic,ck->paik', potential, cas, precision=high)  16 us
    transpose x2, local copies, waits for them, and re-layouts, shards(): pairs = jnp.einsum('paic,ka->pkic', pairs, cas_held, precision=high)  13.4 us
  transfers between devices with their start and end apart: 7, of which 6 were waited for; matrix products, arithmetic and copies ran while one was open for 22% of the time, Pallas kernels for 0%

profile of v1, /device:TPU:1, one launch (start us, length us, event | category | flops | bytes accessed | tf_op | source)
XLA Modules:
  0.0 527.2 jit_solution(9553313124055328877)
XLA Ops:
  6.5 4.2 fusion.56
  15.4 8.6 %all-to-all-start.5 = ((f32[32,108,128]{2,1,0:T(8,128)}), f32[32,108,128]{2,1,0:T(8,128)}, u32[]{:S(2)}, u32[]{:S(2)}) async-start(f32[32,108,128]{2,1,0:T(8,128)} %reshape.143), calls=%async_computation.5 | async-start | bytes 3670016 | tf_op jit(solution)/shard_map/all_to_all | solution.py:38
  24.2 25.6 %all-to-all-done.5 = f32[32,108,128]{2,1,0:T(8,128)} async-done(((f32[32,108,128]{2,1,0:T(8,128)}), f32[32,108,128]{2,1,0:T(8,128)}, u32[]{:S(2)}, u32[]{:S(2)}) %all-to-all-start.5) | async-done | bytes 1769504 | tf_op jit(solution)/shard_map/all_to_all | solution.py:38
  49.8 2.8 reshape.144
  58.1 2.4 reshape.132
  60.5 30.1 %all_to_all.50 = f32[32,108,128]{2,1,0:T(8,128)S(1)} all-to-all(f32[32,108,128]{2,1,0:T(8,128)} %reshape.132), channel_id=1, replica_groups=mesh['x_lo'=2,'y'=4,'x_hi'=2,'z'=8,'core'=2] {'x_lo','y','x_hi','core'}, dimensions={0} | all-to-all | bytes 3538944 | tf_op jit(solution)/shard_map/all_to_all | solution.py:38
  95.4 2.7 reshape.135
  99.0 19.3 %all_to_all.51 = f32[32,54,128]{2,1,0:T(8,128)S(1)} all-to-all(f32[32,54,128]{2,1,0:T(8,128)S(1)} %reshape.136), channel_id=1, replica_groups=mesh['x_lo'=2,'y'=4,'x_hi'=2,'z'=8,'core'=2] {'x_lo','y','x_hi','core'}, dimensions={0} | all-to-all | bytes 1769472 | tf_op jit(solution)/shard_map/all_to_all | solution.py:38
  118.4 43.1 %all_to_all.52 = f32[8,216,128]{2,1,0:T(8,128)S(1)} all-to-all(f32[8,216,128]{2,1,0:T(8,128)S(1)} %reshape.137), channel_id=1, replica_groups=mesh['x_lo'=2,'y'=4,'x_hi'=2,'z'=8,'core'=2] {'z'}, dimensions={0} | all-to-all | bytes 1769472 | tf_op jit(solution)/shard_map/all_to_all | solution.py:42
  165.4 7.0 %all-gather.3.cloned.1.call-done = f32[8,4,24,1152]{3,2,1,0:T(8,128)} async-done(((f32[1,4,24,1152]{3,2,1,0:T(8,128)}), f32[8,4,24,1152]{3,2,1,0:T(8,128)}) %all-gather.3.cloned.1.call-update) | async-done | bytes 3538960 | tf_op jit(solution)/shard_map/all_gather | solution.py:71
  172.4 4.1 copy.27
  176.5 6.5 %reshape.134 = f32[4,192,6,192]{3,2,1,0:T(8,128)} reshape(f32[4,8,24,1152]{3,2,1,0:T(8,128)} %copy.27) | data formatting | bytes 7077888 | tf_op jit(solution)/shard_map/reshape | solution.py:72
  183.0 4.2 reshape.145
  187.2 10.8 %broadcast_multiply_fusion = (f32[4,192,6,192]{3,2,1,0:T(8,128)}, f32[4,192,6,192]{3,2,1,0:T(8,128)}) fusion(f32[4,192,6,192]{3,2,1,0:T(8,128)} %reshape.145, f32[192,6,192]{2,1,0:T(8,128)} %mul.83, f32[4,192,6,192]{3,2,1,0:T(8,128)} %reshape.134), kind=kLoop, calls=%fused_computation.31 | loop fusion | flops 1769472 | bytes 15040512 | tf_op jit(solution)/shard_map/mul | solution.py:75
  198.0 6.2 %fusion.12 = f32[4,192,6,192]{1,3,2,0:T(8,128)S(1)} fusion(f32[192,192,1,1]{1,0,3,2:T(8,128)S(1)} %copy-done.3, f32[4,192,6,192]{3,2,1,0:T(8,128)} %get-tuple-element.7), kind=kOutput, calls=%fused_computation.16 | convolution fusion | flops 1019215872 | bytes 7225344 | tf_op jit(solution)/shard_map/paic,ck->paik/dot_general | solution.py:76
  204.2 4.3 convolution_bitcast_fusion
  208.5 6.7 %copy.46 = f32[4,192,6,192]{3,2,1,0:T(8,128)} copy(f32[4,192,6,192]{1,3,2,0:T(8,128)} %convolution_bitcast_fusion) | data formatting | bytes 7077888 | tf_op jit(solution)/shard_map/paic,ka->pkic/transpose | solution.py:77
  215.2 6.4 %reshape.146 = f32[32,24,1152]{2,1,0:T(8,128)} reshape(f32[4,192,6,192]{3,2,1,0:T(8,128)} %copy.46) | data formatting | bytes 7077888 | tf_op jit(solution)/shard_map/reshape | solution.py:78
  221.7 7.8 %all-to-all-start.6 = ((f32[32,24,1152]{2,1,0:T(8,128)}), f32[32,24,1152]{2,1,0:T(8,128)S(1)}, u32[]{:S(2)}, u32[]{:S(2)}) async-start(f32[32,24,1152]{2,1,0:T(8,128)} %reshape.146), calls=%async_computation.6 | async-start | bytes 7077888 | tf_op jit(solution)/shard_map/all_to_all | solution.py:38
  229.5 6.2 %fusion.20 = f32[4,192,6,192]{1,3,2,0:T(8,128)S(1)} fusion(f32[192,192,1,1]{1,0,3,2:T(8,128)} %constant.69, f32[4,192,6,192]{3,2,1,0:T(8,128)} %get-tuple-element.8), kind=kOutput, calls=%fused_computation.25 | convolution fusion | flops 1019215872 | bytes 7225344 | tf_op jit(solution)/shard_map/paic,ck->paik/dot_general | solution.py:76
  235.7 4.2 convolution_bitcast_fusion.1
  239.9 6.7 %copy.32 = f32[4,192,6,192]{3,2,1,0:T(8,128)} copy(f32[4,192,6,192]{1,3,2,0:T(8,128)} %convolution_bitcast_fusion.1) | data formatting | bytes 7077888 | tf_op jit(solution)/shard_map/paic,ka->pkic/transpose | solution.py:77
  246.6 6.5 %reshape.138 = f32[32,24,1152]{2,1,0:T(8,128)} reshape(f32[4,192,6,192]{3,2,1,0:T(8,128)} %copy.32) | data formatting | bytes 7077888 | tf_op jit(solution)/shard_map/reshape | solution.py:78
  253.1 22.7 %all-to-all-done.6 = f32[32,24,1152]{2,1,0:T(8,128)S(1)} async-done(((f32[32,24,1152]{2,1,0:T(8,128)}), f32[32,24,1152]{2,1,0:T(8,128)S(1)}, u32[]{:S(2)}, u32[]{:S(2)}) %all-to-all-start.6) | async-done | bytes 3538976 | tf_op jit(solution)/shard_map/all_to_all | solution.py:38
  277.7 6.0 %all-to-all-start.3 = ((f32[32,24,1152]{2,1,0:T(8,128)}), f32[32,24,1152]{2,1,0:T(8,128)S(1)}, u32[]{:S(2)}, u32[]{:S(2)}) async-start(f32[32,24,1152]{2,1,0:T(8,128)} %reshape.138), calls=%async_computation.3 | async-start | bytes 7077888 | tf_op jit(solution)/shard_map/all_to_all | solution.py:38
  284.4 6.6 %reshape.147 = f32[32,24,6,192]{3,2,1,0:T(8,128)} reshape(f32[32,24,1152]{2,1,0:T(8,128)} %copy-done.1) | data formatting | bytes 7077888 | tf_op jit(solution)/shard_map/reshape | solution.py:81
  291.0 9.0 %fusion.10 = f32[24,192,192,1]{2,1,3,0:T(8,128)S(1)} fusion(f32[32,6,192,1]{2,0,1,3:T(8,128)} %constant.71, f32[32,24,6,192]{3,2,1,0:T(8,128)} %reshape.147), kind=kOutput, calls=%fused_computation.14 | convolution fusion | flops 1019215872 | bytes 7225344 | tf_op jit(solution)/shard_map/sakc,skb->abc/dot_general | solution.py:83
  300.1 3.3 fusion.37
  303.4 5.8 %copy.49 = f32[32,24,6,192]{3,2,1,0:T(8,128)} copy(f32[32,24,6,192]{3,0,2,1:T(8,128)S(1)} %fusion.37) | data formatting | bytes 7077888 | tf_op jit(solution)/shard_map/abc,skb->sakc/transpose | solution.py:85
  309.2 6.6 %reshape.148 = f32[32,24,1152]{2,1,0:T(8,128)} reshape(f32[32,24,6,192]{3,2,1,0:T(8,128)} %copy.49) | data formatting | bytes 7077888 | tf_op jit(solution)/shard_map/reshape | solution.py:86
  315.8 13.9 %all-to-all-done.3 = f32[32,24,1152]{2,1,0:T(8,128)S(1)} async-done(((f32[32,24,1152]{2,1,0:T(8,128)}), f32[32,24,1152]{2,1,0:T(8,128)S(1)}, u32[]{:S(2)}, u32[]{:S(2)}) %all-to-all-start.3) | async-done | bytes 3538976 | tf_op jit(solution)/shard_map/all_to_all | solution.py:38
  329.7 6.4 %all-to-all-start.7 = ((f32[32,24,1152]{2,1,0:T(8,128)}), f32[32,24,1152]{2,1,0:T(8,128)}, u32[]{:S(2)}, u32[]{:S(2)}) async-start(f32[32,24,1152]{2,1,0:T(8,128)} %reshape.148), calls=%async_computation.7 | async-start | bytes 7077888 | tf_op jit(solution)/shard_map/all_to_all | solution.py:38
  336.1 4.1 reshape.139
  340.2 9.0 %fusion.18 = f32[24,192,192,1]{2,1,3,0:T(8,128)S(1)} fusion(f32[32,6,192,1]{2,0,1,3:T(8,128)} %constant.71, f32[32,24,6,192]{3,2,1,0:T(8,128)} %reshape.139), kind=kOutput, calls=%fused_computation.23 | convolution fusion | flops 1019215872 | bytes 7225344 | tf_op jit(solution)/shard_map/sakc,skb->abc/dot_general | solution.py:83
  349.3 3.3 fusion.34
  352.6 5.6 %copy.35 = f32[32,24,6,192]{3,2,1,0:T(8,128)} copy(f32[32,24,6,192]{3,0,2,1:T(8,128)S(1)} %fusion.34) | data formatting | bytes 7077888 | tf_op jit(solution)/shard_map/abc,skb->sakc/transpose | solution.py:85
  358.2 6.5 %reshape.141 = f32[32,24,1152]{2,1,0:T(8,128)} reshape(f32[32,24,6,192]{3,2,1,0:T(8,128)} %copy.35) | data formatting | bytes 7077888 | tf_op jit(solution)/shard_map/reshape | solution.py:86
  364.7 17.5 %all-to-all-done.7 = f32[32,24,1152]{2,1,0:T(8,128)} async-done(((f32[32,24,1152]{2,1,0:T(8,128)}), f32[32,24,1152]{2,1,0:T(8,128)}, u32[]{:S(2)}, u32[]{:S(2)}) %all-to-all-start.7) | async-done | bytes 3538976 | tf_op jit(solution)/shard_map/all_to_all | solution.py:38
  382.2 6.4 %all-to-all-start.4 = ((f32[32,24,1152]{2,1,0:T(8,128)}), f32[32,24,1152]{2,1,0:T(8,128)}, u32[]{:S(2)}, u32[]{:S(2)}) async-start(f32[32,24,1152]{2,1,0:T(8,128)} %reshape.141), calls=%async_computation.4 | async-start | bytes 7077888 | tf_op jit(solution)/shard_map/all_to_all | solution.py:38
  388.6 6.5 %reshape.149 = f32[4,192,6,192]{3,2,1,0:T(8,128)} reshape(f32[32,24,1152]{2,1,0:T(8,128)} %all-to-all-done.7) | data formatting | bytes 7077888 | tf_op jit(solution)/shard_map/reshape | solution.py:88
  395.1 9.8 %fusion.8 = f32[4,6,192,192]{3,2,1,0:T(8,128)} fusion(f32[192,192,1,1]{1,0,3,2:T(8,128)S(1)} %copy-done.7, f32[4,192,6,192]{3,2,1,0:T(8,128)} %reshape.149), kind=kOutput, calls=%fused_computation.12 | convolution fusion | flops 1019215872 | bytes 7225344 | tf_op jit(solution)/shard_map/pkic,ka->paic/dot_general | solution.py:89
  404.9 29.8 %all-to-all-done.4 = f32[32,24,1152]{2,1,0:T(8,128)} async-done(((f32[32,24,1152]{2,1,0:T(8,128)}), f32[32,24,1152]{2,1,0:T(8,128)}, u32[]{:S(2)}, u32[]{:S(2)}) %all-to-all-start.4) | async-done | bytes 3538976 | tf_op jit(solution)/shard_map/all_to_all | solution.py:38
  434.7 6.8 %reshape.142 = f32[4,192,6,192]{3,2,1,0:T(8,128)} reshape(f32[32,24,1152]{2,1,0:T(8,128)} %all-to-all-done.4) | data formatting | bytes 7077888 | tf_op jit(solution)/shard_map/reshape | solution.py:88
  441.6 7.9 %fusion.16 = f32[4,6,192,192]{3,2,1,0:T(8,128)S(1)} fusion(f32[192,192,1,1]{1,0,3,2:T(8,128)S(1)} %copy-done.7, f32[4,192,6,192]{3,2,1,0:T(8,128)} %reshape.142), kind=kOutput, calls=%fused_computation.21 | convolution fusion | flops 1019215872 | bytes 7225344 | tf_op jit(solution)/shard_map/pkic,ka->paic/dot_general | solution.py:89
  449.5 9.5 %fusion.15 = f32[192,6,192]{2,0,1:T(8,128)S(1)} fusion(f32[4,192,6,192]{3,2,1,0:T(8,128)} %reshape.145, f32[4]{0:T(128)S(1)} %copy-done.10, f32[192,192,1,1]{1,0,3,2:T(8,128)S(1)} %copy-done.4, f32[4,6,192,192]{3,2,1,0:T(8,128)S(1)} %copy-done), kind=kOutput, calls=%fused_computation.20 | convolution fusion | flops 1021648896 | bytes 8110096 | tf_op jit(solution)/shard_map/paic,ck->paik/dot_general | solution.py:90
  459.0 6.5 %fusion.23 = f32[192,6,192]{2,0,1:T(8,128)S(1)} fusion(f32[4,192,6,192]{3,2,1,0:T(8,128)S(1)} %bitcast.94, f32[4]{0:T(128)S(1)} %copy-done.10, f32[192,192,1,1]{1,0,3,2:T(8,128)S(1)} %copy-done.4, f32[4,6,192,192]{3,2,1,0:T(8,128)S(1)} %fusion.16), kind=kOutput, calls=%fused_computation.29 | convolution fusion | flops 1021648896 | bytes 8110096 | tf_op jit(solution)/shard_map/paic,ck->paik/dot_general | solution.py:90
  467.1 26.5 %all_to_all.53 = f32[8,216,128]{2,1,0:T(8,128)S(1)} all-to-all(f32[8,216,128]{2,1,0:T(8,128)S(1)} %add.82), channel_id=1, replica_groups=mesh['x_lo'=2,'y'=4,'x_hi'=2,'z'=8,'core'=2] {'z'}, dimensions={0} | all-to-all | bytes 1769472 | tf_op jit(solution)/shard_map/all_to_all | solution.py:42
  493.7 24.5 %all_to_all.54 = f32[32,54,128]{2,1,0:T(8,128)S(1)} all-to-all(f32[32,54,128]{2,1,0:T(8,128)S(1)} %reshape.150), channel_id=1, replica_groups=mesh['x_lo'=2,'y'=4,'x_hi'=2,'z'=8,'core'=2] {'x_lo','y','x_hi','core'}, dimensions={0} | all-to-all | bytes 1769472 | tf_op jit(solution)/shard_map/all_to_all | solution.py:38
  (66 shorter events, 25.8 us)
Async XLA Ops:
  13.1 11.1 %copy-start.11 = (s32[2]{0:T(128)S(1)}, s32[2]{0:T(128)}, u32[]{:S(2)}) copy-start(s32[2]{0:T(128)} %param.8) | copy-start | bytes 28
  15.4 34.3 %all-to-all-start.5 = ((f32[32,108,128]{2,1,0:T(8,128)}), f32[32,108,128]{2,1,0:T(8,128)}, u32[]{:S(2)}, u32[]{:S(2)}) async-start(f32[32,108,128]{2,1,0:T(8,128)} %reshape.143), calls=%async_computation.5 | async-start | bytes 3670016 | tf_op jit(solution)/shard_map/all_to_all | solution.py:38
  24.1 31.7 %copy-start.2 = (f32[1,2,6,192,192]{4,3,2,1,0:T(8,128)S(1)}, f32[1,2,6,192,192]{4,3,2,1,0:T(8,128)}, u32[]{:S(2)}) copy-start(f32[1,2,6,192,192]{4,3,2,1,0:T(8,128)} %get-tuple-element.6) | copy-start | bytes 5308420
  24.1 139.0 %all-gather.5.cloned.1.call-start = ((), (), s32[]{:S(2)}) async-start(), calls=%async_computation.11 | async-start | bytes 3981312 | tf_op jit(solution)/shard_map/all_gather | solution.py:71
  55.7 116.7 %all-gather.3.cloned.1.call-start = ((), (), s32[]{:S(2)}) async-start(), calls=%async_computation.10 | async-start | bytes 3981312 | tf_op jit(solution)/shard_map/all_gather | solution.py:71
  187.2 10.8 %copy-start.3 = (f32[192,192,1,1]{1,0,3,2:T(8,128)S(1)}, f32[192,192,1,1]{1,0,3,2:T(8,128)}, u32[]{:S(2)}) copy-start(f32[192,192,1,1]{1,0,3,2:T(8,128)} %constant.69) | copy-start | bytes 442372
  198.0 6.2 %copy-start.5 = (f32[192,192,1,1]{1,0,3,2:T(8,128)S(1)}, f32[192,192,1,1]{1,0,3,2:T(8,128)}, u32[]{:S(2)}) copy-start(f32[192,192,1,1]{1,0,3,2:T(8,128)} %constant.70) | copy-start | bytes 442372
  221.7 54.2 %all-to-all-start.6 = ((f32[32,24,1152]{2,1,0:T(8,128)}), f32[32,24,1152]{2,1,0:T(8,128)S(1)}, u32[]{:S(2)}, u32[]{:S(2)}) async-start(f32[32,24,1152]{2,1,0:T(8,128)} %reshape.146), calls=%async_computation.6 | async-start | bytes 7077888 | tf_op jit(solution)/shard_map/all_to_all | solution.py:38
  229.5 6.2 %copy-start.6 = (f32[192,192,1,1]{1,0,3,2:T(8,128)S(1)}, f32[192,192,1,1]{1,0,3,2:T(8,128)}, u32[]{:S(2)}) copy-start(f32[192,192,1,1]{1,0,3,2:T(8,128)} %constant.70) | copy-start | bytes 442372
  275.8 1.8 copy-start.1
  277.7 52.0 %all-to-all-start.3 = ((f32[32,24,1152]{2,1,0:T(8,128)}), f32[32,24,1152]{2,1,0:T(8,128)S(1)}, u32[]{:S(2)}, u32[]{:S(2)}) async-start(f32[32,24,1152]{2,1,0:T(8,128)} %reshape.138), calls=%async_computation.3 | async-start | bytes 7077888 | tf_op jit(solution)/shard_map/all_to_all | solution.py:38
  291.0 9.1 %copy-start.8 = (f32[24,192]{1,0:T(8,128)S(1)}, f32[24,192]{1,0:T(8,128)}, u32[]{:S(2)}) copy-start(f32[24,192]{1,0:T(8,128)} %broadcast_add_fusion) | copy-start | bytes 55300
  291.0 9.1 %copy-start.12 = (f32[32,6,192,1]{2,0,1,3:T(8,128)S(1)}, f32[32,6,192,1]{2,0,1,3:T(8,128)}, u32[]{:S(2)}) copy-start(f32[32,6,192,1]{2,0,1,3:T(8,128)} %constant.71) | copy-start | bytes 442372
  329.7 52.5 %all-to-all-start.7 = ((f32[32,24,1152]{2,1,0:T(8,128)}), f32[32,24,1152]{2,1,0:T(8,128)}, u32[]{:S(2)}, u32[]{:S(2)}) async-start(f32[32,24,1152]{2,1,0:T(8,128)} %reshape.148), calls=%async_computation.7 | async-start | bytes 7077888 | tf_op jit(solution)/shard_map/all_to_all | solution.py:38
  340.2 9.0 %copy-start.9 = (f32[24,192]{1,0:T(8,128)S(1)}, f32[24,192]{1,0:T(8,128)}, u32[]{:S(2)}) copy-start(f32[24,192]{1,0:T(8,128)} %broadcast_add_fusion) | copy-start | bytes 55300
  340.2 9.1 %copy-start.13 = (f32[32,6,192,1]{2,0,1,3:T(8,128)S(1)}, f32[32,6,192,1]{2,0,1,3:T(8,128)}, u32[]{:S(2)}) copy-start(f32[32,6,192,1]{2,0,1,3:T(8,128)} %constant.71) | copy-start | bytes 442372
  382.2 52.5 %all-to-all-start.4 = ((f32[32,24,1152]{2,1,0:T(8,128)}), f32[32,24,1152]{2,1,0:T(8,128)}, u32[]{:S(2)}, u32[]{:S(2)}) async-start(f32[32,24,1152]{2,1,0:T(8,128)} %reshape.141), calls=%async_computation.4 | async-start | bytes 7077888 | tf_op jit(solution)/shard_map/all_to_all | solution.py:38
  388.6 6.5 %copy-start.7 = (f32[192,192,1,1]{1,0,3,2:T(8,128)S(1)}, f32[192,192,1,1]{1,0,3,2:T(8,128)}, u32[]{:S(2)}) copy-start(f32[192,192,1,1]{1,0,3,2:T(8,128)} %constant.70) | copy-start | bytes 442372
  434.7 24.3 %slice-start = ((s8[6291456]{0:T(1024)(128)(4,1)}), s8[2097152]{0:T(1024)(128)(4,1)S(1)}, s32[]{:S(2)}) async-start(s8[6291456]{0:T(1024)(128)(4,1)} %bitcast.93), calls=%async_computation.12 | async-start | bytes 4194304
  441.5 8.0 %copy-start = (f32[4,6,192,192]{3,2,1,0:T(8,128)S(1)}, f32[4,6,192,192]{3,2,1,0:T(8,128)}, u32[]{:S(2)}) copy-start(f32[4,6,192,192]{3,2,1,0:T(8,128)} %fusion.8) | copy-start | bytes 10616836
  441.5 8.0 %copy-start.4 = (f32[192,192,1,1]{1,0,3,2:T(8,128)S(1)}, f32[192,192,1,1]{1,0,3,2:T(8,128)}, u32[]{:S(2)}) copy-start(f32[192,192,1,1]{1,0,3,2:T(8,128)} %constant.69) | copy-start | bytes 442372
  441.6 8.0 %copy-start.10 = (f32[4]{0:T(128)S(1)}, f32[4]{0:T(128)}, u32[]{:S(2)}) copy-start(f32[4]{0:T(128)} %constant.67) | copy-start | bytes 52
  441.6 17.4 %slice-start.1 = ((s8[6291456]{0:T(1024)(128)(4,1)}), s8[4194304]{0:T(1024)(128)(4,1)S(1)}, s32[]{:S(2)}) async-start(s8[6291456]{0:T(1024)(128)(4,1)} %bitcast.93), calls=%async_computation.13 | async-start | bytes 8388608
Sparse Core Ops, SparseCore 0:
  55.8 48.5 all-gather.4
  106.2 66.2 all-gather.2

commit v2 on v1

v2 whole, which is shorter than its diff:
```python
import functools
import math

import jax
import jax.numpy as jnp
import ml_dtypes
import numpy as np
from jax import lax
from jax.experimental import pallas as pl
from jax.experimental.pallas import tpu as pltpu
from jax.sharding import Mesh, PartitionSpec as P

N = 192
LANES = 6 * N
TILES = LANES // 128
PLANE = ("x_lo", "y", "x_hi", "core")
VMEM = 40 * 1024 * 1024


def cas_matrix():
    index = np.arange(N)
    phases = (index[:, None] * index[None, :] % N) * (2.0 * math.pi / N)
    return np.cos(phases) + np.sin(phases)


def held_order():
    z, x_hi, core, row = np.meshgrid(np.arange(8), np.arange(2), np.arange(2), np.arange(6), indexing="ij")
    return (6 * (x_hi * 16 + z * 2 + core) + row).reshape(-1)


def column_order():
    inner, device = np.meshgrid(np.arange(6), np.arange(32), indexing="ij")
    return (6 * device + inner).reshape(-1)


def two_terms(matrix):
    high = matrix.astype(np.float32).astype(ml_dtypes.bfloat16)
    low = (matrix - high.astype(np.float64)).astype(np.float32).astype(ml_dtypes.bfloat16)
    return np.stack([high, low])


def lane_matrices():
    cas = cas_matrix()
    even, odd = np.zeros((256, 256)), np.zeros((256, 256))
    even[:N, :N] = cas
    odd[64:, 64:128] = cas[:, 128:]
    odd[64:, 128:] = cas[:, :128]
    return even, odd


def split(value):
    high = value.astype(jnp.bfloat16)
    return high, (value - high.astype(jnp.float32)).astype(jnp.bfloat16)


def dot(left, right):
    return jnp.dot(left, right, preferred_element_type=jnp.float32)


def product(left, right):
    return dot(left[0], right[0]) + (dot(left[0], right[1]) + dot(left[1], right[0]))


def lane_transform(value, even_ref, odd_ref):
    even, odd = (even_ref[0], even_ref[1]), (odd_ref[0], odd_ref[1])
    high, low = split(value)
    tiles = []
    for start in range(0, LANES, 384):
        first = product((high[:, start : start + 256], low[:, start : start + 256]), even)
        last = product((high[:, start + 128 : start + 384], low[:, start + 128 : start + 384]), odd)
        tiles += [first[:, :128], first[:, 128:] + last[:, :128], last[:, 128:]]
    return jnp.concatenate(tiles, axis=1)


def forward_kernel(orbital_ref, band_ref, even_ref, odd_ref, rows_ref, out_ref):
    pair = orbital_ref[...] * band_ref[:, 0].reshape(N, LANES)
    spectrum = lane_transform(pair, even_ref, odd_ref)
    spectrum = product((rows_ref[0], rows_ref[1]), split(spectrum))
    for tile in range(TILES):
        out_ref[0, :, tile] = spectrum[:, 128 * tile : 128 * tile + 128].reshape(8, 24, 128)


def inverse_kernel(spectrum_ref, band_ref, sum_ref, even_ref, odd_ref, rows_ref, out_ref):
    member = pl.program_id(0)
    spectrum = jnp.concatenate(
        [spectrum_ref[0, :, tile].reshape(N, 128) for tile in range(TILES)], axis=1
    )
    potential = product((rows_ref[0], rows_ref[1]), split(spectrum))
    potential = lane_transform(potential, even_ref, odd_ref)
    prefactor = -1.0 / math.sqrt(N * 8)
    weight = jnp.where(member < 2, prefactor, 2.0 * prefactor)
    term = (weight * band_ref[:, 0].reshape(N, LANES)) * potential

    @pl.when(member == 0)
    def _():
        out_ref[...] = sum_ref[...] + term

    @pl.when(member > 0)
    def _():
        out_ref[...] += term


def filter_kernel(columns_ref, pair_ref, wave_ref, to_ref, from_ref, out_ref):
    source = columns_ref.reshape(32 * TILES * 8, 128)
    target = out_ref.reshape(32 * TILES * 8, 128)
    lower = lax.broadcasted_iota(jnp.int32, (32, 128), 1) < 64

    def rows(tile, k):
        return pl.ds(8 * tile + k, 32, stride=TILES * 8)

    blocks = []
    for k in range(8):
        tiles = [3 * (i // 2) + 2 * (i % 2) for i in range(6)]
        blocks.append(jnp.concatenate([source[rows(tile, k), :] for tile in tiles], axis=0))
    for k in range(0, 8, 2):
        parts = []
        for tile in (1, 4, 7):
            one, two = source[rows(tile, k), :], source[rows(tile, k + 1), :]
            parts.append(jnp.where(lower, one, pltpu.roll(two, 64, 1)))
            parts.append(jnp.where(lower, pltpu.roll(one, 64, 1), two))
        blocks.append(jnp.concatenate(parts, axis=0))
    columns = jnp.concatenate(blocks, axis=1)
    spectrum = product((to_ref[0], to_ref[1]), split(columns))
    spectrum = spectrum * ((4.0 * math.pi / float(N) ** 3) / (wave_ref[...] + pair_ref[0]))
    columns = product((from_ref[0], from_ref[1]), split(spectrum))
    for k in range(8):
        for i in range(6):
            tile = 3 * (i // 2) + 2 * (i % 2)
            target[rows(tile, k), :] = columns[32 * i : 32 * i + 32, 128 * k : 128 * k + 128]
    for k in range(0, 8, 2):
        start = 1024 + 64 * k
        for h in range(3):
            one = columns[64 * h : 64 * h + 32, start : start + 128]
            two = columns[64 * h + 32 : 64 * h + 64, start : start + 128]
            target[rows(3 * h + 1, k), :] = jnp.where(lower, one, pltpu.roll(two, 64, 1))
            target[rows(3 * h + 1, k + 1), :] = jnp.where(lower, pltpu.roll(one, 64, 1), two)


def whole(array):
    return pl.BlockSpec(array.shape, lambda step: (0,) * array.ndim)


PARAMS = pltpu.CompilerParams(vmem_limit_bytes=VMEM)
COST = pl.CostEstimate(flops=16 * 10**9, bytes_accessed=10**7, transcendentals=0)
BANDS = pl.BlockSpec((8, 1, 24, LANES), lambda step: (0, step, 0, 0))
SPECTRA = pl.BlockSpec((1, 8, TILES, 24, 128), lambda step: (step, 0, 0, 0, 0))
COLUMNS = pl.BlockSpec((32, TILES, 8, 128), lambda step: (0, 0, step, 0))


def forward(orbital, bands):
    even, odd = lane_matrices()
    even, odd = jnp.asarray(two_terms(even)), jnp.asarray(two_terms(odd))
    rows = jnp.asarray(two_terms(cas_matrix()[:, held_order()]))
    return pl.pallas_call(
        forward_kernel,
        grid=(4,),
        in_specs=[whole(orbital), BANDS, whole(even), whole(odd), whole(rows)],
        out_specs=SPECTRA,
        out_shape=jax.ShapeDtypeStruct((4, 8, TILES, 24, 128), jnp.float32),
        compiler_params=PARAMS,
        cost_estimate=COST,
        name="forward",
    )(orbital, bands, even, odd, rows)


def inverse(spectra, bands, total):
    even, odd = lane_matrices()
    even, odd = jnp.asarray(two_terms(even)), jnp.asarray(two_terms(odd.T))
    rows = jnp.asarray(two_terms(cas_matrix()[held_order(), :]))
    return pl.pallas_call(
        inverse_kernel,
        grid=(4,),
        in_specs=[SPECTRA, BANDS, whole(total), whole(even), whole(odd), whole(rows)],
        out_specs=whole(total),
        out_shape=jax.ShapeDtypeStruct((N, LANES), jnp.float32),
        compiler_params=PARAMS,
        cost_estimate=COST,
        name="inverse",
    )(spectra, bands, total, even, odd, rows)


def filtered(columns, pair_wave, wave):
    to = jnp.asarray(two_terms(cas_matrix()[:, column_order()]))
    back = jnp.asarray(two_terms(cas_matrix()[column_order(), :]))
    return pl.pallas_call(
        filter_kernel,
        grid=(3,),
        in_specs=[COLUMNS, pl.BlockSpec((1, 1, 8 * N), lambda step: (step, 0, 0)), whole(wave), whole(to), whole(back)],
        out_specs=COLUMNS,
        out_shape=jax.ShapeDtypeStruct((32, TILES, 24, 128), jnp.float32),
        compiler_params=PARAMS,
        cost_estimate=COST,
        name="filter",
    )(columns, pair_wave, wave, to, back)


def wavenumber(index):
    folded = jnp.minimum(index, N - index)
    return folded.astype(jnp.float32) * (2.0 * math.pi / N)


def filter_waves(place):
    wave = wavenumber(jnp.arange(N, dtype=jnp.int32)) ** 2
    mine = wavenumber((place % 8) * 24 + jnp.arange(24, dtype=jnp.int32)) ** 2
    screen = (4.0 * math.pi / N) ** 2
    pair = mine.reshape(3, 8, 1) + wave[None, None, :] + screen
    pair = jnp.concatenate([pair[:, :, :128].reshape(3, 1024), pair[:, :, 128:].reshape(3, 512)], axis=1)
    return pair.reshape(3, 1, 8 * N), wave.reshape(N, 1)


def exchange_plane(blocks):
    return lax.all_to_all(blocks, PLANE, 0, 0, tiled=True)


def exchange_z(blocks):
    return lax.all_to_all(blocks, "z", 0, 0, tiled=True)


def to_blocks(planes):
    count = planes.shape[0]
    blocks = planes.reshape(count, 6, 32, 6, N).transpose(2, 0, 1, 3, 4)
    return blocks.reshape(32, count * 54, 128)


def shards(resident, owned, owner):
    pair_wave, wave = filter_waves(lax.axis_index(PLANE))
    orbital = exchange_z(exchange_plane(to_blocks(resident)).reshape(8, 216, 128))
    orbital = orbital.reshape(N, LANES)
    halves = []
    for half in range(2):
        spread = exchange_plane(to_blocks(owned[0, 2 * half : 2 * half + 2])).reshape(8, 4, 108, 128)
        chosen = [lax.dynamic_index_in_dim(spread, owner[turn], 0, keepdims=False) for turn in range(2)]
        chosen = jnp.stack(chosen).reshape(2, 4, 2, 6, LANES).transpose(0, 2, 1, 3, 4)
        halves.append(lax.all_gather(chosen.reshape(4, 24, LANES), "z", axis=0, tiled=False))
    spectra = []
    for bands in halves:
        spectra.append(exchange_plane(forward(orbital, bands).reshape(32, TILES, 24, 128)))
    potentials = []
    for columns in spectra:
        potentials.append(exchange_plane(filtered(columns, pair_wave, wave)))
    total = jnp.zeros((N, LANES), jnp.float32)
    for bands, potential in zip(halves, potentials):
        total = inverse(potential.reshape(4, 8, TILES, 24, 128), bands, total)
    back = exchange_z(total.reshape(8, 216, 128))
    back = exchange_plane(back.reshape(32, 54, 128))
    return back.reshape(32, 6, 6, N).transpose(1, 0, 2, 3).reshape(1, 6, N, N)


def solution(mesh):
    fine = Mesh(mesh.devices.reshape(2, 4, 2, 8, 2), ("x_lo", "y", "x_hi", "z", "core"))
    band, slab = ("x_lo", "y"), ("x_hi", "z", "core")
    return jax.shard_map(
        shards,
        mesh=fine,
        in_specs=(P(band, slab), P(band, None, slab), P()),
        out_specs=P(band, slab),
        check_vma=False,
    )
```

time: 537 us -> 444 us (0.83); the launches traced: 527 us -> 442 us
  matrix products: 79.2 us -> 0 us
  local copies, waits for them, and re-layouts: 127 us -> 59 us
  waiting for transfers between devices: 117 us -> 179 us
  Pallas kernels: 0 us -> 31.6 us
  blocking collectives: 143 us -> 114 us
  other arithmetic: 11.7 us -> 0.89 us
    dot_general x12 -> x0, matrix products: 79.2 us -> none  [the longest x2 18.1 us: shards(): columns = jnp.einsum('sakc,skb->abc', columns, matrix, precision=high)]
    reshape x12 -> x6, local copies, waits for them, and re-layouts: 65.1 us -> 1.8 us  [the longest x1 1.38 us: filter_waves(): pair[:, :, 128:].reshape(3, 512)]
    all_to_all x5 -> x6, waiting for transfers between devices: 110 us -> 146 us  [exchange_plane(): return lax.all_to_all(blocks, PLANE, 0, 0, tiled=True)]
    unnamed x32 -> x70, local copies, waits for them, and re-layouts: 1.91 us -> 33.9 us
    pallas_call x0 -> x6, Pallas kernels: none -> 31.6 us  [the longest x2 11.2 us: filtered(): pl.pallas_call(filter_kernel, grid=(3,), in_specs=[COLUMNS, pl.BlockSpec(...]
    transpose x6 -> x0, local copies, waits for them, and re-layouts: 31.2 us -> none  [the longest x2 13.4 us: shards(): pairs = jnp.einsum('paic,ka->pkic', pairs, cas_held, precision=high)]
    all_to_all x3 -> x2, blocking collectives: 73.9 us -> 44.6 us  [exchange_plane(): return lax.all_to_all(blocks, PLANE, 0, 0, tiled=True)]
    all_gather x2, waiting for transfers between devices: 7 us -> 32.7 us  [shards(): lax.all_gather(chosen.reshape(4, 24, LANES), 'z', axis=0, tiled=False)]
  transfers between devices with their start and end apart: 7 -> 8, of which waited for: 6 -> 7; matrix products, arithmetic and copies ran while one was open for 22% -> 3% of each run, Pallas kernels for 0% -> 6%
where the time goes in v2:
time: 444 us; the launch traced here: 442 us
  waiting for transfers between devices  179 us (40%)
  blocking collectives  114 us (26%)
  local copies, waits for them, and re-layouts  59 us (13%)
  starting transfers between devices  40.2 us (9%)
  Pallas kernels  31.6 us (7%)
  between operations  17.9 us (4%)
    all_to_all x6, waiting for transfers between devices, exchange_plane(): return lax.all_to_all(blocks, PLANE, 0, 0, tiled=True)  146 us
    all_to_all x2, blocking collectives, exchange_z(): return lax.all_to_all(blocks, 'z', 0, 0, tiled=True)  69.2 us
    all_to_all x2, blocking collectives, exchange_plane(): return lax.all_to_all(blocks, PLANE, 0, 0, tiled=True)  44.6 us
    all_to_all x6, starting transfers between devices, exchange_plane(): return lax.all_to_all(blocks, PLANE, 0, 0, tiled=True)  40.1 us
    unnamed x70, local copies, waits for them, and re-layouts  33.9 us
    all_gather x2, waiting for transfers between devices, shards(): lax.all_gather(chosen.reshape(4, 24, LANES), 'z', axis=0, tiled=False)  32.7 us
    pallas_call x2, Pallas kernels, filtered(): pl.pallas_call(filter_kernel, grid=(3,), in_specs=[COLUMNS, pl.BlockSpec(...  11.2 us
    pallas_call x2, Pallas kernels, inverse(): pl.pallas_call(inverse_kernel, grid=(4,), in_specs=[SPECTRA, BANDS, whole...  10.5 us
  transfers between devices with their start and end apart: 8, of which 7 were waited for; matrix products, arithmetic and copies ran while one was open for 3% of the time, Pallas kernels for 6%

profile of v2, /device:TPU:1, one launch (start us, length us, event | category | flops | bytes accessed | tf_op | source)
XLA Modules:
  0.0 442.1 jit_solution(4521378587454061220)
XLA Ops:
  6.5 4.2 fusion.9
  10.8 1.8 copy.46
  13.1 2.4 reshape.121
  15.5 8.8 %all-to-all-start.5 = ((f32[32,108,128]{2,1,0:T(8,128)}), f32[32,108,128]{2,1,0:T(8,128)}, u32[]{:S(2)}, u32[]{:S(2)}) async-start(f32[32,108,128]{2,1,0:T(8,128)} %reshape.121), calls=%async_computation.5 | async-start | bytes 3670016 | tf_op jit(solution)/shard_map/all_to_all | solution.py:212
  24.2 1.8 copy.41
  26.6 2.4 reshape.113
  28.9 21.0 %all-to-all-done.5 = f32[32,108,128]{2,1,0:T(8,128)} async-done(((f32[32,108,128]{2,1,0:T(8,128)}), f32[32,108,128]{2,1,0:T(8,128)}, u32[]{:S(2)}, u32[]{:S(2)}) %all-to-all-start.5) | async-done | bytes 1769504 | tf_op jit(solution)/shard_map/all_to_all | solution.py:212
  49.9 4.6 %all-to-all-start.2 = ((f32[32,108,128]{2,1,0:T(8,128)}), f32[32,108,128]{2,1,0:T(8,128)S(1)}, u32[]{:S(2)}, u32[]{:S(2)}) async-start(f32[32,108,128]{2,1,0:T(8,128)} %reshape.113), calls=%async_computation.2 | async-start | bytes 3670016 | tf_op jit(solution)/shard_map/all_to_all | solution.py:212
  59.3 20.9 %all-to-all-done.2 = f32[32,108,128]{2,1,0:T(8,128)S(1)} async-done(((f32[32,108,128]{2,1,0:T(8,128)}), f32[32,108,128]{2,1,0:T(8,128)S(1)}, u32[]{:S(2)}, u32[]{:S(2)}) %all-to-all-start.2) | async-done | bytes 1769504 | tf_op jit(solution)/shard_map/all_to_all | solution.py:212
  80.2 1.1 constant_dynamic-slice_fusion.1
  83.4 2.7 reshape.109
  87.1 20.1 %all_to_all.50 = f32[32,54,128]{2,1,0:T(8,128)S(1)} all-to-all(f32[32,54,128]{2,1,0:T(8,128)S(1)} %reshape.110), channel_id=1, replica_groups=mesh['x_lo'=2,'y'=4,'x_hi'=2,'z'=8,'core'=2] {'x_lo','y','x_hi','core'}, dimensions={0} | all-to-all | bytes 1769472 | tf_op jit(solution)/shard_map/all_to_all | solution.py:212
  107.2 42.8 %all_to_all.51 = f32[8,216,128]{2,1,0:T(8,128)S(1)} all-to-all(f32[8,216,128]{2,1,0:T(8,128)S(1)} %reshape.111), channel_id=1, replica_groups=mesh['x_lo'=2,'y'=4,'x_hi'=2,'z'=8,'core'=2] {'z'}, dimensions={0} | all-to-all | bytes 1769472 | tf_op jit(solution)/shard_map/all_to_all | solution.py:216
  150.3 2.3 copy-done.10
  152.6 5.0 %forward.3 = f32[4,8,9,24,128]{4,3,2,1,0:T(8,128)S(1)} custom-call(f32[192,1152]{1,0:T(8,128)S(1)} %reshape.112.orbital_ref, f32[8,4,24,1152]{3,2,1,0:T(8,128)S(1)} %copy-done.10, bf16[2,256,256]{2,1,0:T(8,128)(2,1)S(1)} %copy-done.14, bf16[2,256,256]{2,1,0:T(8,128)(2,1)S(1)} %copy-done.20, bf16[2,192,192]{2,1,0:T(8,128)(2,1)S(1)} %copy-done.28), custom_call_target="tpu_custom_call" | custom-call | flops 16000000000 | bytes 10000000 | tf_op jit(solution)/shard_map/forward/pallas_call | solution.py:154
  157.5 1.9 copy-done.3
  159.4 7.0 %all-to-all-start.6 = ((f32[32,9,24,128]{3,2,1,0:T(8,128)}), f32[32,9,24,128]{3,2,1,0:T(8,128)S(1)}, u32[]{:S(2)}, u32[]{:S(2)}) async-start(f32[32,9,24,128]{3,2,1,0:T(8,128)} %bitcast.29), calls=%async_computation.6 | async-start | bytes 7077888 | tf_op jit(solution)/shard_map/all_to_all | solution.py:212
  166.4 32.7 %all-gather.3.cloned.1.call-done.band_ref = f32[8,4,24,1152]{3,2,1,0:T(8,128)} async-done(((f32[1,4,24,1152]{3,2,1,0:T(8,128)}), f32[8,4,24,1152]{3,2,1,0:T(8,128)}) %all-gather.3.cloned.1.call-update) | async-done | bytes 3538960 | tf_op jit(solution)/shard_map/all_gather | solution.py:234
  199.1 1.2 copy-done.5
  200.3 2.0 copy-done.12
  202.3 0.9 copy-done.15
  203.2 0.9 copy-done.21
  205.1 5.0 %forward.2 = f32[4,8,9,24,128]{4,3,2,1,0:T(8,128)S(1)} custom-call(f32[192,1152]{1,0:T(8,128)S(1)} %copy-done.5, f32[8,4,24,1152]{3,2,1,0:T(8,128)S(1)} %copy-done.12, bf16[2,256,256]{2,1,0:T(8,128)(2,1)S(1)} %copy-done.15, bf16[2,256,256]{2,1,0:T(8,128)(2,1)S(1)} %copy-done.21, bf16[2,192,192]{2,1,0:T(8,128)(2,1)S(1)} %copy-done.29), custom_call_target="tpu_custom_call" | custom-call | flops 16000000000 | bytes 10000000 | tf_op jit(solution)/shard_map/forward/pallas_call | solution.py:154
  210.1 1.9 copy-done
  212.5 7.0 %all-to-all-start.3 = ((f32[32,9,24,128]{3,2,1,0:T(8,128)}), f32[32,9,24,128]{3,2,1,0:T(8,128)}, u32[]{:S(2)}, u32[]{:S(2)}) async-start(f32[32,9,24,128]{3,2,1,0:T(8,128)} %bitcast.27), calls=%async_computation.3 | async-start | bytes 7077888 | tf_op jit(solution)/shard_map/all_to_all | solution.py:212
  220.3 1.4 reshape.118
  223.0 0.9 copy-done.24
  224.8 5.1 %filter.3 = f32[32,9,24,128]{3,2,1,0:T(8,128)S(1)} custom-call(f32[32,9,24,128]{3,2,1,0:T(8,128)S(1)} %all-to-all-done.6.columns_ref, f32[3,1,1536]{2,1,0:T(1,128)S(1)} %reshape.119.pair_ref, f32[192,1]{1,0:T(8,128)S(1)} %fusion.2.wave_ref, bf16[2,192,192]{2,1,0:T(8,128)(2,1)S(1)} %copy-done.24, bf16[2,192,192]{2,1,0:T(8,128)(2,1)S(1)} %copy-done.26), custom_call_target="tpu_custom_call" | custom-call | flops 16000000000 | bytes 10000000 | tf_op jit(solution)/shard_map/filter/pallas_call | solution.py:185
  229.9 1.8 copy-done.2
  232.3 33.3 %all-to-all-done.3.columns_ref = f32[32,9,24,128]{3,2,1,0:T(8,128)} async-done(((f32[32,9,24,128]{3,2,1,0:T(8,128)}), f32[32,9,24,128]{3,2,1,0:T(8,128)}, u32[]{:S(2)}, u32[]{:S(2)}) %all-to-all-start.3) | async-done | bytes 3538976 | tf_op jit(solution)/shard_map/all_to_all | solution.py:212
  265.6 6.3 %all-to-all-start.7 = ((f32[32,9,24,128]{3,2,1,0:T(8,128)}), f32[32,9,24,128]{3,2,1,0:T(8,128)S(1)}, u32[]{:S(2)}, u32[]{:S(2)}) async-start(f32[32,9,24,128]{3,2,1,0:T(8,128)} %copy-done.2), calls=%async_computation.7 | async-start | bytes 7077888 | tf_op jit(solution)/shard_map/all_to_all | solution.py:212
  275.5 6.1 %filter.2 = f32[32,9,24,128]{3,2,1,0:T(8,128)S(1)} custom-call(f32[32,9,24,128]{3,2,1,0:T(8,128)} %all-to-all-done.3.columns_ref, f32[3,1,1536]{2,1,0:T(1,128)S(1)} %copy-done.9, f32[192,1]{1,0:T(8,128)S(1)} %copy-done.7, bf16[2,192,192]{2,1,0:T(8,128)(2,1)S(1)} %copy-done.25, bf16[2,192,192]{2,1,0:T(8,128)(2,1)S(1)} %copy-done.27), custom_call_target="tpu_custom_call" | custom-call | flops 16000000000 | bytes 10000000 | tf_op jit(solution)/shard_map/filter/pallas_call | solution.py:185
  281.6 1.9 copy-done.1
  283.4 34.6 %all-to-all-done.7 = f32[32,9,24,128]{3,2,1,0:T(8,128)S(1)} async-done(((f32[32,9,24,128]{3,2,1,0:T(8,128)}), f32[32,9,24,128]{3,2,1,0:T(8,128)S(1)}, u32[]{:S(2)}, u32[]{:S(2)}) %all-to-all-start.7) | async-done | bytes 3538976 | tf_op jit(solution)/shard_map/all_to_all | solution.py:212
  318.1 6.4 %all-to-all-start.4 = ((f32[32,9,24,128]{3,2,1,0:T(8,128)}), f32[32,9,24,128]{3,2,1,0:T(8,128)}, u32[]{:S(2)}, u32[]{:S(2)}) async-start(f32[32,9,24,128]{3,2,1,0:T(8,128)} %copy-done.1), calls=%async_computation.4 | async-start | bytes 7077888 | tf_op jit(solution)/shard_map/all_to_all | solution.py:212
  324.5 2.0 copy-done.11
  326.5 0.9 copy-done.16
  327.5 0.9 copy-done.18
  329.4 4.7 %inverse.2.sum_ref = f32[192,1152]{1,0:T(8,128)S(1)} custom-call(f32[4,8,9,24,128]{4,3,2,1,0:T(8,128)S(1)} %bitcast.28, f32[8,4,24,1152]{3,2,1,0:T(8,128)S(1)} %copy-done.11, f32[192,1152]{1,0:T(8,128)S(1)} %broadcast_in_dim.4.sum_ref, bf16[2,256,256]{2,1,0:T(8,128)(2,1)S(1)} %copy-done.16, bf16[2,256,256]{2,1,0:T(8,128)(2,1)S(1)} %copy-done.18, ...), custom_call_target="tpu_custom_call" | custom-call | flops 16000000000 | bytes 10000000 | tf_op jit(solution)/shard_map/inverse/pallas_call | solution.py:170
  335.0 35.6 %all-to-all-done.4 = f32[32,9,24,128]{3,2,1,0:T(8,128)} async-done(((f32[32,9,24,128]{3,2,1,0:T(8,128)}), f32[32,9,24,128]{3,2,1,0:T(8,128)}, u32[]{:S(2)}, u32[]{:S(2)}) %all-to-all-start.4) | async-done | bytes 3538976 | tf_op jit(solution)/shard_map/all_to_all | solution.py:212
  370.6 2.0 copy-done.13
  372.6 0.9 copy-done.17
  373.5 0.9 copy-done.19
  375.4 1.2 copy-done.31
  376.6 5.8 %inverse.3 = f32[192,1152]{1,0:T(8,128)S(1)} custom-call(f32[4,8,9,24,128]{4,3,2,1,0:T(8,128)} %bitcast.8.spectrum_ref, f32[8,4,24,1152]{3,2,1,0:T(8,128)S(1)} %copy-done.13, f32[192,1152]{1,0:T(8,128)S(1)} %copy-done.31, bf16[2,256,256]{2,1,0:T(8,128)(2,1)S(1)} %copy-done.17, bf16[2,256,256]{2,1,0:T(8,128)(2,1)S(1)} %copy-done.19, ...), custom_call_target="tpu_custom_call" | custom-call | flops 16000000000 | bytes 10000000 | tf_op jit(solution)/shard_map/inverse/pallas_call | solution.py:170
  382.5 26.5 %all_to_all.52 = f32[8,216,128]{2,1,0:T(8,128)S(1)} all-to-all(f32[8,216,128]{2,1,0:T(8,128)S(1)} %reshape.126), channel_id=1, replica_groups=mesh['x_lo'=2,'y'=4,'x_hi'=2,'z'=8,'core'=2] {'z'}, dimensions={0} | all-to-all | bytes 1769472 | tf_op jit(solution)/shard_map/all_to_all | solution.py:216
  409.0 24.5 %all_to_all.53 = f32[32,54,128]{2,1,0:T(8,128)S(1)} all-to-all(f32[32,54,128]{2,1,0:T(8,128)S(1)} %reshape.127), channel_id=1, replica_groups=mesh['x_lo'=2,'y'=4,'x_hi'=2,'z'=8,'core'=2] {'x_lo','y','x_hi','core'}, dimensions={0} | all-to-all | bytes 1769472 | tf_op jit(solution)/shard_map/all_to_all | solution.py:212
  434.1 1.2 reshape.129
  (86 shorter events, 17.0 us)
Async XLA Ops:
  15.5 8.8 %copy-start.32 = (f32[1,2,6,192,192]{4,3,2,1,0:T(8,128)S(1)}, f32[1,2,6,192,192]{4,3,2,1,0:T(8,128)}, u32[]{:S(2)}) copy-start(f32[1,2,6,192,192]{4,3,2,1,0:T(8,128)} %get-tuple-element.6) | copy-start | bytes 5308420
  15.5 34.4 %all-to-all-start.5 = ((f32[32,108,128]{2,1,0:T(8,128)}), f32[32,108,128]{2,1,0:T(8,128)}, u32[]{:S(2)}, u32[]{:S(2)}) async-start(f32[32,108,128]{2,1,0:T(8,128)} %reshape.121), calls=%async_computation.5 | async-start | bytes 3670016 | tf_op jit(solution)/shard_map/all_to_all | solution.py:212
  28.9 25.7 %copy-start.33 = (s32[2]{0:T(128)S(1)}, s32[2]{0:T(128)}, u32[]{:S(2)}) copy-start(s32[2]{0:T(128)} %param.21) | copy-start | bytes 28
  49.9 30.3 %all-to-all-start.2 = ((f32[32,108,128]{2,1,0:T(8,128)}), f32[32,108,128]{2,1,0:T(8,128)S(1)}, u32[]{:S(2)}, u32[]{:S(2)}) async-start(f32[32,108,128]{2,1,0:T(8,128)} %reshape.113), calls=%async_computation.2 | async-start | bytes 3670016 | tf_op jit(solution)/shard_map/all_to_all | solution.py:212
  54.5 95.7 %all-gather.5.cloned.1.call-start = ((), (), s32[]{:S(2)}) async-start(), calls=%async_computation.11 | async-start | bytes 3981312 | tf_op jit(solution)/shard_map/all_gather | solution.py:234
  82.3 116.7 %all-gather.3.cloned.1.call-start = ((), (), s32[]{:S(2)}) async-start(), calls=%async_computation.10 | async-start | bytes 3981312 | tf_op jit(solution)/shard_map/all_gather | solution.py:234
  107.2 43.1 %copy-start.14 = (bf16[2,256,256]{2,1,0:T(8,128)(2,1)S(1)}, bf16[2,256,256]{2,1,0:T(8,128)(2,1)}, u32[]{:S(2)}) copy-start(bf16[2,256,256]{2,1,0:T(8,128)(2,1)} %constant.74.clone.even_ref) | copy-start | bytes 786436
  107.2 43.1 %copy-start.20 = (bf16[2,256,256]{2,1,0:T(8,128)(2,1)S(1)}, bf16[2,256,256]{2,1,0:T(8,128)(2,1)}, u32[]{:S(2)}) copy-start(bf16[2,256,256]{2,1,0:T(8,128)(2,1)} %constant.75.clone.odd_ref) | copy-start | bytes 786436
  107.2 43.1 %copy-start.28 = (bf16[2,192,192]{2,1,0:T(8,128)(2,1)S(1)}, bf16[2,192,192]{2,1,0:T(8,128)(2,1)}, u32[]{:S(2)}) copy-start(bf16[2,192,192]{2,1,0:T(8,128)(2,1)} %constant.76.clone.rows_ref) | copy-start | bytes 442372
  150.2 7.3 %copy-start.4 = (f32[192,1152]{1,0:T(8,128)}, f32[192,1152]{1,0:T(8,128)S(1)}, u32[]{:S(2)}) copy-start(f32[192,1152]{1,0:T(8,128)S(1)} %reshape.112.orbital_ref) | copy-start | bytes 2654212
  150.3 2.3 copy-start.10
  157.5 1.9 copy-start.3
  159.4 53.1 %all-to-all-start.6 = ((f32[32,9,24,128]{3,2,1,0:T(8,128)}), f32[32,9,24,128]{3,2,1,0:T(8,128)S(1)}, u32[]{:S(2)}, u32[]{:S(2)}) async-start(f32[32,9,24,128]{3,2,1,0:T(8,128)} %bitcast.29), calls=%async_computation.6 | async-start | bytes 7077888 | tf_op jit(solution)/shard_map/all_to_all | solution.py:212
  199.1 1.2 copy-start.5
  200.3 2.0 copy-start.12
  202.3 0.9 copy-start.15
  203.2 0.9 copy-start.21
  204.2 0.9 copy-start.29
  210.1 1.9 copy-start
  212.5 53.1 %all-to-all-start.3 = ((f32[32,9,24,128]{3,2,1,0:T(8,128)}), f32[32,9,24,128]{3,2,1,0:T(8,128)}, u32[]{:S(2)}, u32[]{:S(2)}) async-start(f32[32,9,24,128]{3,2,1,0:T(8,128)} %bitcast.27), calls=%async_computation.3 | async-start | bytes 7077888 | tf_op jit(solution)/shard_map/all_to_all | solution.py:212
  222.4 0.6 copy-start.8
  223.0 0.9 copy-start.24
  223.9 0.9 copy-start.26
  229.9 1.8 copy-start.2
  231.7 0.6 copy-start.6
  265.6 52.4 %all-to-all-start.7 = ((f32[32,9,24,128]{3,2,1,0:T(8,128)}), f32[32,9,24,128]{3,2,1,0:T(8,128)S(1)}, u32[]{:S(2)}, u32[]{:S(2)}) async-start(f32[32,9,24,128]{3,2,1,0:T(8,128)} %copy-done.2), calls=%async_computation.7 | async-start | bytes 7077888 | tf_op jit(solution)/shard_map/all_to_all | solution.py:212
  272.0 0.9 copy-start.7
  272.9 0.7 copy-start.9
  273.6 0.9 copy-start.25
  274.5 0.9 copy-start.27
  281.6 1.9 copy-start.1
  318.1 52.5 %all-to-all-start.4 = ((f32[32,9,24,128]{3,2,1,0:T(8,128)}), f32[32,9,24,128]{3,2,1,0:T(8,128)}, u32[]{:S(2)}, u32[]{:S(2)}) async-start(f32[32,9,24,128]{3,2,1,0:T(8,128)} %copy-done.1), calls=%async_computation.4 | async-start | bytes 7077888 | tf_op jit(solution)/shard_map/all_to_all | solution.py:212
  324.5 2.0 copy-start.11
  326.5 0.9 copy-start.16
  327.5 0.9 copy-start.18
  328.4 0.9 copy-start.22
  334.1 0.9 copy-start.30
  370.6 2.0 copy-start.13
  372.6 0.9 copy-start.17
  373.5 0.9 copy-start.19
  374.5 0.9 copy-start.23
  375.4 1.2 copy-start.31
Sparse Core Ops, SparseCore 0:
  82.5 67.2 all-gather.4
  151.5 47.5 all-gather.2

commit v3 on v2

--- a/solution.py
+++ b/solution.py
@@ -14,7 +14,7 @@
 LANES = 6 * N
 TILES = LANES // 128
 PLANE = ("x_lo", "y", "x_hi", "core")
-VMEM = 40 * 1024 * 1024
+VMEM = 60 * 1024 * 1024
 
 
 def cas_matrix():
@@ -72,8 +72,53 @@
     return jnp.concatenate(tiles, axis=1)
 
 
-def forward_kernel(orbital_ref, band_ref, even_ref, odd_ref, rows_ref, out_ref):
-    pair = orbital_ref[...] * band_ref[:, 0].reshape(N, LANES)
+def pack_kernel(planes_ref, out_ref, left_ref, right_ref):
+    fields, rows = planes_ref.shape[0], out_ref.shape[1]
+    target = out_ref.reshape(32 * rows, 128)
+    lower = lax.broadcasted_iota(jnp.int32, (32, 128), 1) < 64
+    for field in range(fields):
+        for a in range(6):
+            slot = (6 * field + a) % 2
+            left, right = left_ref.at[slot], right_ref.at[slot]
+            left[...] = planes_ref[field, a, :, :128]
+            right[:, :64] = planes_ref[field, a, :, 128:]
+            for h in range(3):
+                even, odd = pl.ds(2 * h, 32, stride=6), pl.ds(2 * h + 1, 32, stride=6)
+                start = pltpu.roll(left[odd, :], 64, 1)
+                end = pltpu.roll(right[odd, :], 64, 1)
+                row = field * 54 + a * TILES + 3 * h
+                target[pl.ds(row, 32, stride=rows), :] = left[even, :]
+                target[pl.ds(row + 1, 32, stride=rows), :] = jnp.where(lower, right[even, :], start)
+                target[pl.ds(row + 2, 32, stride=rows), :] = jnp.where(lower, start, end)
+
+
+def slots_kernel(slots_ref, spread_ref, *out_refs):
+    for slot, out_ref in enumerate(out_refs):
+        for source in range(4):
+            block = spread_ref.at[slots_ref[slot], source]
+            for tile in range(TILES):
+                rows = block[pl.ds(tile, 6, stride=TILES), :]
+                out_ref[6 * source : 6 * source + 6, 128 * tile : 128 * tile + 128] = rows
+
+
+def choose_kernel(owner_ref, spread_ref, out_ref):
+    for source in range(4):
+        block = spread_ref.at[0, source]
+        for member in range(2):
+            for tile in range(TILES):
+                rows = block[pl.ds(54 * member + tile, 6, stride=TILES), :]
+                out_ref[member, 6 * source : 6 * source + 6, 128 * tile : 128 * tile + 128] = rows
+
+
+def forward_kernel(slots_ref, *refs):
+    piece_refs, (band_ref, even_ref, odd_ref, rows_ref, out_ref, orbital_ref) = refs[:8], refs[8:]
+
+    @pl.when(pl.program_id(0) == 0)
+    def _():
+        for slot, piece_ref in enumerate(piece_refs):
+            orbital_ref[slots_ref[slot]] = piece_ref[...]
+
+    pair = orbital_ref[...].reshape(N, LANES) * band_ref[:, 0].reshape(N, LANES)
     spectrum = lane_transform(pair, even_ref, odd_ref)
     spectrum = product((rows_ref[0], rows_ref[1]), split(spectrum))
     for tile in range(TILES):
@@ -147,20 +192,72 @@
 COLUMNS = pl.BlockSpec((32, TILES, 8, 128), lambda step: (0, 0, step, 0))
 
 
-def forward(orbital, bands):
+MOVES = pltpu.CompilerParams(vmem_limit_bytes=16 * 1024 * 1024)
+MOVED = pl.CostEstimate(flops=0, bytes_accessed=4 * 10**6, transcendentals=0)
+
+
+def to_blocks(planes):
+    rows = 56 * planes.shape[0]
+    return pl.pallas_call(
+        pack_kernel,
+        out_shape=jax.ShapeDtypeStruct((32, rows, 128), jnp.float32),
+        scratch_shapes=[pltpu.VMEM((2, N, 128), jnp.float32)] * 2,
+        compiler_params=MOVES,
+        cost_estimate=MOVED,
+        name="pack",
+    )(planes)
+
+
+def by_slots(slots, spread):
+    return pl.pallas_call(
+        slots_kernel,
+        in_specs=[pl.BlockSpec(memory_space=pltpu.SMEM), pl.BlockSpec(memory_space=pltpu.VMEM)],
+        out_specs=[pl.BlockSpec(memory_space=pltpu.VMEM)] * 8,
+        out_shape=[jax.ShapeDtypeStruct((24, LANES), jnp.float32)] * 8,
+        compiler_params=MOVES,
+        cost_estimate=MOVED,
+        name="slots",
+    )(slots, spread)
+
+
+def choose(owner, spread):
+    return pl.pallas_call(
+        choose_kernel,
+        grid_spec=pltpu.PrefetchScalarGridSpec(
+            num_scalar_prefetch=1,
+            grid=(2,),
+            in_specs=[pl.BlockSpec((1, 4, 112, 128), lambda turn, owner: (owner[turn], 0, 0, 0))],
+            out_specs=pl.BlockSpec((2, 24, LANES), lambda turn, owner: (turn, 0, 0)),
+        ),
+        out_shape=jax.ShapeDtypeStruct((4, 24, LANES), jnp.float32),
+        compiler_params=MOVES,
+        cost_estimate=MOVED,
+        name="choose",
+    )(owner, spread)
+
+
+def forward(slots, pieces, bands):
     even, odd = lane_matrices()
     even, odd = jnp.asarray(two_terms(even)), jnp.asarray(two_terms(odd))
     rows = jnp.asarray(two_terms(cas_matrix()[:, held_order()]))
     return pl.pallas_call(
         forward_kernel,
         grid=(4,),
-        in_specs=[whole(orbital), BANDS, whole(even), whole(odd), whole(rows)],
+        in_specs=[
+            pl.BlockSpec(memory_space=pltpu.SMEM),
+            *[whole(piece) for piece in pieces],
+            BANDS,
+            whole(even),
+            whole(odd),
+            whole(rows),
+        ],
         out_specs=SPECTRA,
         out_shape=jax.ShapeDtypeStruct((4, 8, TILES, 24, 128), jnp.float32),
+        scratch_shapes=[pltpu.VMEM((8, 24, LANES), jnp.float32)],
         compiler_params=PARAMS,
         cost_estimate=COST,
         name="forward",
-    )(orbital, bands, even, odd, rows)
+    )(slots, *pieces, bands, even, odd, rows)
 
 
 def inverse(spectra, bands, total):
@@ -216,28 +313,33 @@
     return lax.all_to_all(blocks, "z", 0, 0, tiled=True)
 
 
-def to_blocks(planes):
-    count = planes.shape[0]
-    blocks = planes.reshape(count, 6, 32, 6, N).transpose(2, 0, 1, 3, 4)
-    return blocks.reshape(32, count * 54, 128)
+def gather_orbital(spread, slots):
+    pieces = by_slots(slots, spread)
+    return [pieces[0]] + [
+        lax.ppermute(pieces[m], "z", [(z, z ^ m) for z in range(8)]) for m in range(1, 8)
+    ]
 
 
 def shards(resident, owned, owner):
     pair_wave, wave = filter_waves(lax.axis_index(PLANE))
-    orbital = exchange_z(exchange_plane(to_blocks(resident)).reshape(8, 216, 128))
-    orbital = orbital.reshape(N, LANES)
-    halves = []
-    for half in range(2):
-        spread = exchange_plane(to_blocks(owned[0, 2 * half : 2 * half + 2])).reshape(8, 4, 108, 128)
-        chosen = [lax.dynamic_index_in_dim(spread, owner[turn], 0, keepdims=False) for turn in range(2)]
-        chosen = jnp.stack(chosen).reshape(2, 4, 2, 6, LANES).transpose(0, 2, 1, 3, 4)
-        halves.append(lax.all_gather(chosen.reshape(4, 24, LANES), "z", axis=0, tiled=False))
+    slots = lax.axis_index("z") ^ jnp.arange(8, dtype=jnp.int32)
+    spread = exchange_plane(to_blocks(resident))
+    first, second = to_blocks(owned[0, :2]), to_blocks(owned[0, 2:])
+    first, spread = lax.optimization_barrier((first, spread))
+    orbital = gather_orbital(spread.reshape(8, 4, 56, 128), slots)
+    first, orbital = lax.optimization_barrier((exchange_plane(first), orbital))
+    first = choose(owner, first.reshape(8, 4, 112, 128))
+    second, first = lax.optimization_barrier((second, first))
+    halves = [lax.all_gather(first, "z", axis=0, tiled=False)]
+    second = choose(owner, exchange_plane(second).reshape(8, 4, 112, 128))
+    halves.append(lax.all_gather(second, "z", axis=0, tiled=False))
     spectra = []
     for bands in halves:
-        spectra.append(exchange_plane(forward(orbital, bands).reshape(32, TILES, 24, 128)))
+        spectra.append(exchange_plane(forward(slots, orbital, bands).reshape(32, 216, 128)))
     potentials = []
     for columns in spectra:
-        potentials.append(exchange_plane(filtered(columns, pair_wave, wave)))
+        columns = filtered(columns.reshape(32, TILES, 24, 128), pair_wave, wave)
+        potentials.append(exchange_plane(columns.reshape(32, 216, 128)))
     total = jnp.zeros((N, LANES), jnp.float32)
     for bands, potential in zip(halves, potentials):
         total = inverse(potential.reshape(4, 8, TILES, 24, 128), bands, total)

time: 444 us -> 413 us (0.930)
  local copies, waits for them, and re-layouts: 59 us -> 15.5 us
  blocking collectives: 114 us -> 84.7 us
  Pallas kernels: 31.6 us -> 53.1 us
  starting transfers between devices: 40.2 us -> 54.3 us
  waiting for transfers between devices: 179 us -> 190 us
    all_to_all x2 -> x1, blocking collectives: 69.2 us -> 26.5 us  [exchange_z(): return lax.all_to_all(blocks, 'z', 0, 0, tiled=True)]
    unnamed x70 -> x34, local copies, waits for them, and re-layouts: 33.9 us -> 8.08 us
    all_to_all x6, waiting for transfers between devices: 146 us -> 129 us  [exchange_plane(): return lax.all_to_all(blocks, PLANE, 0, 0, tiled=True)]
    ppermute x0 -> x7, starting transfers between devices: none -> 14.5 us  [gather_orbital(): lax.ppermute(pieces[m], 'z', [(z, z ^ m) for z in range(8)])]
    all_gather x2, waiting for transfers between devices: 32.7 us -> 47.2 us  [the longest x1 33.8 us: shards(): halves.append(lax.all_gather(second, 'z', axis=0, tiled=False))]
    ppermute x0 -> x7, waiting for transfers between devices: none -> 13.8 us  [gather_orbital(): lax.ppermute(pieces[m], 'z', [(z, z ^ m) for z in range(8)])]
    all_to_all x2, blocking collectives: 44.6 us -> 58.3 us  [exchange_plane(): return lax.all_to_all(blocks, PLANE, 0, 0, tiled=True)]
    pallas_call x2 -> x8, Pallas kernels: 9.92 us -> 23 us  [the longest x2 15.6 us: forward(): pl.pallas_call(forward_kernel, grid=(4,), in_specs=[pl.BlockSpec(memory_s...]
  transfers between devices with their start and end apart: 8 -> 15, of which waited for: 7 -> 10; matrix products, arithmetic and copies ran while one was open for 3% -> 1% of each run, Pallas kernels for 6% -> 10%
where the time goes in v3:
time: 413 us; the launch traced here: 412 us
  waiting for transfers between devices  190 us (46%)
  blocking collectives  84.7 us (21%)
  starting transfers between devices  54.3 us (13%)
  Pallas kernels  53.1 us (13%)
  local copies, waits for them, and re-layouts  15.5 us (4%)
  between operations  13.6 us (3%)
    all_to_all x6, waiting for transfers between devices, exchange_plane(): return lax.all_to_all(blocks, PLANE, 0, 0, tiled=True)  129 us
    all_to_all x2, blocking collectives, exchange_plane(): return lax.all_to_all(blocks, PLANE, 0, 0, tiled=True)  58.3 us
    all_to_all x6, starting transfers between devices, exchange_plane(): return lax.all_to_all(blocks, PLANE, 0, 0, tiled=True)  39.7 us
    all_gather x1, waiting for transfers between devices, shards(): halves.append(lax.all_gather(second, 'z', axis=0, tiled=False))  33.8 us
    all_to_all x1, blocking collectives, exchange_z(): return lax.all_to_all(blocks, 'z', 0, 0, tiled=True)  26.5 us
    pallas_call x2, Pallas kernels, forward(): pl.pallas_call(forward_kernel, grid=(4,), in_specs=[pl.BlockSpec(memory_s...  15.6 us
    pallas_call x2, Pallas kernels, inverse(): pl.pallas_call(inverse_kernel, grid=(4,), in_specs=[SPECTRA, BANDS, whole...  15.4 us
    pallas_call x2, Pallas kernels, filtered(): pl.pallas_call(filter_kernel, grid=(3,), in_specs=[COLUMNS, pl.BlockSpec(...  14.8 us
  transfers between devices with their start and end apart: 15, of which 10 were waited for; matrix products, arithmetic and copies ran while one was open for 1% of the time, Pallas kernels for 10%

profile of v3, /device:TPU:1, one launch (start us, length us, event | category | flops | bytes accessed | tf_op | source)
XLA Modules:
  0.0 411.8 jit_solution(12544512481017934887)
XLA Ops:
  6.5 1.3 copy-done.3
  7.8 1.2 pack.4
  9.0 8.6 %all-to-all-start = ((f32[32,56,128]{2,1,0:T(8,128)}), f32[32,56,128]{2,1,0:T(8,128)S(1)}, u32[]{:S(2)}, u32[]{:S(2)}) async-start(f32[32,56,128]{2,1,0:T(8,128)} %pack.4), calls=%async_computation | async-start | bytes 1835008 | tf_op jit(solution)/shard_map/all_to_all | solution.py:309
  17.6 2.7 slice_bitcast_fusion
  20.3 0.9 pack.3
  21.2 1.2 copy-done
  22.4 10.8 %all-to-all-done = f32[32,56,128]{2,1,0:T(8,128)S(1)} async-done(((f32[32,56,128]{2,1,0:T(8,128)}), f32[32,56,128]{2,1,0:T(8,128)S(1)}, u32[]{:S(2)}, u32[]{:S(2)}) %all-to-all-start) | async-done | bytes 917536 | tf_op jit(solution)/shard_map/all_to_all | solution.py:309
  33.3 4.5 %all-to-all-start.1 = ((f32[32,112,128]{2,1,0:T(8,128)}), f32[32,112,128]{2,1,0:T(8,128)}, u32[]{:S(2)}, u32[]{:S(2)}) async-start(f32[32,112,128]{2,1,0:T(8,128)} %copy-done), calls=%async_computation.1 | async-start | bytes 3670016 | tf_op jit(solution)/shard_map/all_to_all | solution.py:309
  37.9 0.7 slots.1
  38.6 0.6 copy-done.6
  39.3 1.6 collective-permute-start
  40.9 3.0 collective-permute-start.1
  43.9 5.8 %collective-permute-start.3 = (f32[24,1152]{1,0:T(8,128)S(1)}, f32[24,1152]{1,0:T(8,128)S(1)}, u32[]{:S(2)}, u32[]{:S(2)}) collective-permute-start(f32[24,1152]{1,0:T(8,128)S(1)} %get-tuple-element.32), channel_id=1, source_target_pairs={{0,8},{2,10},{4,12},{6,14},{8,0},{10,2},{12,4},{14,6},{1,9},{3,11}... | collective-permute-start | bytes 331784 | tf_op jit(solution)/shard_map/ppermute | solution.py:319
  49.7 4.0 collective-permute-start.5
  53.8 0.9 pack.5
  54.7 1.3 copy-done.1
  56.0 4.2 %collective-permute-done.3.refs_4_ = f32[24,1152]{1,0:T(8,128)S(1)} collective-permute-done((f32[24,1152]{1,0:T(8,128)S(1)}, f32[24,1152]{1,0:T(8,128)S(1)}, u32[]{:S(2)}, u32[]{:S(2)}) %collective-permute-start.3) | collective-permute-done | bytes 110624 | tf_op jit(solution)/shard_map/ppermute | solution.py:319
  60.2 6.1 %collective-permute-done.4.refs_5_ = f32[24,1152]{1,0:T(8,128)S(1)} collective-permute-done((f32[24,1152]{1,0:T(8,128)S(1)}, f32[24,1152]{1,0:T(8,128)S(1)}, u32[]{:S(2)}, u32[]{:S(2)}) %collective-permute-start.4) | collective-permute-done | bytes 110624 | tf_op jit(solution)/shard_map/ppermute | solution.py:319
  66.2 3.6 collective-permute-done.6.refs_7_
  69.8 2.3 choose.2
  72.2 33.8 %all_to_all.45 = f32[32,112,128]{2,1,0:T(8,128)S(1)} all-to-all(f32[32,112,128]{2,1,0:T(8,128)S(1)} %copy-done.2), channel_id=1, replica_groups=mesh['x_lo'=2,'y'=4,'x_hi'=2,'z'=8,'core'=2] {'x_lo','y','x_hi','core'}, dimensions={0} | all-to-all | bytes 3670016 | tf_op jit(solution)/shard_map/all_to_all | solution.py:309
  106.0 1.4 choose.3
  107.4 13.4 %all-gather.7.cloned.1.call-done = f32[32,24,1152]{2,1,0:T(8,128)} async-done(((f32[4,24,1152]{2,1,0:T(8,128)}), f32[32,24,1152]{2,1,0:T(8,128)}) %all-gather.7.cloned.1.call-update) | async-done | bytes 3538960 | tf_op jit(solution)/shard_map/all_gather | solution.py:333
  120.8 7.8 %forward.3 = f32[4,8,9,24,128]{4,3,2,1,0:T(8,128)} custom-call(s32[8]{0:T(128)} %copy-done.5, f32[24,1152]{1,0:T(8,128)} %copy-done.6, f32[24,1152]{1,0:T(8,128)} %copy-done.9, f32[24,1152]{1,0:T(8,128)} %copy-done.10, f32[24,1152]{1,0:T(8,128)} %copy-done.11, f32[24,1152]{1,0:T(8,128)} %copy-done.12, f32[24,1152]{1,0:T(8,128)} %copy-done.13, ...), custom_call_target="tpu_custom_call" | custom-call | flops 16000000000 | bytes 10000000 | tf_op jit(solution)/shard_map/forward/pallas_call | solution.py:243
  128.6 7.5 %all-to-all-start.5 = ((f32[32,216,128]{2,1,0:T(8,128)}), f32[32,216,128]{2,1,0:T(8,128)S(1)}, u32[]{:S(2)}, u32[]{:S(2)}) async-start(f32[32,216,128]{2,1,0:T(8,128)} %bitcast.29), calls=%async_computation.5 | async-start | bytes 7077888 | tf_op jit(solution)/shard_map/all_to_all | solution.py:309
  136.1 33.8 %all-gather.5.cloned.1.call-done = f32[32,24,1152]{2,1,0:T(8,128)} async-done(((f32[4,24,1152]{2,1,0:T(8,128)}), f32[32,24,1152]{2,1,0:T(8,128)}) %all-gather.5.cloned.1.call-update) | async-done | bytes 3538960 | tf_op jit(solution)/shard_map/all_gather | solution.py:335
  169.9 7.8 %forward.2 = f32[4,8,9,24,128]{4,3,2,1,0:T(8,128)} custom-call(s32[8]{0:T(128)} %copy-done.5, f32[24,1152]{1,0:T(8,128)} %copy-done.6, f32[24,1152]{1,0:T(8,128)} %copy-done.9, f32[24,1152]{1,0:T(8,128)} %copy-done.10, f32[24,1152]{1,0:T(8,128)} %copy-done.11, f32[24,1152]{1,0:T(8,128)} %copy-done.12, f32[24,1152]{1,0:T(8,128)} %copy-done.13, ...), custom_call_target="tpu_custom_call" | custom-call | flops 16000000000 | bytes 10000000 | tf_op jit(solution)/shard_map/forward/pallas_call | solution.py:243
  177.7 4.5 %all-to-all-done.5 = f32[32,216,128]{2,1,0:T(8,128)S(1)} async-done(((f32[32,216,128]{2,1,0:T(8,128)}), f32[32,216,128]{2,1,0:T(8,128)S(1)}, u32[]{:S(2)}, u32[]{:S(2)}) %all-to-all-start.5) | async-done | bytes 3538976 | tf_op jit(solution)/shard_map/all_to_all | solution.py:309
  182.2 1.8 copy-done.7
  184.0 6.4 %all-to-all-start.3 = ((f32[32,216,128]{2,1,0:T(8,128)}), f32[32,216,128]{2,1,0:T(8,128)}, u32[]{:S(2)}, u32[]{:S(2)}) async-start(f32[32,216,128]{2,1,0:T(8,128)} %bitcast.27), calls=%async_computation.3 | async-start | bytes 7077888 | tf_op jit(solution)/shard_map/all_to_all | solution.py:309
  190.6 0.6 reshape.107.pair_ref
  191.3 0.7 fusion.2.wave_ref
  191.9 7.3 %filter.3 = f32[32,9,24,128]{3,2,1,0:T(8,128)} custom-call(f32[32,9,24,128]{3,2,1,0:T(8,128)} %bitcast.26, f32[3,1,1536]{2,1,0:T(1,128)} %reshape.107.pair_ref, f32[192,1]{1,0:T(8,128)} %fusion.2.wave_ref, bf16[2,192,192]{2,1,0:T(8,128)(2,1)} %constant.70.clone.to_ref, bf16[2,192,192]{2,1,0:T(8,128)(2,1)} %constant.71.clone.from_ref), custom_call_target="tpu_custom_call" | custom-call | flops 16000000000 | bytes 10000000 | tf_op jit(solution)/shard_map/filter/pallas_call | solution.py:282
  199.2 37.3 %all-to-all-done.3 = f32[32,216,128]{2,1,0:T(8,128)} async-done(((f32[32,216,128]{2,1,0:T(8,128)}), f32[32,216,128]{2,1,0:T(8,128)}, u32[]{:S(2)}, u32[]{:S(2)}) %all-to-all-start.3) | async-done | bytes 3538976 | tf_op jit(solution)/shard_map/all_to_all | solution.py:309
  236.5 6.3 %all-to-all-start.6 = ((f32[32,216,128]{2,1,0:T(8,128)}), f32[32,216,128]{2,1,0:T(8,128)S(1)}, u32[]{:S(2)}, u32[]{:S(2)}) async-start(f32[32,216,128]{2,1,0:T(8,128)} %bitcast.31), calls=%async_computation.6 | async-start | bytes 7077888 | tf_op jit(solution)/shard_map/all_to_all | solution.py:309
  242.9 7.5 %filter.2 = f32[32,9,24,128]{3,2,1,0:T(8,128)} custom-call(f32[32,9,24,128]{3,2,1,0:T(8,128)} %bitcast.7.columns_ref, f32[3,1,1536]{2,1,0:T(1,128)} %reshape.107.pair_ref, f32[192,1]{1,0:T(8,128)} %fusion.2.wave_ref, bf16[2,192,192]{2,1,0:T(8,128)(2,1)} %constant.70.clone.to_ref, bf16[2,192,192]{2,1,0:T(8,128)(2,1)} %constant.71.clone.from_ref), custom_call_target="tpu_custom_call" | custom-call | flops 16000000000 | bytes 10000000 | tf_op jit(solution)/shard_map/filter/pallas_call | solution.py:282
  250.3 38.6 %all-to-all-done.6 = f32[32,216,128]{2,1,0:T(8,128)S(1)} async-done(((f32[32,216,128]{2,1,0:T(8,128)}), f32[32,216,128]{2,1,0:T(8,128)S(1)}, u32[]{:S(2)}, u32[]{:S(2)}) %all-to-all-start.6) | async-done | bytes 3538976 | tf_op jit(solution)/shard_map/all_to_all | solution.py:309
  288.9 1.8 copy-done.8
  290.7 6.4 %all-to-all-start.4 = ((f32[32,216,128]{2,1,0:T(8,128)}), f32[32,216,128]{2,1,0:T(8,128)}, u32[]{:S(2)}, u32[]{:S(2)}) async-start(f32[32,216,128]{2,1,0:T(8,128)} %bitcast.30), calls=%async_computation.4 | async-start | bytes 7077888 | tf_op jit(solution)/shard_map/all_to_all | solution.py:309
  297.1 1.0 broadcast_in_dim.4.sum_ref
  298.1 7.7 %inverse.2.sum_ref = f32[192,1152]{1,0:T(8,128)} custom-call(f32[4,8,9,24,128]{4,3,2,1,0:T(8,128)} %bitcast.28, f32[8,4,24,1152]{3,2,1,0:T(8,128)} %bitcast.34, f32[192,1152]{1,0:T(8,128)} %broadcast_in_dim.4.sum_ref, bf16[2,256,256]{2,1,0:T(8,128)(2,1)} %constant.67.clone.refs_9_.even_ref, bf16[2,256,256]{2,1,0:T(8,128)(2,1)} %constant.72.clone.odd_ref, ...), custom_call_target="tpu_custom_call" | custom-call | flops 16000000000 | bytes 10000000 | tf_op jit(solution)/shard_map/inverse/pallas_call | solution.py:267
  305.8 37.5 %all-to-all-done.4 = f32[32,216,128]{2,1,0:T(8,128)} async-done(((f32[32,216,128]{2,1,0:T(8,128)}), f32[32,216,128]{2,1,0:T(8,128)}, u32[]{:S(2)}, u32[]{:S(2)}) %all-to-all-start.4) | async-done | bytes 3538976 | tf_op jit(solution)/shard_map/all_to_all | solution.py:309
  343.2 7.7 %inverse.3 = f32[192,1152]{1,0:T(8,128)} custom-call(f32[4,8,9,24,128]{4,3,2,1,0:T(8,128)} %bitcast.9.spectrum_ref, f32[8,4,24,1152]{3,2,1,0:T(8,128)} %bitcast.36, f32[192,1152]{1,0:T(8,128)} %inverse.2.sum_ref, bf16[2,256,256]{2,1,0:T(8,128)(2,1)} %constant.67.clone.refs_9_.even_ref, bf16[2,256,256]{2,1,0:T(8,128)(2,1)} %constant.72.clone.odd_ref, ...), custom_call_target="tpu_custom_call" | custom-call | flops 16000000000 | bytes 10000000 | tf_op jit(solution)/shard_map/inverse/pallas_call | solution.py:267
  350.9 1.2 reshape.114
  352.2 26.5 %all_to_all.46 = f32[8,216,128]{2,1,0:T(8,128)S(1)} all-to-all(f32[8,216,128]{2,1,0:T(8,128)S(1)} %reshape.114), channel_id=1, replica_groups=mesh['x_lo'=2,'y'=4,'x_hi'=2,'z'=8,'core'=2] {'z'}, dimensions={0} | all-to-all | bytes 1769472 | tf_op jit(solution)/shard_map/all_to_all | solution.py:313
  378.7 24.5 %all_to_all.47 = f32[32,54,128]{2,1,0:T(8,128)S(1)} all-to-all(f32[32,54,128]{2,1,0:T(8,128)S(1)} %reshape.115), channel_id=1, replica_groups=mesh['x_lo'=2,'y'=4,'x_hi'=2,'z'=8,'core'=2] {'x_lo','y','x_hi','core'}, dimensions={0} | all-to-all | bytes 1769472 | tf_op jit(solution)/shard_map/all_to_all | solution.py:309
  403.2 0.5 reshape.116
  403.8 1.2 reshape.117
  (49 shorter events, 0.6 us)
Async XLA Ops:
  6.5 1.3 copy-start.3
  9.0 24.3 %all-to-all-start = ((f32[32,56,128]{2,1,0:T(8,128)}), f32[32,56,128]{2,1,0:T(8,128)S(1)}, u32[]{:S(2)}, u32[]{:S(2)}) async-start(f32[32,56,128]{2,1,0:T(8,128)} %pack.4), calls=%async_computation | async-start | bytes 1835008 | tf_op jit(solution)/shard_map/all_to_all | solution.py:309
  21.2 1.2 copy-start
  22.4 47.3 %copy-start.4 = (s32[2]{0:T(128)S(1)}, s32[2]{0:T(128)}, u32[]{:S(2)}) copy-start(s32[2]{0:T(128)} %owner_ref.3) | copy-start | bytes 28
  33.3 36.5 %all-to-all-start.1 = ((f32[32,112,128]{2,1,0:T(8,128)}), f32[32,112,128]{2,1,0:T(8,128)}, u32[]{:S(2)}, u32[]{:S(2)}) async-start(f32[32,112,128]{2,1,0:T(8,128)} %copy-done), calls=%async_computation.1 | async-start | bytes 3670016 | tf_op jit(solution)/shard_map/all_to_all | solution.py:309
  37.8 83.0 %all-gather.7.cloned.1.call-start = ((), (), s32[]{:S(2)}) async-start(), calls=%async_computation.10 | async-start | bytes 3981312 | tf_op jit(solution)/shard_map/all_gather | solution.py:333
  37.9 34.3 %copy-start.5 = (s32[8]{0:T(128)}, s32[8]{0:T(128)S(1)}, u32[]{:S(2)}) copy-start(s32[8]{0:T(128)S(1)} %iota_xor_fusion.slots_ref) | copy-start | bytes 100
  38.6 0.7 copy-start.6
  39.3 10.5 %collective-permute-start = (f32[24,1152]{1,0:T(8,128)S(1)}, f32[24,1152]{1,0:T(8,128)S(1)}, u32[]{:S(2)}, u32[]{:S(2)}) collective-permute-start(f32[24,1152]{1,0:T(8,128)S(1)} %get-tuple-element.29), channel_id=1, source_target_pairs={{0,2},{2,0},{4,6},{6,4},{8,10},{10,8},{12,14},{14,12},{1,3},{3,1},... | collective-permute-start | bytes 331784 | tf_op jit(solution)/shard_map/ppermute | solution.py:319
  40.9 12.9 %collective-permute-start.1 = (f32[24,1152]{1,0:T(8,128)S(1)}, f32[24,1152]{1,0:T(8,128)S(1)}, u32[]{:S(2)}, u32[]{:S(2)}) collective-permute-start(f32[24,1152]{1,0:T(8,128)S(1)} %get-tuple-element.30), channel_id=1, source_target_pairs={{0,4},{2,6},{4,0},{6,2},{8,12},{10,14},{12,8},{14,10},{1,5},{3,7},... | collective-permute-start | bytes 331784 | tf_op jit(solution)/shard_map/ppermute | solution.py:319
  43.9 12.1 %collective-permute-start.2 = (f32[24,1152]{1,0:T(8,128)S(1)}, f32[24,1152]{1,0:T(8,128)S(1)}, u32[]{:S(2)}, u32[]{:S(2)}) collective-permute-start(f32[24,1152]{1,0:T(8,128)S(1)} %get-tuple-element.31), channel_id=1, source_target_pairs={{0,6},{2,4},{4,2},{6,0},{8,14},{10,12},{12,10},{14,8},{1,7},{3,5},... | collective-permute-start | bytes 331784 | tf_op jit(solution)/shard_map/ppermute | solution.py:319
  43.9 16.2 %collective-permute-start.3 = (f32[24,1152]{1,0:T(8,128)S(1)}, f32[24,1152]{1,0:T(8,128)S(1)}, u32[]{:S(2)}, u32[]{:S(2)}) collective-permute-start(f32[24,1152]{1,0:T(8,128)S(1)} %get-tuple-element.32), channel_id=1, source_target_pairs={{0,8},{2,10},{4,12},{6,14},{8,0},{10,2},{12,4},{14,6},{1,9},{3,11}... | collective-permute-start | bytes 331784 | tf_op jit(solution)/shard_map/ppermute | solution.py:319
  49.7 16.5 %collective-permute-start.4 = (f32[24,1152]{1,0:T(8,128)S(1)}, f32[24,1152]{1,0:T(8,128)S(1)}, u32[]{:S(2)}, u32[]{:S(2)}) collective-permute-start(f32[24,1152]{1,0:T(8,128)S(1)} %get-tuple-element.33), channel_id=1, source_target_pairs={{0,10},{2,8},{4,14},{6,12},{8,2},{10,0},{12,6},{14,4},{1,11},{3,9}... | collective-permute-start | bytes 331784 | tf_op jit(solution)/shard_map/ppermute | solution.py:319
  49.7 56.3 %copy-start.9 = (f32[24,1152]{1,0:T(8,128)}, f32[24,1152]{1,0:T(8,128)S(1)}, u32[]{:S(2)}) copy-start(f32[24,1152]{1,0:T(8,128)S(1)} %collective-permute-done.refs_1_) | copy-start | bytes 331780
  49.7 16.5 %collective-permute-start.5 = (f32[24,1152]{1,0:T(8,128)S(1)}, f32[24,1152]{1,0:T(8,128)S(1)}, u32[]{:S(2)}, u32[]{:S(2)}) collective-permute-start(f32[24,1152]{1,0:T(8,128)S(1)} %get-tuple-element.34), channel_id=1, source_target_pairs={{0,12},{2,14},{4,8},{6,10},{8,4},{10,6},{12,0},{14,2},{1,13},{3,15... | collective-permute-start | bytes 331784 | tf_op jit(solution)/shard_map/ppermute | solution.py:319
  53.8 52.2 %copy-start.10 = (f32[24,1152]{1,0:T(8,128)}, f32[24,1152]{1,0:T(8,128)S(1)}, u32[]{:S(2)}) copy-start(f32[24,1152]{1,0:T(8,128)S(1)} %collective-permute-done.1.refs_2_) | copy-start | bytes 331780
  53.8 16.0 %collective-permute-start.6 = (f32[24,1152]{1,0:T(8,128)S(1)}, f32[24,1152]{1,0:T(8,128)S(1)}, u32[]{:S(2)}, u32[]{:S(2)}) collective-permute-start(f32[24,1152]{1,0:T(8,128)S(1)} %get-tuple-element.35), channel_id=1, source_target_pairs={{0,14},{2,12},{4,10},{6,8},{8,6},{10,4},{12,2},{14,0},{1,15},{3,13... | collective-permute-start | bytes 331784 | tf_op jit(solution)/shard_map/ppermute | solution.py:319
  54.7 1.3 copy-start.1
  56.0 51.4 %copy-start.11 = (f32[24,1152]{1,0:T(8,128)}, f32[24,1152]{1,0:T(8,128)S(1)}, u32[]{:S(2)}) copy-start(f32[24,1152]{1,0:T(8,128)S(1)} %collective-permute-done.2.refs_3_) | copy-start | bytes 331780
  56.0 16.2 %copy-start.2 = (f32[32,112,128]{2,1,0:T(8,128)S(1)}, f32[32,112,128]{2,1,0:T(8,128)}, u32[]{:S(2)}) copy-start(f32[32,112,128]{2,1,0:T(8,128)} %copy-done.1) | copy-start | bytes 5505028
  60.2 47.2 %copy-start.12 = (f32[24,1152]{1,0:T(8,128)}, f32[24,1152]{1,0:T(8,128)S(1)}, u32[]{:S(2)}) copy-start(f32[24,1152]{1,0:T(8,128)S(1)} %collective-permute-done.3.refs_4_) | copy-start | bytes 331780
  66.2 41.2 %copy-start.13 = (f32[24,1152]{1,0:T(8,128)}, f32[24,1152]{1,0:T(8,128)S(1)}, u32[]{:S(2)}) copy-start(f32[24,1152]{1,0:T(8,128)S(1)} %collective-permute-done.4.refs_5_) | copy-start | bytes 331780
  66.2 41.2 %copy-start.14 = (f32[24,1152]{1,0:T(8,128)}, f32[24,1152]{1,0:T(8,128)S(1)}, u32[]{:S(2)}) copy-start(f32[24,1152]{1,0:T(8,128)S(1)} %collective-permute-done.5.refs_6_) | copy-start | bytes 331780
  69.8 37.6 %copy-start.15 = (f32[24,1152]{1,0:T(8,128)}, f32[24,1152]{1,0:T(8,128)S(1)}, u32[]{:S(2)}) copy-start(f32[24,1152]{1,0:T(8,128)S(1)} %collective-permute-done.6.refs_7_) | copy-start | bytes 331780
  72.2 97.8 %all-gather.5.cloned.1.call-start = ((), (), s32[]{:S(2)}) async-start(), calls=%async_computation.9 | async-start | bytes 3981312 | tf_op jit(solution)/shard_map/all_gather | solution.py:335
  128.6 53.6 %all-to-all-start.5 = ((f32[32,216,128]{2,1,0:T(8,128)}), f32[32,216,128]{2,1,0:T(8,128)S(1)}, u32[]{:S(2)}, u32[]{:S(2)}) async-start(f32[32,216,128]{2,1,0:T(8,128)} %bitcast.29), calls=%async_computation.5 | async-start | bytes 7077888 | tf_op jit(solution)/shard_map/all_to_all | solution.py:309
  182.2 1.8 copy-start.7
  184.0 52.5 %all-to-all-start.3 = ((f32[32,216,128]{2,1,0:T(8,128)}), f32[32,216,128]{2,1,0:T(8,128)}, u32[]{:S(2)}, u32[]{:S(2)}) async-start(f32[32,216,128]{2,1,0:T(8,128)} %bitcast.27), calls=%async_computation.3 | async-start | bytes 7077888 | tf_op jit(solution)/shard_map/all_to_all | solution.py:309
  236.5 52.4 %all-to-all-start.6 = ((f32[32,216,128]{2,1,0:T(8,128)}), f32[32,216,128]{2,1,0:T(8,128)S(1)}, u32[]{:S(2)}, u32[]{:S(2)}) async-start(f32[32,216,128]{2,1,0:T(8,128)} %bitcast.31), calls=%async_computation.6 | async-start | bytes 7077888 | tf_op jit(solution)/shard_map/all_to_all | solution.py:309
  288.9 1.8 copy-start.8
  290.7 52.5 %all-to-all-start.4 = ((f32[32,216,128]{2,1,0:T(8,128)}), f32[32,216,128]{2,1,0:T(8,128)}, u32[]{:S(2)}, u32[]{:S(2)}) async-start(f32[32,216,128]{2,1,0:T(8,128)} %bitcast.30), calls=%async_computation.4 | async-start | bytes 7077888 | tf_op jit(solution)/shard_map/all_to_all | solution.py:309
Sparse Core Ops, SparseCore 0:
  72.3 48.4 all-gather.6
  122.6 47.2 all-gather.4

commit v4 on v3

--- a/solution.py
+++ b/solution.py
@@ -14,7 +14,7 @@
 LANES = 6 * N
 TILES = LANES // 128
 PLANE = ("x_lo", "y", "x_hi", "core")
-VMEM = 60 * 1024 * 1024
+VMEM = 62 * 1024 * 1024
 
 
 def cas_matrix():
@@ -125,27 +125,57 @@
         out_ref[0, :, tile] = spectrum[:, 128 * tile : 128 * tile + 128].reshape(8, 24, 128)
 
 
-def inverse_kernel(spectrum_ref, band_ref, sum_ref, even_ref, odd_ref, rows_ref, out_ref):
-    member = pl.program_id(0)
+def inverse_kernel(spectrum_ref, first_ref, last_ref, even_ref, odd_ref, rows_ref, out_ref, total_ref):
+    step = pl.program_id(0)
     spectrum = jnp.concatenate(
-        [spectrum_ref[0, :, tile].reshape(N, 128) for tile in range(TILES)], axis=1
+        [spectrum_ref[0, :, 0, tile].reshape(N, 128) for tile in range(TILES)], axis=1
     )
     potential = product((rows_ref[0], rows_ref[1]), split(spectrum))
     potential = lane_transform(potential, even_ref, odd_ref)
     prefactor = -1.0 / math.sqrt(N * 8)
-    weight = jnp.where(member < 2, prefactor, 2.0 * prefactor)
-    term = (weight * band_ref[:, 0].reshape(N, LANES)) * potential
-
-    @pl.when(member == 0)
+    potential = jnp.where(step % 4 < 2, prefactor, 2.0 * prefactor) * potential
+
+    @pl.when(step == 0)
     def _():
-        out_ref[...] = sum_ref[...] + term
-
-    @pl.when(member > 0)
+        total_ref[...] = first_ref[:, 0].reshape(N, LANES) * potential
+
+    @pl.when((step > 0) & (step < 4))
     def _():
-        out_ref[...] += term
-
-
-def filter_kernel(columns_ref, pair_ref, wave_ref, to_ref, from_ref, out_ref):
+        total_ref[...] += first_ref[:, 0].reshape(N, LANES) * potential
+
+    @pl.when(step >= 4)
+    def _():
+        total_ref[...] += last_ref[:, 0].reshape(N, LANES) * potential
+
+    @pl.when(step == 7)
+    def _():
+        for z in range(8):
+            for source in range(4):
+                rows = pl.ds(24 * z + 6 * source, 6)
+                for tile in range(TILES):
+                    block = total_ref[rows, 128 * tile : 128 * tile + 128]
+                    out_ref[z, 56 * source + 6 * tile : 56 * source + 6 * tile + 6, :] = block
+
+
+def unpack_kernel(blocks_ref, out_ref, left_ref, right_ref):
+    source = blocks_ref.reshape(32 * 56, 128)
+    lower = lax.broadcasted_iota(jnp.int32, (32, 128), 1) < 64
+    for a in range(6):
+        left, right = left_ref.at[a % 2], right_ref.at[a % 2]
+        for h in range(3):
+            tiles = [source[pl.ds(18 * h + 6 * k + a, 32, stride=56), :] for k in range(3)]
+            even, odd = pl.ds(2 * h, 32, stride=6), pl.ds(2 * h + 1, 32, stride=6)
+            turned = pltpu.roll(tiles[2], 64, 1)
+            left[even, :] = tiles[0]
+            right[even, :] = tiles[1]
+            left[odd, :] = jnp.where(lower, pltpu.roll(tiles[1], 64, 1), turned)
+            right[odd, :] = turned
+        out_ref[0, a, :, :128] = left[...]
+        out_ref[0, a, :, 128:] = right[:, :64]
+
+
+def filter_kernel(columns_ref, pair_ref, wave_ref, to_ref, from_ref, *refs):
+    out_ref = refs[-1]
     source = columns_ref.reshape(32 * TILES * 8, 128)
     target = out_ref.reshape(32 * TILES * 8, 128)
     lower = lax.broadcasted_iota(jnp.int32, (32, 128), 1) < 64
@@ -182,7 +212,7 @@
 
 
 def whole(array):
-    return pl.BlockSpec(array.shape, lambda step: (0,) * array.ndim)
+    return pl.BlockSpec(array.shape, lambda step: (0,) * len(array.shape))
 
 
 PARAMS = pltpu.CompilerParams(vmem_limit_bytes=VMEM)
@@ -196,16 +226,29 @@
 MOVED = pl.CostEstimate(flops=0, bytes_accessed=4 * 10**6, transcendentals=0)
 
 
-def to_blocks(planes):
-    rows = 56 * planes.shape[0]
+def to_blocks(planes, count, part):
     return pl.pallas_call(
         pack_kernel,
-        out_shape=jax.ShapeDtypeStruct((32, rows, 128), jnp.float32),
+        grid=(1,),
+        in_specs=[pl.BlockSpec((count, 6, N, N), lambda step: (part, 0, 0, 0))],
+        out_specs=pl.BlockSpec((32, 56 * count, 128), lambda step: (0, 0, 0)),
+        out_shape=jax.ShapeDtypeStruct((32, 56 * count, 128), jnp.float32),
+        scratch_shapes=[pltpu.VMEM((2, N, 128), jnp.float32)] * 2,
+        compiler_params=PARAMS,
+        cost_estimate=MOVED,
+        name="pack",
+    )(planes)
+
+
+def from_blocks(blocks):
+    return pl.pallas_call(
+        unpack_kernel,
+        out_shape=jax.ShapeDtypeStruct((1, 6, N, N), jnp.float32),
         scratch_shapes=[pltpu.VMEM((2, N, 128), jnp.float32)] * 2,
         compiler_params=MOVES,
         cost_estimate=MOVED,
-        name="pack",
-    )(planes)
+        name="unpack",
+    )(blocks)
 
 
 def by_slots(slots, spread):
@@ -260,35 +303,46 @@
     )(slots, *pieces, bands, even, odd, rows)
 
 
-def inverse(spectra, bands, total):
+def inverse(spectra, bands):
     even, odd = lane_matrices()
     even, odd = jnp.asarray(two_terms(even)), jnp.asarray(two_terms(odd.T))
     rows = jnp.asarray(two_terms(cas_matrix()[held_order(), :]))
+    out = jax.ShapeDtypeStruct((8, 224, 128), jnp.float32)
     return pl.pallas_call(
         inverse_kernel,
-        grid=(4,),
-        in_specs=[SPECTRA, BANDS, whole(total), whole(even), whole(odd), whole(rows)],
-        out_specs=whole(total),
-        out_shape=jax.ShapeDtypeStruct((N, LANES), jnp.float32),
+        grid=(8,),
+        in_specs=[
+            pl.BlockSpec((1, 8, 1, TILES, 24, 128), lambda step: (step % 4, 0, step // 4, 0, 0, 0)),
+            pl.BlockSpec((8, 1, 24, LANES), lambda step: (0, jnp.minimum(step, 3), 0, 0)),
+            pl.BlockSpec((8, 1, 24, LANES), lambda step: (0, jnp.maximum(step - 4, 0), 0, 0)),
+            whole(even),
+            whole(odd),
+            whole(rows),
+        ],
+        out_specs=whole(out),
+        out_shape=out,
+        scratch_shapes=[pltpu.VMEM((N, LANES), jnp.float32)],
         compiler_params=PARAMS,
         cost_estimate=COST,
         name="inverse",
-    )(spectra, bands, total, even, odd, rows)
-
-
-def filtered(columns, pair_wave, wave):
+    )(spectra, *bands, even, odd, rows)
+
+
+def filtered(columns, pair_wave, wave, half, *earlier):
     to = jnp.asarray(two_terms(cas_matrix()[:, column_order()]))
     back = jnp.asarray(two_terms(cas_matrix()[column_order(), :]))
+    waves = pl.BlockSpec((1, 1, 8 * N), lambda step: (step, 0, 0))
     return pl.pallas_call(
         filter_kernel,
         grid=(3,),
-        in_specs=[COLUMNS, pl.BlockSpec((1, 1, 8 * N), lambda step: (step, 0, 0)), whole(wave), whole(to), whole(back)],
-        out_specs=COLUMNS,
-        out_shape=jax.ShapeDtypeStruct((32, TILES, 24, 128), jnp.float32),
+        in_specs=[COLUMNS, waves, whole(wave), whole(to), whole(back), *[pl.BlockSpec(memory_space=pl.ANY) for _ in earlier]],
+        out_specs=pl.BlockSpec((32, 1, TILES, 8, 128), lambda step: (0, half, 0, step, 0)),
+        out_shape=jax.ShapeDtypeStruct((32, 2, TILES, 24, 128), jnp.float32),
+        input_output_aliases={5: 0} if earlier else {},
         compiler_params=PARAMS,
         cost_estimate=COST,
         name="filter",
-    )(columns, pair_wave, wave, to, back)
+    )(columns, pair_wave, wave, to, back, *earlier)
 
 
 def wavenumber(index):
@@ -323,29 +377,25 @@
 def shards(resident, owned, owner):
     pair_wave, wave = filter_waves(lax.axis_index(PLANE))
     slots = lax.axis_index("z") ^ jnp.arange(8, dtype=jnp.int32)
-    spread = exchange_plane(to_blocks(resident))
-    first, second = to_blocks(owned[0, :2]), to_blocks(owned[0, 2:])
-    first, spread = lax.optimization_barrier((first, spread))
+    first = exchange_plane(to_blocks(owned[0], 2, 0))
+    spread, first = lax.optimization_barrier((to_blocks(resident, 1, 0), first))
+    halves = [lax.all_gather(choose(owner, first.reshape(8, 4, 112, 128)), "z", axis=0, tiled=False)]
+    spread = exchange_plane(spread)
+    second, spread = lax.optimization_barrier((to_blocks(owned[0], 2, 1), spread))
     orbital = gather_orbital(spread.reshape(8, 4, 56, 128), slots)
-    first, orbital = lax.optimization_barrier((exchange_plane(first), orbital))
-    first = choose(owner, first.reshape(8, 4, 112, 128))
-    second, first = lax.optimization_barrier((second, first))
-    halves = [lax.all_gather(first, "z", axis=0, tiled=False)]
-    second = choose(owner, exchange_plane(second).reshape(8, 4, 112, 128))
+    second, orbital = lax.optimization_barrier((exchange_plane(second), orbital))
+    second = choose(owner, second.reshape(8, 4, 112, 128))
     halves.append(lax.all_gather(second, "z", axis=0, tiled=False))
     spectra = []
     for bands in halves:
         spectra.append(exchange_plane(forward(slots, orbital, bands).reshape(32, 216, 128)))
-    potentials = []
-    for columns in spectra:
-        columns = filtered(columns.reshape(32, TILES, 24, 128), pair_wave, wave)
-        potentials.append(exchange_plane(columns.reshape(32, 216, 128)))
-    total = jnp.zeros((N, LANES), jnp.float32)
-    for bands, potential in zip(halves, potentials):
-        total = inverse(potential.reshape(4, 8, TILES, 24, 128), bands, total)
-    back = exchange_z(total.reshape(8, 216, 128))
-    back = exchange_plane(back.reshape(32, 54, 128))
-    return back.reshape(32, 6, 6, N).transpose(1, 0, 2, 3).reshape(1, 6, N, N)
+    columns = []
+    for half, arrived in enumerate(spectra):
+        columns = [filtered(arrived.reshape(32, TILES, 24, 128), pair_wave, wave, half, *columns)]
+    potentials = exchange_plane(columns[0].reshape(32, 432, 128))
+    total = inverse(potentials.reshape(4, 8, 2, TILES, 24, 128), halves)
+    back = exchange_plane(exchange_z(total).reshape(32, 56, 128))
+    return from_blocks(back)
 
 
 def solution(mesh):

time: 413 us -> 396 us (0.959)
  waiting for transfers between devices: 190 us -> 133 us
  blocking collectives: 84.7 us -> 137 us
  local copies, waits for them, and re-layouts: 15.5 us -> 0.74 us
  Pallas kernels: 53.1 us -> 58.5 us
    all_to_all x6 -> x5, waiting for transfers between devices: 129 us -> 77.5 us  [exchange_plane(): return lax.all_to_all(blocks, PLANE, 0, 0, tiled=True)]
    all_to_all x2, blocking collectives: 58.3 us -> 107 us  [exchange_plane(): return lax.all_to_all(blocks, PLANE, 0, 0, tiled=True)]
    all_to_all x6 -> x5, starting transfers between devices: 39.7 us -> 31.5 us  [exchange_plane(): return lax.all_to_all(blocks, PLANE, 0, 0, tiled=True)]
    unnamed x34 -> x22, local copies, waits for them, and re-layouts: 8.08 us -> 0.05 us
    all_gather x1, waiting for transfers between devices: 13.4 us -> 5.51 us  [shards(): lax.all_gather(choose(owner, first.reshape(8, 4, 112, 128)), 'z', axis=0,...]
    pallas_call x7, Pallas kernels: 33.1 us -> 39.4 us  [the longest x2 14.7 us: filtered(): pl.pallas_call(filter_kernel, grid=(3,), in_specs=[COLUMNS, waves, whole(...]
    ppermute x7, starting transfers between devices: 14.5 us -> 19.8 us  [gather_orbital(): lax.ppermute(pieces[m], 'z', [(z, z ^ m) for z in range(8)])]
  transfers between devices with their start and end apart: 15 -> 14, of which waited for: 10 -> 9; matrix products, arithmetic and copies ran while one was open for 1% -> 0% of each run, Pallas kernels for 10% -> 8%
where the time goes in v4:
time: 396 us; the launch traced here: 395 us
  blocking collectives  137 us (35%)
  waiting for transfers between devices  133 us (34%)
  Pallas kernels  58.5 us (15%)
  starting transfers between devices  51.3 us (13%)
  between operations  13.6 us (3%)
    all_to_all x2, blocking collectives, exchange_plane(): return lax.all_to_all(blocks, PLANE, 0, 0, tiled=True)  107 us
    all_to_all x5, waiting for transfers between devices, exchange_plane(): return lax.all_to_all(blocks, PLANE, 0, 0, tiled=True)  77.5 us
    all_gather x1, waiting for transfers between devices, shards(): halves.append(lax.all_gather(second, 'z', axis=0, tiled=False))  33 us
    all_to_all x5, starting transfers between devices, exchange_plane(): return lax.all_to_all(blocks, PLANE, 0, 0, tiled=True)  31.5 us
    all_to_all x1, blocking collectives, exchange_z(): return lax.all_to_all(blocks, 'z', 0, 0, tiled=True)  29.8 us
    ppermute x7, starting transfers between devices, gather_orbital(): lax.ppermute(pieces[m], 'z', [(z, z ^ m) for z in range(8)])  19.8 us
    ppermute x7, waiting for transfers between devices, gather_orbital(): lax.ppermute(pieces[m], 'z', [(z, z ^ m) for z in range(8)])  17 us
    pallas_call x2, Pallas kernels, forward(): pl.pallas_call(forward_kernel, grid=(4,), in_specs=[pl.BlockSpec(memory_s...  15.6 us
  transfers between devices with their start and end apart: 14, of which 9 were waited for; matrix products, arithmetic and copies ran while one was open for 0% of the time, Pallas kernels for 8%

profile of v4, /device:TPU:1, one launch (start us, length us, event | category | flops | bytes accessed | tf_op | source)
XLA Modules:
  0.0 395.2 jit_solution(9950322286673865238)
XLA Ops:
  6.5 3.8 pack.5
  10.4 8.7 %all-to-all-start = ((f32[32,112,128]{2,1,0:T(8,128)}), f32[32,112,128]{2,1,0:T(8,128)S(1)}, u32[]{:S(2)}, u32[]{:S(2)}) async-start(f32[32,112,128]{2,1,0:T(8,128)} %pack.5), calls=%async_computation | async-start | bytes 3670016 | tf_op jit(solution)/shard_map/all_to_all | solution.py:363
  19.1 0.0 all-gather.7.cloned.1.call-start
  19.1 2.5 pack.4
  21.6 23.1 %all-to-all-done = f32[32,112,128]{2,1,0:T(8,128)S(1)} async-done(((f32[32,112,128]{2,1,0:T(8,128)}), f32[32,112,128]{2,1,0:T(8,128)S(1)}, u32[]{:S(2)}, u32[]{:S(2)}) %all-to-all-start) | async-done | bytes 1835040 | tf_op jit(solution)/shard_map/all_to_all | solution.py:363
  44.7 1.4 choose.3
  46.1 0.0 all-gather.7.cloned.1.call-update
  46.1 4.7 %all-to-all-start.1 = ((f32[32,56,128]{2,1,0:T(8,128)}), f32[32,56,128]{2,1,0:T(8,128)S(1)}, u32[]{:S(2)}, u32[]{:S(2)}) async-start(f32[32,56,128]{2,1,0:T(8,128)} %pack.4), calls=%async_computation.1 | async-start | bytes 1835008 | tf_op jit(solution)/shard_map/all_to_all | solution.py:363
  50.8 3.8 pack.3
  54.6 11.8 %all-to-all-done.1 = f32[32,56,128]{2,1,0:T(8,128)S(1)} async-done(((f32[32,56,128]{2,1,0:T(8,128)}), f32[32,56,128]{2,1,0:T(8,128)S(1)}, u32[]{:S(2)}, u32[]{:S(2)}) %all-to-all-start.1) | async-done | bytes 917536 | tf_op jit(solution)/shard_map/all_to_all | solution.py:363
  66.5 3.9 all-to-all-start.2
  70.3 0.0 all-gather.5.cloned.1.call-start
  70.4 0.7 slots.1
  71.1 1.7 collective-permute-start
  72.9 3.0 collective-permute-start.1
  75.9 0.0 collective-permute-start.2
  75.9 5.8 %collective-permute-start.3 = (f32[24,1152]{1,0:T(8,128)S(1)}, f32[24,1152]{1,0:T(8,128)S(1)}, u32[]{:S(2)}, u32[]{:S(2)}) collective-permute-start(f32[24,1152]{1,0:T(8,128)S(1)} %get-tuple-element.33), channel_id=1, source_target_pairs={{0,8},{2,10},{4,12},{6,14},{8,0},{10,2},{12,4},{14,6},{1,9},{3,11}... | collective-permute-start | bytes 331784 | tf_op jit(solution)/shard_map/ppermute | solution.py:373
  81.7 0.0 collective-permute-start.4
  81.7 0.0 collective-permute-done.refs_1_
  81.7 4.0 %collective-permute-start.5 = (f32[24,1152]{1,0:T(8,128)S(1)}, f32[24,1152]{1,0:T(8,128)S(1)}, u32[]{:S(2)}, u32[]{:S(2)}) collective-permute-start(f32[24,1152]{1,0:T(8,128)S(1)} %get-tuple-element.35), channel_id=1, source_target_pairs={{0,12},{2,14},{4,8},{6,10},{8,4},{10,6},{12,0},{14,2},{1,13},{3,15... | collective-permute-start | bytes 331784 | tf_op jit(solution)/shard_map/ppermute | solution.py:373
  85.7 0.0 collective-permute-done.1.refs_2_
  85.7 5.2 %collective-permute-start.6 = (f32[24,1152]{1,0:T(8,128)S(1)}, f32[24,1152]{1,0:T(8,128)S(1)}, u32[]{:S(2)}, u32[]{:S(2)}) collective-permute-start(f32[24,1152]{1,0:T(8,128)S(1)} %get-tuple-element.36), channel_id=1, source_target_pairs={{0,14},{2,12},{4,10},{6,8},{8,6},{10,4},{12,2},{14,0},{1,15},{3,13... | collective-permute-start | bytes 331784 | tf_op jit(solution)/shard_map/ppermute | solution.py:373
  91.0 5.0 %collective-permute-done.2.refs_3_ = f32[24,1152]{1,0:T(8,128)S(1)} collective-permute-done((f32[24,1152]{1,0:T(8,128)S(1)}, f32[24,1152]{1,0:T(8,128)S(1)}, u32[]{:S(2)}, u32[]{:S(2)}) %collective-permute-start.2) | collective-permute-done | bytes 110624 | tf_op jit(solution)/shard_map/ppermute | solution.py:373
  96.0 11.2 %collective-permute-done.3.refs_4_ = f32[24,1152]{1,0:T(8,128)S(1)} collective-permute-done((f32[24,1152]{1,0:T(8,128)S(1)}, f32[24,1152]{1,0:T(8,128)S(1)}, u32[]{:S(2)}, u32[]{:S(2)}) %collective-permute-start.3) | collective-permute-done | bytes 110624 | tf_op jit(solution)/shard_map/ppermute | solution.py:373
  107.1 0.0 collective-permute-done.4.refs_5_
  107.2 0.9 collective-permute-done.6.refs_7_
  108.0 0.0 all-to-all-done.2
  108.0 1.4 choose.2
  109.4 0.0 all-gather.5.cloned.1.call-update
  109.4 5.5 %all-gather.7.cloned.1.call-done = f32[32,24,1152]{2,1,0:T(8,128)} async-done(((f32[4,24,1152]{2,1,0:T(8,128)}), f32[32,24,1152]{2,1,0:T(8,128)}) %all-gather.7.cloned.1.call-update) | async-done | bytes 3538960 | tf_op jit(solution)/shard_map/all_gather | solution.py:382
  115.0 7.8 %forward.3 = f32[4,8,9,24,128]{4,3,2,1,0:T(8,128)} custom-call(s32[8]{0:T(128)} %copy-done.1, f32[24,1152]{1,0:T(8,128)} %copy-done.2, f32[24,1152]{1,0:T(8,128)} %copy-done.3, f32[24,1152]{1,0:T(8,128)} %copy-done.4, f32[24,1152]{1,0:T(8,128)} %copy-done.5, f32[24,1152]{1,0:T(8,128)} %copy-done.6, f32[24,1152]{1,0:T(8,128)} %copy-done.7, ...), custom_call_target="tpu_custom_call" | custom-call | flops 16000000000 | bytes 10000000 | tf_op jit(solution)/shard_map/forward/pallas_call | solution.py:286
  122.8 7.8 %all-to-all-start.4 = ((f32[32,216,128]{2,1,0:T(8,128)}), f32[32,216,128]{2,1,0:T(8,128)}, u32[]{:S(2)}, u32[]{:S(2)}) async-start(f32[32,216,128]{2,1,0:T(8,128)} %bitcast.27), calls=%async_computation.4 | async-start | bytes 7077888 | tf_op jit(solution)/shard_map/all_to_all | solution.py:363
  130.6 33.0 %all-gather.5.cloned.1.call-done = f32[32,24,1152]{2,1,0:T(8,128)} async-done(((f32[4,24,1152]{2,1,0:T(8,128)}), f32[32,24,1152]{2,1,0:T(8,128)}) %all-gather.5.cloned.1.call-update) | async-done | bytes 3538960 | tf_op jit(solution)/shard_map/all_gather | solution.py:388
  163.7 7.8 %forward.2 = f32[4,8,9,24,128]{4,3,2,1,0:T(8,128)} custom-call(s32[8]{0:T(128)} %copy-done.1, f32[24,1152]{1,0:T(8,128)} %copy-done.2, f32[24,1152]{1,0:T(8,128)} %copy-done.3, f32[24,1152]{1,0:T(8,128)} %copy-done.4, f32[24,1152]{1,0:T(8,128)} %copy-done.5, f32[24,1152]{1,0:T(8,128)} %copy-done.6, f32[24,1152]{1,0:T(8,128)} %copy-done.7, ...), custom_call_target="tpu_custom_call" | custom-call | flops 16000000000 | bytes 10000000 | tf_op jit(solution)/shard_map/forward/pallas_call | solution.py:286
  171.5 5.3 %all-to-all-done.4 = f32[32,216,128]{2,1,0:T(8,128)} async-done(((f32[32,216,128]{2,1,0:T(8,128)}), f32[32,216,128]{2,1,0:T(8,128)}, u32[]{:S(2)}, u32[]{:S(2)}) %all-to-all-start.4) | async-done | bytes 3538976 | tf_op jit(solution)/shard_map/all_to_all | solution.py:363
  176.8 6.4 %all-to-all-start.3 = ((f32[32,216,128]{2,1,0:T(8,128)}), f32[32,216,128]{2,1,0:T(8,128)}, u32[]{:S(2)}, u32[]{:S(2)}) async-start(f32[32,216,128]{2,1,0:T(8,128)} %bitcast.26), calls=%async_computation.3 | async-start | bytes 7077888 | tf_op jit(solution)/shard_map/all_to_all | solution.py:363
  183.2 0.1 add_add_fusion
  183.3 0.1 reshape.90
  183.4 0.6 reshape.91.pair_ref
  184.0 0.7 fusion.2.wave_ref
  184.7 7.3 %filter.2.refs_0_ = f32[32,2,9,24,128]{4,3,2,1,0:T(8,128)} custom-call(f32[32,9,24,128]{3,2,1,0:T(8,128)} %bitcast.9.columns_ref, f32[3,1,1536]{2,1,0:T(1,128)} %reshape.91.pair_ref, f32[192,1]{1,0:T(8,128)} %fusion.2.wave_ref, bf16[2,192,192]{2,1,0:T(8,128)(2,1)} %constant.68.clone.to_ref, bf16[2,192,192]{2,1,0:T(8,128)(2,1)} %constant.69.clone.from_ref), custom_call_target="tpu_custom_call" | custom-call | flops 16000000000 | bytes 10000000 | tf_op jit(solution)/shard_map/filter/pallas_call | solution.py:335
  192.0 37.3 %all-to-all-done.3 = f32[32,216,128]{2,1,0:T(8,128)} async-done(((f32[32,216,128]{2,1,0:T(8,128)}), f32[32,216,128]{2,1,0:T(8,128)}, u32[]{:S(2)}, u32[]{:S(2)}) %all-to-all-start.3) | async-done | bytes 3538976 | tf_op jit(solution)/shard_map/all_to_all | solution.py:363
  229.3 7.4 %filter.3 = f32[32,2,9,24,128]{4,3,2,1,0:T(8,128)} custom-call(f32[32,9,24,128]{3,2,1,0:T(8,128)} %bitcast.5.columns_ref, f32[3,1,1536]{2,1,0:T(1,128)} %reshape.91.pair_ref, f32[192,1]{1,0:T(8,128)} %fusion.2.wave_ref, bf16[2,192,192]{2,1,0:T(8,128)(2,1)} %constant.68.clone.to_ref, ...), custom_call_target="tpu_custom_call", output_to_operand_aliasing={{}: (5, {})} | custom-call | flops 16000000000 | bytes 10000000 | tf_op jit(solution)/shard_map/filter/pallas_call | solution.py:335
  236.6 88.1 %all_to_all.40 = f32[32,432,128]{2,1,0:T(8,128)} all-to-all(f32[32,432,128]{2,1,0:T(8,128)} %bitcast.23), channel_id=1, replica_groups=mesh['x_lo'=2,'y'=4,'x_hi'=2,'z'=8,'core'=2] {'x_lo','y','x_hi','core'}, dimensions={0} | all-to-all | bytes 14155776 | tf_op jit(solution)/shard_map/all_to_all | solution.py:363
  324.8 13.3 %inverse.1 = f32[8,224,128]{2,1,0:T(8,128)} custom-call(f32[4,8,2,9,24,128]{5,4,3,2,1,0:T(8,128)} %bitcast.24, f32[8,4,24,1152]{3,2,1,0:T(8,128)} %bitcast.30, f32[8,4,24,1152]{3,2,1,0:T(8,128)} %bitcast.32, bf16[2,256,256]{2,1,0:T(8,128)(2,1)} %constant.65.clone.refs_9_.even_ref, bf16[2,256,256]{2,1,0:T(8,128)(2,1)} %constant.70.clone.odd_ref, ...), custom_call_target="tpu_custom_call" | custom-call | flops 16000000000 | bytes 10000000 | tf_op jit(solution)/shard_map/inverse/pallas_call | solution.py:311
  338.1 29.8 %all_to_all.41 = f32[8,224,128]{2,1,0:T(8,128)S(1)} all-to-all(f32[8,224,128]{2,1,0:T(8,128)} %inverse.1), channel_id=1, replica_groups=mesh['x_lo'=2,'y'=4,'x_hi'=2,'z'=8,'core'=2] {'z'}, dimensions={0} | all-to-all | bytes 1835008 | tf_op jit(solution)/shard_map/all_to_all | solution.py:367
  367.8 19.2 %all_to_all.42.blocks_ref = f32[32,56,128]{2,1,0:T(8,128)S(1)} all-to-all(f32[32,56,128]{2,1,0:T(8,128)S(1)} %bitcast.25), channel_id=1, replica_groups=mesh['x_lo'=2,'y'=4,'x_hi'=2,'z'=8,'core'=2] {'x_lo','y','x_hi','core'}, dimensions={0} | all-to-all | bytes 1835008 | tf_op jit(solution)/shard_map/all_to_all | solution.py:363
  387.0 1.3 unpack.1
  (28 shorter events, 0.1 us)
Async XLA Ops:
  10.4 34.3 %copy-start = (s32[2]{0:T(128)S(1)}, s32[2]{0:T(128)}, u32[]{:S(2)}) copy-start(s32[2]{0:T(128)} %owner_ref.3) | copy-start | bytes 28
  10.4 34.3 %all-to-all-start = ((f32[32,112,128]{2,1,0:T(8,128)}), f32[32,112,128]{2,1,0:T(8,128)S(1)}, u32[]{:S(2)}, u32[]{:S(2)}) async-start(f32[32,112,128]{2,1,0:T(8,128)} %pack.5), calls=%async_computation | async-start | bytes 3670016 | tf_op jit(solution)/shard_map/all_to_all | solution.py:363
  19.1 95.8 %all-gather.7.cloned.1.call-start = ((), (), s32[]{:S(2)}) async-start(), calls=%async_computation.9 | async-start | bytes 3981312 | tf_op jit(solution)/shard_map/all_gather | solution.py:382
  46.1 20.3 %all-to-all-start.1 = ((f32[32,56,128]{2,1,0:T(8,128)}), f32[32,56,128]{2,1,0:T(8,128)S(1)}, u32[]{:S(2)}, u32[]{:S(2)}) async-start(f32[32,56,128]{2,1,0:T(8,128)} %pack.4), calls=%async_computation.1 | async-start | bytes 1835008 | tf_op jit(solution)/shard_map/all_to_all | solution.py:363
  66.5 41.6 %all-to-all-start.2 = ((f32[32,112,128]{2,1,0:T(8,128)}), f32[32,112,128]{2,1,0:T(8,128)S(1)}, u32[]{:S(2)}, u32[]{:S(2)}) async-start(f32[32,112,128]{2,1,0:T(8,128)} %pack.3), calls=%async_computation.2 | async-start | bytes 3670016 | tf_op jit(solution)/shard_map/all_to_all | solution.py:363
  70.3 93.3 %all-gather.5.cloned.1.call-start = ((), (), s32[]{:S(2)}) async-start(), calls=%async_computation.8 | async-start | bytes 3981312 | tf_op jit(solution)/shard_map/all_gather | solution.py:388
  70.4 44.5 %copy-start.1 = (s32[8]{0:T(128)}, s32[8]{0:T(128)S(1)}, u32[]{:S(2)}) copy-start(s32[8]{0:T(128)S(1)} %iota_xor_fusion.slots_ref) | copy-start | bytes 100
  71.1 43.8 %copy-start.2 = (f32[24,1152]{1,0:T(8,128)}, f32[24,1152]{1,0:T(8,128)S(1)}, u32[]{:S(2)}) copy-start(f32[24,1152]{1,0:T(8,128)S(1)} %get-tuple-element.37.refs_0_) | copy-start | bytes 331780
  71.1 10.6 %collective-permute-start = (f32[24,1152]{1,0:T(8,128)S(1)}, f32[24,1152]{1,0:T(8,128)S(1)}, u32[]{:S(2)}, u32[]{:S(2)}) collective-permute-start(f32[24,1152]{1,0:T(8,128)S(1)} %get-tuple-element.30), channel_id=1, source_target_pairs={{0,2},{2,0},{4,6},{6,4},{8,10},{10,8},{12,14},{14,12},{1,3},{3,1},... | collective-permute-start | bytes 331784 | tf_op jit(solution)/shard_map/ppermute | solution.py:373
  72.9 12.9 %collective-permute-start.1 = (f32[24,1152]{1,0:T(8,128)S(1)}, f32[24,1152]{1,0:T(8,128)S(1)}, u32[]{:S(2)}, u32[]{:S(2)}) collective-permute-start(f32[24,1152]{1,0:T(8,128)S(1)} %get-tuple-element.31), channel_id=1, source_target_pairs={{0,4},{2,6},{4,0},{6,2},{8,12},{10,14},{12,8},{14,10},{1,5},{3,7},... | collective-permute-start | bytes 331784 | tf_op jit(solution)/shard_map/ppermute | solution.py:373
  75.9 20.1 %collective-permute-start.2 = (f32[24,1152]{1,0:T(8,128)S(1)}, f32[24,1152]{1,0:T(8,128)S(1)}, u32[]{:S(2)}, u32[]{:S(2)}) collective-permute-start(f32[24,1152]{1,0:T(8,128)S(1)} %get-tuple-element.32), channel_id=1, source_target_pairs={{0,6},{2,4},{4,2},{6,0},{8,14},{10,12},{12,10},{14,8},{1,7},{3,5},... | collective-permute-start | bytes 331784 | tf_op jit(solution)/shard_map/ppermute | solution.py:373
  75.9 31.3 %collective-permute-start.3 = (f32[24,1152]{1,0:T(8,128)S(1)}, f32[24,1152]{1,0:T(8,128)S(1)}, u32[]{:S(2)}, u32[]{:S(2)}) collective-permute-start(f32[24,1152]{1,0:T(8,128)S(1)} %get-tuple-element.33), channel_id=1, source_target_pairs={{0,8},{2,10},{4,12},{6,14},{8,0},{10,2},{12,4},{14,6},{1,9},{3,11}... | collective-permute-start | bytes 331784 | tf_op jit(solution)/shard_map/ppermute | solution.py:373
  81.7 25.4 %collective-permute-start.4 = (f32[24,1152]{1,0:T(8,128)S(1)}, f32[24,1152]{1,0:T(8,128)S(1)}, u32[]{:S(2)}, u32[]{:S(2)}) collective-permute-start(f32[24,1152]{1,0:T(8,128)S(1)} %get-tuple-element.34), channel_id=1, source_target_pairs={{0,10},{2,8},{4,14},{6,12},{8,2},{10,0},{12,6},{14,4},{1,11},{3,9}... | collective-permute-start | bytes 331784 | tf_op jit(solution)/shard_map/ppermute | solution.py:373
  81.7 33.2 %copy-start.3 = (f32[24,1152]{1,0:T(8,128)}, f32[24,1152]{1,0:T(8,128)S(1)}, u32[]{:S(2)}) copy-start(f32[24,1152]{1,0:T(8,128)S(1)} %collective-permute-done.refs_1_) | copy-start | bytes 331780
  81.7 25.4 %collective-permute-start.5 = (f32[24,1152]{1,0:T(8,128)S(1)}, f32[24,1152]{1,0:T(8,128)S(1)}, u32[]{:S(2)}, u32[]{:S(2)}) collective-permute-start(f32[24,1152]{1,0:T(8,128)S(1)} %get-tuple-element.35), channel_id=1, source_target_pairs={{0,12},{2,14},{4,8},{6,10},{8,4},{10,6},{12,0},{14,2},{1,13},{3,15... | collective-permute-start | bytes 331784 | tf_op jit(solution)/shard_map/ppermute | solution.py:373
  85.7 29.2 %copy-start.4 = (f32[24,1152]{1,0:T(8,128)}, f32[24,1152]{1,0:T(8,128)S(1)}, u32[]{:S(2)}) copy-start(f32[24,1152]{1,0:T(8,128)S(1)} %collective-permute-done.1.refs_2_) | copy-start | bytes 331780
  85.7 22.3 %collective-permute-start.6 = (f32[24,1152]{1,0:T(8,128)S(1)}, f32[24,1152]{1,0:T(8,128)S(1)}, u32[]{:S(2)}, u32[]{:S(2)}) collective-permute-start(f32[24,1152]{1,0:T(8,128)S(1)} %get-tuple-element.36), channel_id=1, source_target_pairs={{0,14},{2,12},{4,10},{6,8},{8,6},{10,4},{12,2},{14,0},{1,15},{3,13... | collective-permute-start | bytes 331784 | tf_op jit(solution)/shard_map/ppermute | solution.py:373
  96.0 19.0 %copy-start.5 = (f32[24,1152]{1,0:T(8,128)}, f32[24,1152]{1,0:T(8,128)S(1)}, u32[]{:S(2)}) copy-start(f32[24,1152]{1,0:T(8,128)S(1)} %collective-permute-done.2.refs_3_) | copy-start | bytes 331780
  107.1 7.8 %copy-start.6 = (f32[24,1152]{1,0:T(8,128)}, f32[24,1152]{1,0:T(8,128)S(1)}, u32[]{:S(2)}) copy-start(f32[24,1152]{1,0:T(8,128)S(1)} %collective-permute-done.3.refs_4_) | copy-start | bytes 331780
  107.1 7.8 %copy-start.7 = (f32[24,1152]{1,0:T(8,128)}, f32[24,1152]{1,0:T(8,128)S(1)}, u32[]{:S(2)}) copy-start(f32[24,1152]{1,0:T(8,128)S(1)} %collective-permute-done.4.refs_5_) | copy-start | bytes 331780
  107.1 7.8 %copy-start.8 = (f32[24,1152]{1,0:T(8,128)}, f32[24,1152]{1,0:T(8,128)S(1)}, u32[]{:S(2)}) copy-start(f32[24,1152]{1,0:T(8,128)S(1)} %collective-permute-done.5.refs_6_) | copy-start | bytes 331780
  108.0 7.0 %copy-start.9 = (f32[24,1152]{1,0:T(8,128)}, f32[24,1152]{1,0:T(8,128)S(1)}, u32[]{:S(2)}) copy-start(f32[24,1152]{1,0:T(8,128)S(1)} %collective-permute-done.6.refs_7_) | copy-start | bytes 331780
  122.8 54.0 %all-to-all-start.4 = ((f32[32,216,128]{2,1,0:T(8,128)}), f32[32,216,128]{2,1,0:T(8,128)}, u32[]{:S(2)}, u32[]{:S(2)}) async-start(f32[32,216,128]{2,1,0:T(8,128)} %bitcast.27), calls=%async_computation.4 | async-start | bytes 7077888 | tf_op jit(solution)/shard_map/all_to_all | solution.py:363
  176.8 52.5 %all-to-all-start.3 = ((f32[32,216,128]{2,1,0:T(8,128)}), f32[32,216,128]{2,1,0:T(8,128)}, u32[]{:S(2)}, u32[]{:S(2)}) async-start(f32[32,216,128]{2,1,0:T(8,128)} %bitcast.26), calls=%async_computation.3 | async-start | bytes 7077888 | tf_op jit(solution)/shard_map/all_to_all | solution.py:363
Sparse Core Ops, SparseCore 0:
  46.2 68.6 all-gather.6
  116.7 46.9 all-gather.4

commit v5 on v4

--- a/solution.py
+++ b/solution.py
@@ -14,6 +14,7 @@
 LANES = 6 * N
 TILES = LANES // 128
 PLANE = ("x_lo", "y", "x_hi", "core")
+PARTS = 1
 VMEM = 62 * 1024 * 1024
 
 
@@ -37,6 +38,16 @@
     high = matrix.astype(np.float32).astype(ml_dtypes.bfloat16)
     low = (matrix - high.astype(np.float64)).astype(np.float32).astype(ml_dtypes.bfloat16)
     return np.stack([high, low])
+
+
+def stacked_terms(matrix):
+    high, low = two_terms(matrix)
+    return jnp.asarray(np.concatenate([high, low, high], axis=1))
+
+
+def lane_terms(matrix):
+    high, low = two_terms(matrix)
+    return jnp.asarray(np.concatenate([high, high, low], axis=0))
 
 
 def lane_matrices():
@@ -57,18 +68,28 @@
     return jnp.dot(left, right, preferred_element_type=jnp.float32)
 
 
-def product(left, right):
-    return dot(left[0], right[0]) + (dot(left[0], right[1]) + dot(left[1], right[0]))
+def left_product(matrix_ref, value):
+    high, low = split(value)
+    return dot(matrix_ref[...], jnp.concatenate([high, high, low], axis=0))
+
+
+def right_product(high, low, matrix_ref):
+    return dot(jnp.concatenate([high, low, high], axis=1), matrix_ref[...])
 
 
 def lane_transform(value, even_ref, odd_ref):
-    even, odd = (even_ref[0], even_ref[1]), (odd_ref[0], odd_ref[1])
     high, low = split(value)
+
+    def stacked(terms, offset):
+        return jnp.concatenate([terms[:, s + offset : s + offset + 256] for s in range(0, LANES, 384)], axis=0)
+
+    first = right_product(stacked(high, 0), stacked(low, 0), even_ref)
+    last = right_product(stacked(high, 128), stacked(low, 128), odd_ref)
+    middle = first[:, 128:] + last[:, :128]
     tiles = []
-    for start in range(0, LANES, 384):
-        first = product((high[:, start : start + 256], low[:, start : start + 256]), even)
-        last = product((high[:, start + 128 : start + 384], low[:, start + 128 : start + 384]), odd)
-        tiles += [first[:, :128], first[:, 128:] + last[:, :128], last[:, 128:]]
+    for start in range(0, 3 * N, N):
+        for part in (first[:, :128], middle, last[:, 128:]):
+            tiles.append(part[start : start + N])
     return jnp.concatenate(tiles, axis=1)
 
 
@@ -120,32 +141,40 @@
 
     pair = orbital_ref[...].reshape(N, LANES) * band_ref[:, 0].reshape(N, LANES)
     spectrum = lane_transform(pair, even_ref, odd_ref)
-    spectrum = product((rows_ref[0], rows_ref[1]), split(spectrum))
+    spectrum = left_product(rows_ref, spectrum)
     for tile in range(TILES):
         out_ref[0, :, tile] = spectrum[:, 128 * tile : 128 * tile + 128].reshape(8, 24, 128)
 
 
-def inverse_kernel(spectrum_ref, first_ref, last_ref, even_ref, odd_ref, rows_ref, out_ref, total_ref):
+def joined(refs):
+    return jnp.concatenate([ref[:, 0].reshape(N // PARTS, LANES) for ref in refs], axis=0)
+
+
+def inverse_kernel(*refs):
+    spectrum_refs, first_refs, last_refs = refs[:PARTS], refs[PARTS : 2 * PARTS], refs[2 * PARTS : 3 * PARTS]
+    even_ref, odd_ref, rows_ref, out_ref, total_ref = refs[3 * PARTS :]
     step = pl.program_id(0)
-    spectrum = jnp.concatenate(
-        [spectrum_ref[0, :, 0, tile].reshape(N, 128) for tile in range(TILES)], axis=1
-    )
-    potential = product((rows_ref[0], rows_ref[1]), split(spectrum))
+    spectrum = []
+    for ref in spectrum_refs:
+        tiles = [ref[0, :, 0, tile].reshape(N // PARTS, 128) for tile in range(TILES)]
+        spectrum.append(jnp.concatenate(tiles, axis=1))
+    spectrum = jnp.concatenate(spectrum, axis=0)
+    potential = left_product(rows_ref, spectrum)
     potential = lane_transform(potential, even_ref, odd_ref)
     prefactor = -1.0 / math.sqrt(N * 8)
     potential = jnp.where(step % 4 < 2, prefactor, 2.0 * prefactor) * potential
 
     @pl.when(step == 0)
     def _():
-        total_ref[...] = first_ref[:, 0].reshape(N, LANES) * potential
+        total_ref[...] = joined(first_refs) * potential
 
     @pl.when((step > 0) & (step < 4))
     def _():
-        total_ref[...] += first_ref[:, 0].reshape(N, LANES) * potential
+        total_ref[...] += joined(first_refs) * potential
 
     @pl.when(step >= 4)
     def _():
-        total_ref[...] += last_ref[:, 0].reshape(N, LANES) * potential
+        total_ref[...] += joined(last_refs) * potential
 
     @pl.when(step == 7)
     def _():
@@ -195,9 +224,9 @@
             parts.append(jnp.where(lower, pltpu.roll(one, 64, 1), two))
         blocks.append(jnp.concatenate(parts, axis=0))
     columns = jnp.concatenate(blocks, axis=1)
-    spectrum = product((to_ref[0], to_ref[1]), split(columns))
+    spectrum = left_product(to_ref, columns)
     spectrum = spectrum * ((4.0 * math.pi / float(N) ** 3) / (wave_ref[...] + pair_ref[0]))
-    columns = product((from_ref[0], from_ref[1]), split(spectrum))
+    columns = left_product(from_ref, spectrum)
     for k in range(8):
         for i in range(6):
             tile = 3 * (i // 2) + 2 * (i % 2)
@@ -238,6 +267,16 @@
         cost_estimate=MOVED,
         name="pack",
     )(planes)
+
+
+def in_parts(shape, dim, place):
+    block = shape[:dim] + (shape[dim] // PARTS,) + shape[dim + 1 :]
+
+    def part_place(part, step):
+        at = place(step)
+        return at[:dim] + (part,) + at[dim + 1 :]
+
+    return [pl.BlockSpec(block, functools.partial(part_place, part)) for part in range(PARTS)]
 
 
 def from_blocks(blocks):
@@ -281,8 +320,8 @@
 
 def forward(slots, pieces, bands):
     even, odd = lane_matrices()
-    even, odd = jnp.asarray(two_terms(even)), jnp.asarray(two_terms(odd))
-    rows = jnp.asarray(two_terms(cas_matrix()[:, held_order()]))
+    even, odd = lane_terms(even), lane_terms(odd)
+    rows = stacked_terms(cas_matrix()[:, held_order()])
     return pl.pallas_call(
         forward_kernel,
         grid=(4,),
@@ -305,16 +344,16 @@
 
 def inverse(spectra, bands):
     even, odd = lane_matrices()
-    even, odd = jnp.asarray(two_terms(even)), jnp.asarray(two_terms(odd.T))
-    rows = jnp.asarray(two_terms(cas_matrix()[held_order(), :]))
+    even, odd = lane_terms(even), lane_terms(odd.T)
+    rows = stacked_terms(cas_matrix()[held_order(), :])
     out = jax.ShapeDtypeStruct((8, 224, 128), jnp.float32)
     return pl.pallas_call(
         inverse_kernel,
         grid=(8,),
         in_specs=[
-            pl.BlockSpec((1, 8, 1, TILES, 24, 128), lambda step: (step % 4, 0, step // 4, 0, 0, 0)),
-            pl.BlockSpec((8, 1, 24, LANES), lambda step: (0, jnp.minimum(step, 3), 0, 0)),
-            pl.BlockSpec((8, 1, 24, LANES), lambda step: (0, jnp.maximum(step - 4, 0), 0, 0)),
+            *in_parts((1, 8, 1, TILES, 24, 128), 1, lambda step: (step % 4, 0, step // 4, 0, 0, 0)),
+            *in_parts((8, 1, 24, LANES), 0, lambda step: (0, jnp.minimum(step, 3), 0, 0)),
+            *in_parts((8, 1, 24, LANES), 0, lambda step: (0, jnp.maximum(step - 4, 0), 0, 0)),
             whole(even),
             whole(odd),
             whole(rows),
@@ -322,15 +361,15 @@
         out_specs=whole(out),
         out_shape=out,
         scratch_shapes=[pltpu.VMEM((N, LANES), jnp.float32)],
-        compiler_params=PARAMS,
+        compiler_params=pltpu.CompilerParams(vmem_limit_bytes=32 * 1024 * 1024),
         cost_estimate=COST,
         name="inverse",
-    )(spectra, *bands, even, odd, rows)
+    )(*[spectra] * PARTS, *[bands[0]] * PARTS, *[bands[1]] * PARTS, even, odd, rows)
 
 
 def filtered(columns, pair_wave, wave, half, *earlier):
-    to = jnp.asarray(two_terms(cas_matrix()[:, column_order()]))
-    back = jnp.asarray(two_terms(cas_matrix()[column_order(), :]))
+    to = stacked_terms(cas_matrix()[:, column_order()])
+    back = stacked_terms(cas_matrix()[column_order(), :])
     waves = pl.BlockSpec((1, 1, 8 * N), lambda step: (step, 0, 0))
     return pl.pallas_call(
         filter_kernel,
@@ -367,22 +406,27 @@
     return lax.all_to_all(blocks, "z", 0, 0, tiled=True)
 
 
-def gather_orbital(spread, slots):
-    pieces = by_slots(slots, spread)
-    return [pieces[0]] + [
-        lax.ppermute(pieces[m], "z", [(z, z ^ m) for z in range(8)]) for m in range(1, 8)
+SHIFTS = (0, 4, 3, 5, 2, 6, 1, 7)
+
+
+def gather_orbital(spread, place):
+    shifts = jnp.array(SHIFTS, jnp.int32)
+    pieces = by_slots((place + shifts) % 8, spread)
+    moved = [
+        lax.ppermute(piece, "z", [(z, (z + shift) % 8) for z in range(8)])
+        for piece, shift in zip(pieces[1:], SHIFTS[1:])
     ]
+    return [pieces[0]] + moved, (place - shifts) % 8
 
 
 def shards(resident, owned, owner):
     pair_wave, wave = filter_waves(lax.axis_index(PLANE))
-    slots = lax.axis_index("z") ^ jnp.arange(8, dtype=jnp.int32)
     first = exchange_plane(to_blocks(owned[0], 2, 0))
     spread, first = lax.optimization_barrier((to_blocks(resident, 1, 0), first))
     halves = [lax.all_gather(choose(owner, first.reshape(8, 4, 112, 128)), "z", axis=0, tiled=False)]
     spread = exchange_plane(spread)
     second, spread = lax.optimization_barrier((to_blocks(owned[0], 2, 1), spread))
-    orbital = gather_orbital(spread.reshape(8, 4, 56, 128), slots)
+    orbital, slots = gather_orbital(spread.reshape(8, 4, 56, 128), lax.axis_index("z"))
     second, orbital = lax.optimization_barrier((exchange_plane(second), orbital))
     second = choose(owner, second.reshape(8, 4, 112, 128))
     halves.append(lax.all_gather(second, "z", axis=0, tiled=False))

time: 396 us -> 392 us (0.990)
  starting transfers between devices: 51.3 us -> 47.1 us
    ppermute x7, waiting for transfers between devices: 17 us -> 21.2 us  [gather_orbital(): lax.ppermute(piece, 'z', [(z, (z + shift) % 8) for z in range(8)])]
    ppermute x7, starting transfers between devices: 19.8 us -> 15.8 us  [gather_orbital(): lax.ppermute(piece, 'z', [(z, (z + shift) % 8) for z in range(8)])]
  transfers between devices with their start and end apart: 14 -> 14, of which waited for: 9 -> 12; matrix products, arithmetic and copies ran while one was open for 0% -> 1% of each run, Pallas kernels for 8% -> 8%
where the time goes in v5:
time: 392 us; the launch traced here: 391 us
  blocking collectives  138 us (35%)
  waiting for transfers between devices  136 us (35%)
  Pallas kernels  54.6 us (14%)
  starting transfers between devices  47.1 us (12%)
  between operations  13.6 us (3%)
    all_to_all x2, blocking collectives, exchange_plane(): return lax.all_to_all(blocks, PLANE, 0, 0, tiled=True)  108 us
    all_to_all x5, waiting for transfers between devices, exchange_plane(): return lax.all_to_all(blocks, PLANE, 0, 0, tiled=True)  77.2 us
    all_gather x1, waiting for transfers between devices, shards(): halves.append(lax.all_gather(second, 'z', axis=0, tiled=False))  33.8 us
    all_to_all x5, starting transfers between devices, exchange_plane(): return lax.all_to_all(blocks, PLANE, 0, 0, tiled=True)  31.2 us
    all_to_all x1, blocking collectives, exchange_z(): return lax.all_to_all(blocks, 'z', 0, 0, tiled=True)  29.4 us
    ppermute x7, waiting for transfers between devices, gather_orbital(): lax.ppermute(piece, 'z', [(z, (z + shift) % 8) for z in range(8)])  21.2 us
    ppermute x7, starting transfers between devices, gather_orbital(): lax.ppermute(piece, 'z', [(z, (z + shift) % 8) for z in range(8)])  15.8 us
    pallas_call x2, Pallas kernels, forward(): pl.pallas_call(forward_kernel, grid=(4,), in_specs=[pl.BlockSpec(memory_s...  15.2 us
  transfers between devices with their start and end apart: 14, of which 12 were waited for; matrix products, arithmetic and copies ran while one was open for 1% of the time, Pallas kernels for 8%

profile of v5, /device:TPU:1, one launch (start us, length us, event | category | flops | bytes accessed | tf_op | source)
XLA Modules:
  0.0 391.0 jit_solution(13125288440082981062)
XLA Ops:
  6.5 3.8 pack.5
  10.3 8.7 %all-to-all-start = ((f32[32,112,128]{2,1,0:T(8,128)}), f32[32,112,128]{2,1,0:T(8,128)S(1)}, u32[]{:S(2)}, u32[]{:S(2)}) async-start(f32[32,112,128]{2,1,0:T(8,128)} %pack.5), calls=%async_computation | async-start | bytes 3670016 | tf_op jit(solution)/shard_map/all_to_all | solution.py:402
  19.1 0.0 all-gather.7.cloned.1.call-start
  19.1 2.5 pack.4
  21.6 23.1 %all-to-all-done = f32[32,112,128]{2,1,0:T(8,128)S(1)} async-done(((f32[32,112,128]{2,1,0:T(8,128)}), f32[32,112,128]{2,1,0:T(8,128)S(1)}, u32[]{:S(2)}, u32[]{:S(2)}) %all-to-all-start) | async-done | bytes 1835040 | tf_op jit(solution)/shard_map/all_to_all | solution.py:402
  44.7 1.4 choose.3
  46.1 0.0 all-gather.7.cloned.1.call-update
  46.1 4.7 %all-to-all-start.1 = ((f32[32,56,128]{2,1,0:T(8,128)}), f32[32,56,128]{2,1,0:T(8,128)S(1)}, u32[]{:S(2)}, u32[]{:S(2)}) async-start(f32[32,56,128]{2,1,0:T(8,128)} %pack.4), calls=%async_computation.1 | async-start | bytes 1835008 | tf_op jit(solution)/shard_map/all_to_all | solution.py:402
  50.8 0.0 copy-start.15
  50.8 3.8 pack.3
  54.6 11.8 %all-to-all-done.1 = f32[32,56,128]{2,1,0:T(8,128)S(1)} async-done(((f32[32,56,128]{2,1,0:T(8,128)}), f32[32,56,128]{2,1,0:T(8,128)S(1)}, u32[]{:S(2)}, u32[]{:S(2)}) %all-to-all-start.1) | async-done | bytes 917536 | tf_op jit(solution)/shard_map/all_to_all | solution.py:402
  66.4 3.8 all-to-all-start.2
  70.3 0.0 all-gather.5.cloned.1.call-start
  70.4 0.7 slots.1
  71.1 7.0 %collective-permute-start = (f32[24,1152]{1,0:T(8,128)S(1)}, f32[24,1152]{1,0:T(8,128)S(1)}, u32[]{:S(2)}, u32[]{:S(2)}) collective-permute-start(f32[24,1152]{1,0:T(8,128)S(1)} %get-tuple-element.30), channel_id=1, source_target_pairs={{0,8},{2,10},{4,12},{6,14},{8,0},{10,2},{12,4},{14,6},{1,9},{3,11}... | collective-permute-start | bytes 331784 | tf_op jit(solution)/shard_map/ppermute | solution.py:416
  78.1 1.6 collective-permute-start.1
  79.8 2.8 collective-permute-start.2
  82.6 1.2 collective-permute-start.3
  83.8 2.4 collective-permute-start.4
  86.2 0.7 collective-permute-start.5
  86.9 9.3 %collective-permute-done.1.refs_2_ = f32[24,1152]{1,0:T(8,128)S(1)} collective-permute-done((f32[24,1152]{1,0:T(8,128)S(1)}, f32[24,1152]{1,0:T(8,128)S(1)}, u32[]{:S(2)}, u32[]{:S(2)}) %collective-permute-start.1) | collective-permute-done | bytes 110624 | tf_op jit(solution)/shard_map/ppermute | solution.py:416
  96.2 1.2 collective-permute-done.2.refs_3_
  97.4 4.5 %collective-permute-done.3.refs_4_ = f32[24,1152]{1,0:T(8,128)S(1)} collective-permute-done((f32[24,1152]{1,0:T(8,128)S(1)}, f32[24,1152]{1,0:T(8,128)S(1)}, u32[]{:S(2)}, u32[]{:S(2)}) %collective-permute-start.3) | collective-permute-done | bytes 110624 | tf_op jit(solution)/shard_map/ppermute | solution.py:416
  101.9 0.3 collective-permute-done.4.refs_5_
  102.2 4.2 %collective-permute-done.5.refs_6_ = f32[24,1152]{1,0:T(8,128)S(1)} collective-permute-done((f32[24,1152]{1,0:T(8,128)S(1)}, f32[24,1152]{1,0:T(8,128)S(1)}, u32[]{:S(2)}, u32[]{:S(2)}) %collective-permute-start.5) | collective-permute-done | bytes 110624 | tf_op jit(solution)/shard_map/ppermute | solution.py:416
  106.4 1.7 collective-permute-done.6.refs_7_
  108.1 1.4 choose.2
  109.5 0.0 all-gather.5.cloned.1.call-update
  109.5 0.5 and_select_fusion.1.slots_ref
  110.1 3.7 all-gather.7.cloned.1.call-done
  113.8 7.6 %forward.3 = f32[4,8,9,24,128]{4,3,2,1,0:T(8,128)} custom-call(s32[8]{0:T(128)} %and_select_fusion.1.slots_ref, f32[24,1152]{1,0:T(8,128)} %copy-done.3, f32[24,1152]{1,0:T(8,128)} %copy-done.7, f32[24,1152]{1,0:T(8,128)} %copy-done.8, f32[24,1152]{1,0:T(8,128)} %copy-done.9, f32[24,1152]{1,0:T(8,128)} %copy-done.10, f32[24,1152]{1,0:T(8,128)} %copy-done.11, ...), custom_call_target="tpu_custom_call" | custom-call | flops 16000000000 | bytes 10000000 | tf_op jit(solution)/shard_map/forward/pallas_call | solution.py:325
  121.4 7.6 %all-to-all-start.4 = ((f32[32,216,128]{2,1,0:T(8,128)}), f32[32,216,128]{2,1,0:T(8,128)}, u32[]{:S(2)}, u32[]{:S(2)}) async-start(f32[32,216,128]{2,1,0:T(8,128)} %bitcast.31), calls=%async_computation.4 | async-start | bytes 7077888 | tf_op jit(solution)/shard_map/all_to_all | solution.py:402
  129.0 33.8 %all-gather.5.cloned.1.call-done = f32[32,24,1152]{2,1,0:T(8,128)} async-done(((f32[4,24,1152]{2,1,0:T(8,128)}), f32[32,24,1152]{2,1,0:T(8,128)}) %all-gather.5.cloned.1.call-update) | async-done | bytes 3538960 | tf_op jit(solution)/shard_map/all_gather | solution.py:432
  162.8 7.6 %forward.2 = f32[4,8,9,24,128]{4,3,2,1,0:T(8,128)} custom-call(s32[8]{0:T(128)} %and_select_fusion.1.slots_ref, f32[24,1152]{1,0:T(8,128)} %copy-done.3, f32[24,1152]{1,0:T(8,128)} %copy-done.7, f32[24,1152]{1,0:T(8,128)} %copy-done.8, f32[24,1152]{1,0:T(8,128)} %copy-done.9, f32[24,1152]{1,0:T(8,128)} %copy-done.10, f32[24,1152]{1,0:T(8,128)} %copy-done.11, ...), custom_call_target="tpu_custom_call" | custom-call | flops 16000000000 | bytes 10000000 | tf_op jit(solution)/shard_map/forward/pallas_call | solution.py:325
  170.4 4.7 %all-to-all-done.4 = f32[32,216,128]{2,1,0:T(8,128)} async-done(((f32[32,216,128]{2,1,0:T(8,128)}), f32[32,216,128]{2,1,0:T(8,128)}, u32[]{:S(2)}, u32[]{:S(2)}) %all-to-all-start.4) | async-done | bytes 3538976 | tf_op jit(solution)/shard_map/all_to_all | solution.py:402
  175.1 6.4 %all-to-all-start.3 = ((f32[32,216,128]{2,1,0:T(8,128)}), f32[32,216,128]{2,1,0:T(8,128)}, u32[]{:S(2)}, u32[]{:S(2)}) async-start(f32[32,216,128]{2,1,0:T(8,128)} %bitcast.30), calls=%async_computation.3 | async-start | bytes 7077888 | tf_op jit(solution)/shard_map/all_to_all | solution.py:402
  181.6 0.1 add_add_fusion
  181.7 0.1 reshape.90
  181.8 0.6 reshape.91.pair_ref
  182.4 0.7 fusion.2.wave_ref
  183.0 7.0 %filter.2.refs_0_ = f32[32,2,9,24,128]{4,3,2,1,0:T(8,128)} custom-call(f32[32,9,24,128]{3,2,1,0:T(8,128)} %bitcast.9.columns_ref, f32[3,1,1536]{2,1,0:T(1,128)} %reshape.91.pair_ref, f32[192,1]{1,0:T(8,128)} %fusion.2.wave_ref, bf16[192,576]{1,0:T(8,128)(2,1)} %constant.84.clone.to_ref, bf16[192,576]{1,0:T(8,128)(2,1)} %constant.85.clone.from_ref), custom_call_target="tpu_custom_call" | custom-call | flops 16000000000 | bytes 10000000 | tf_op jit(solution)/shard_map/filter/pallas_call | solution.py:374
  190.0 37.6 %all-to-all-done.3 = f32[32,216,128]{2,1,0:T(8,128)} async-done(((f32[32,216,128]{2,1,0:T(8,128)}), f32[32,216,128]{2,1,0:T(8,128)}, u32[]{:S(2)}, u32[]{:S(2)}) %all-to-all-start.3) | async-done | bytes 3538976 | tf_op jit(solution)/shard_map/all_to_all | solution.py:402
  227.7 7.0 %filter.3 = f32[32,2,9,24,128]{4,3,2,1,0:T(8,128)} custom-call(f32[32,9,24,128]{3,2,1,0:T(8,128)} %bitcast.5.columns_ref, f32[3,1,1536]{2,1,0:T(1,128)} %reshape.91.pair_ref, f32[192,1]{1,0:T(8,128)} %fusion.2.wave_ref, bf16[192,576]{1,0:T(8,128)(2,1)} %constant.84.clone.to_ref, ...), custom_call_target="tpu_custom_call", output_to_operand_aliasing={{}: (5, {})} | custom-call | flops 16000000000 | bytes 10000000 | tf_op jit(solution)/shard_map/filter/pallas_call | solution.py:374
  234.7 88.3 %all_to_all.40 = f32[32,432,128]{2,1,0:T(8,128)S(1)} all-to-all(f32[32,432,128]{2,1,0:T(8,128)} %bitcast.28), channel_id=1, replica_groups=mesh['x_lo'=2,'y'=4,'x_hi'=2,'z'=8,'core'=2] {'x_lo','y','x_hi','core'}, dimensions={0} | all-to-all | bytes 14155776 | tf_op jit(solution)/shard_map/all_to_all | solution.py:402
  323.0 10.5 %inverse.1 = f32[8,224,128]{2,1,0:T(8,128)S(1)} custom-call(f32[4,8,2,9,24,128]{5,4,3,2,1,0:T(8,128)S(1)} %bitcast.20, f32[8,4,24,1152]{3,2,1,0:T(8,128)S(1)} %bitcast.23, f32[8,4,24,1152]{3,2,1,0:T(8,128)S(1)} %bitcast.25, bf16[768,256]{1,0:T(8,128)(2,1)S(1)} %copy-done.4, bf16[768,256]{1,0:T(8,128)(2,1)S(1)} %copy-done.5, bf16[192,576]{1,0:T(8,128)(2,1)S(1)} %copy-done.6), custom_call_target="tpu_custom_call" | custom-call | flops 16000000000 | bytes 10000000 | tf_op jit(solution)/shard_map/inverse/pallas_call | solution.py:350
  333.5 29.4 %all_to_all.41 = f32[8,224,128]{2,1,0:T(8,128)S(1)} all-to-all(f32[8,224,128]{2,1,0:T(8,128)S(1)} %inverse.1), channel_id=1, replica_groups=mesh['x_lo'=2,'y'=4,'x_hi'=2,'z'=8,'core'=2] {'z'}, dimensions={0} | all-to-all | bytes 1835008 | tf_op jit(solution)/shard_map/all_to_all | solution.py:406
  362.9 19.9 %all_to_all.42.blocks_ref = f32[32,56,128]{2,1,0:T(8,128)S(1)} all-to-all(f32[32,56,128]{2,1,0:T(8,128)S(1)} %bitcast.29), channel_id=1, replica_groups=mesh['x_lo'=2,'y'=4,'x_hi'=2,'z'=8,'core'=2] {'x_lo','y','x_hi','core'}, dimensions={0} | all-to-all | bytes 1835008 | tf_op jit(solution)/shard_map/all_to_all | solution.py:402
  382.9 1.3 unpack.1
  (41 shorter events, 0.1 us)
Async XLA Ops:
  10.3 34.3 %copy-start = (s32[2]{0:T(128)S(1)}, s32[2]{0:T(128)}, u32[]{:S(2)}) copy-start(s32[2]{0:T(128)} %owner_ref.3) | copy-start | bytes 28
  10.3 34.3 %all-to-all-start = ((f32[32,112,128]{2,1,0:T(8,128)}), f32[32,112,128]{2,1,0:T(8,128)S(1)}, u32[]{:S(2)}, u32[]{:S(2)}) async-start(f32[32,112,128]{2,1,0:T(8,128)} %pack.5), calls=%async_computation | async-start | bytes 3670016 | tf_op jit(solution)/shard_map/all_to_all | solution.py:402
  19.1 94.7 %all-gather.7.cloned.1.call-start = ((), (), s32[]{:S(2)}) async-start(), calls=%async_computation.9 | async-start | bytes 3981312 | tf_op jit(solution)/shard_map/all_gather | solution.py:426
  46.1 20.3 %all-to-all-start.1 = ((f32[32,56,128]{2,1,0:T(8,128)}), f32[32,56,128]{2,1,0:T(8,128)S(1)}, u32[]{:S(2)}, u32[]{:S(2)}) async-start(f32[32,56,128]{2,1,0:T(8,128)} %pack.4), calls=%async_computation.1 | async-start | bytes 1835008 | tf_op jit(solution)/shard_map/all_to_all | solution.py:402
  50.8 19.6 %copy-start.15 = (s32[8]{0:T(128)S(1)}, s32[8]{0:T(128)}, u32[]{:S(2)}) copy-start(s32[8]{0:T(128)} %constant.80.clone) | copy-start | bytes 100
  54.6 55.0 %copy-start.14 = (s32[8]{0:T(128)S(1)}, s32[8]{0:T(128)}, u32[]{:S(2)}) copy-start(s32[8]{0:T(128)} %constant.90) | copy-start | bytes 100
  66.4 41.7 %all-to-all-start.2 = ((f32[32,112,128]{2,1,0:T(8,128)}), f32[32,112,128]{2,1,0:T(8,128)S(1)}, u32[]{:S(2)}, u32[]{:S(2)}) async-start(f32[32,112,128]{2,1,0:T(8,128)} %pack.3), calls=%async_computation.2 | async-start | bytes 3670016 | tf_op jit(solution)/shard_map/all_to_all | solution.py:402
  70.3 92.6 %all-gather.5.cloned.1.call-start = ((), (), s32[]{:S(2)}) async-start(), calls=%async_computation.8 | async-start | bytes 3981312 | tf_op jit(solution)/shard_map/all_gather | solution.py:432
  71.1 42.6 %copy-start.3 = (f32[24,1152]{1,0:T(8,128)}, f32[24,1152]{1,0:T(8,128)S(1)}, u32[]{:S(2)}) copy-start(f32[24,1152]{1,0:T(8,128)S(1)} %get-tuple-element.37.refs_0_) | copy-start | bytes 331780
  71.1 15.1 %collective-permute-start = (f32[24,1152]{1,0:T(8,128)S(1)}, f32[24,1152]{1,0:T(8,128)S(1)}, u32[]{:S(2)}, u32[]{:S(2)}) collective-permute-start(f32[24,1152]{1,0:T(8,128)S(1)} %get-tuple-element.30), channel_id=1, source_target_pairs={{0,8},{2,10},{4,12},{6,14},{8,0},{10,2},{12,4},{14,6},{1,9},{3,11}... | collective-permute-start | bytes 331784 | tf_op jit(solution)/shard_map/ppermute | solution.py:416
  78.1 18.1 %collective-permute-start.1 = (f32[24,1152]{1,0:T(8,128)S(1)}, f32[24,1152]{1,0:T(8,128)S(1)}, u32[]{:S(2)}, u32[]{:S(2)}) collective-permute-start(f32[24,1152]{1,0:T(8,128)S(1)} %get-tuple-element.31), channel_id=1, source_target_pairs={{0,6},{2,8},{4,10},{6,12},{8,14},{10,0},{12,2},{14,4},{1,7},{3,9},... | collective-permute-start | bytes 331784 | tf_op jit(solution)/shard_map/ppermute | solution.py:416
  79.8 17.7 %collective-permute-start.2 = (f32[24,1152]{1,0:T(8,128)S(1)}, f32[24,1152]{1,0:T(8,128)S(1)}, u32[]{:S(2)}, u32[]{:S(2)}) collective-permute-start(f32[24,1152]{1,0:T(8,128)S(1)} %get-tuple-element.32), channel_id=1, source_target_pairs={{0,10},{2,12},{4,14},{6,0},{8,2},{10,4},{12,6},{14,8},{1,11},{3,13... | collective-permute-start | bytes 331784 | tf_op jit(solution)/shard_map/ppermute | solution.py:416
  82.6 19.3 %collective-permute-start.3 = (f32[24,1152]{1,0:T(8,128)S(1)}, f32[24,1152]{1,0:T(8,128)S(1)}, u32[]{:S(2)}, u32[]{:S(2)}) collective-permute-start(f32[24,1152]{1,0:T(8,128)S(1)} %get-tuple-element.33), channel_id=1, source_target_pairs={{0,4},{2,6},{4,8},{6,10},{8,12},{10,14},{12,0},{14,2},{1,5},{3,7},... | collective-permute-start | bytes 331784 | tf_op jit(solution)/shard_map/ppermute | solution.py:416
  83.8 18.4 %collective-permute-start.4 = (f32[24,1152]{1,0:T(8,128)S(1)}, f32[24,1152]{1,0:T(8,128)S(1)}, u32[]{:S(2)}, u32[]{:S(2)}) collective-permute-start(f32[24,1152]{1,0:T(8,128)S(1)} %get-tuple-element.34), channel_id=1, source_target_pairs={{0,12},{2,14},{4,0},{6,2},{8,4},{10,6},{12,8},{14,10},{1,13},{3,15... | collective-permute-start | bytes 331784 | tf_op jit(solution)/shard_map/ppermute | solution.py:416
  86.2 27.6 %copy-start.7 = (f32[24,1152]{1,0:T(8,128)}, f32[24,1152]{1,0:T(8,128)S(1)}, u32[]{:S(2)}) copy-start(f32[24,1152]{1,0:T(8,128)S(1)} %collective-permute-done.refs_1_) | copy-start | bytes 331780
  86.2 20.2 %collective-permute-start.5 = (f32[24,1152]{1,0:T(8,128)S(1)}, f32[24,1152]{1,0:T(8,128)S(1)}, u32[]{:S(2)}, u32[]{:S(2)}) collective-permute-start(f32[24,1152]{1,0:T(8,128)S(1)} %get-tuple-element.35), channel_id=1, source_target_pairs={{0,2},{2,4},{4,6},{6,8},{8,10},{10,12},{12,14},{14,0},{1,3},{3,5},... | collective-permute-start | bytes 331784 | tf_op jit(solution)/shard_map/ppermute | solution.py:416
  96.2 17.6 %copy-start.8 = (f32[24,1152]{1,0:T(8,128)}, f32[24,1152]{1,0:T(8,128)S(1)}, u32[]{:S(2)}) copy-start(f32[24,1152]{1,0:T(8,128)S(1)} %collective-permute-done.1.refs_2_) | copy-start | bytes 331780
  96.2 11.9 %collective-permute-start.6 = (f32[24,1152]{1,0:T(8,128)S(1)}, f32[24,1152]{1,0:T(8,128)S(1)}, u32[]{:S(2)}, u32[]{:S(2)}) collective-permute-start(f32[24,1152]{1,0:T(8,128)S(1)} %get-tuple-element.36), channel_id=1, source_target_pairs={{0,14},{2,0},{4,2},{6,4},{8,6},{10,8},{12,10},{14,12},{1,15},{3,1}... | collective-permute-start | bytes 331784 | tf_op jit(solution)/shard_map/ppermute | solution.py:416
  97.4 16.3 %copy-start.9 = (f32[24,1152]{1,0:T(8,128)}, f32[24,1152]{1,0:T(8,128)S(1)}, u32[]{:S(2)}) copy-start(f32[24,1152]{1,0:T(8,128)S(1)} %collective-permute-done.2.refs_3_) | copy-start | bytes 331780
  101.9 11.8 %copy-start.10 = (f32[24,1152]{1,0:T(8,128)}, f32[24,1152]{1,0:T(8,128)S(1)}, u32[]{:S(2)}) copy-start(f32[24,1152]{1,0:T(8,128)S(1)} %collective-permute-done.3.refs_4_) | copy-start | bytes 331780
  102.2 11.5 %copy-start.11 = (f32[24,1152]{1,0:T(8,128)}, f32[24,1152]{1,0:T(8,128)S(1)}, u32[]{:S(2)}) copy-start(f32[24,1152]{1,0:T(8,128)S(1)} %collective-permute-done.4.refs_5_) | copy-start | bytes 331780
  106.4 7.4 %copy-start.12 = (f32[24,1152]{1,0:T(8,128)}, f32[24,1152]{1,0:T(8,128)S(1)}, u32[]{:S(2)}) copy-start(f32[24,1152]{1,0:T(8,128)S(1)} %collective-permute-done.5.refs_6_) | copy-start | bytes 331780
  108.1 5.7 %copy-start.13 = (f32[24,1152]{1,0:T(8,128)}, f32[24,1152]{1,0:T(8,128)S(1)}, u32[]{:S(2)}) copy-start(f32[24,1152]{1,0:T(8,128)S(1)} %collective-permute-done.6.refs_7_) | copy-start | bytes 331780
  121.4 53.7 %all-to-all-start.4 = ((f32[32,216,128]{2,1,0:T(8,128)}), f32[32,216,128]{2,1,0:T(8,128)}, u32[]{:S(2)}, u32[]{:S(2)}) async-start(f32[32,216,128]{2,1,0:T(8,128)} %bitcast.31), calls=%async_computation.4 | async-start | bytes 7077888 | tf_op jit(solution)/shard_map/all_to_all | solution.py:402
  175.1 52.5 %all-to-all-start.3 = ((f32[32,216,128]{2,1,0:T(8,128)}), f32[32,216,128]{2,1,0:T(8,128)}, u32[]{:S(2)}, u32[]{:S(2)}) async-start(f32[32,216,128]{2,1,0:T(8,128)} %bitcast.30), calls=%async_computation.3 | async-start | bytes 7077888 | tf_op jit(solution)/shard_map/all_to_all | solution.py:402
  234.6 88.3 %copy-start.1 = (f32[32,24,1152]{2,1,0:T(8,128)S(1)}, f32[32,24,1152]{2,1,0:T(8,128)}, u32[]{:S(2)}) copy-start(f32[32,24,1152]{2,1,0:T(8,128)} %all-gather.7.cloned.1.call-done) | copy-start | bytes 10616836
  234.6 88.3 %copy-start.2 = (f32[32,24,1152]{2,1,0:T(8,128)S(1)}, f32[32,24,1152]{2,1,0:T(8,128)}, u32[]{:S(2)}) copy-start(f32[32,24,1152]{2,1,0:T(8,128)} %all-gather.5.cloned.1.call-done) | copy-start | bytes 10616836
  234.6 88.3 %copy-start.4 = (bf16[768,256]{1,0:T(8,128)(2,1)S(1)}, bf16[768,256]{1,0:T(8,128)(2,1)}, u32[]{:S(2)}) copy-start(bf16[768,256]{1,0:T(8,128)(2,1)} %constant.81.clone.refs_9_.refs_3_) | copy-start | bytes 1179652
  234.7 88.3 %copy-start.5 = (bf16[768,256]{1,0:T(8,128)(2,1)S(1)}, bf16[768,256]{1,0:T(8,128)(2,1)}, u32[]{:S(2)}) copy-start(bf16[768,256]{1,0:T(8,128)(2,1)} %constant.86.clone.refs_4_) | copy-start | bytes 1179652
  234.7 88.3 %copy-start.6 = (bf16[192,576]{1,0:T(8,128)(2,1)S(1)}, bf16[192,576]{1,0:T(8,128)(2,1)}, u32[]{:S(2)}) copy-start(bf16[192,576]{1,0:T(8,128)(2,1)} %constant.87.clone.refs_5_) | copy-start | bytes 663556
Sparse Core Ops, SparseCore 0:
  46.2 67.4 all-gather.6
  115.5 47.2 all-gather.4

commit v6 on v5

--- a/solution.py
+++ b/solution.py
@@ -203,8 +203,7 @@
         out_ref[0, a, :, 128:] = right[:, :64]
 
 
-def filter_kernel(columns_ref, pair_ref, wave_ref, to_ref, from_ref, *refs):
-    out_ref = refs[-1]
+def filter_block(columns_ref, pair_ref, wave_ref, to_ref, from_ref, out_ref):
     source = columns_ref.reshape(32 * TILES * 8, 128)
     target = out_ref.reshape(32 * TILES * 8, 128)
     lower = lax.broadcasted_iota(jnp.int32, (32, 128), 1) < 64
@@ -240,6 +239,18 @@
             target[rows(3 * h + 1, k + 1), :] = jnp.where(lower, pltpu.roll(one, 64, 1), two)
 
 
+def filter_kernel(first_ref, last_ref, *refs):
+    step = pl.program_id(0)
+
+    @pl.when(step < 3)
+    def _():
+        filter_block(first_ref, *refs)
+
+    @pl.when(step >= 3)
+    def _():
+        filter_block(last_ref, *refs)
+
+
 def whole(array):
     return pl.BlockSpec(array.shape, lambda step: (0,) * len(array.shape))
 
@@ -248,7 +259,6 @@
 COST = pl.CostEstimate(flops=16 * 10**9, bytes_accessed=10**7, transcendentals=0)
 BANDS = pl.BlockSpec((8, 1, 24, LANES), lambda step: (0, step, 0, 0))
 SPECTRA = pl.BlockSpec((1, 8, TILES, 24, 128), lambda step: (step, 0, 0, 0, 0))
-COLUMNS = pl.BlockSpec((32, TILES, 8, 128), lambda step: (0, 0, step, 0))
 
 
 MOVES = pltpu.CompilerParams(vmem_limit_bytes=16 * 1024 * 1024)
@@ -367,21 +377,27 @@
     )(*[spectra] * PARTS, *[bands[0]] * PARTS, *[bands[1]] * PARTS, even, odd, rows)
 
 
-def filtered(columns, pair_wave, wave, half, *earlier):
+def filtered(first, last, pair_wave, wave):
     to = stacked_terms(cas_matrix()[:, column_order()])
     back = stacked_terms(cas_matrix()[column_order(), :])
-    waves = pl.BlockSpec((1, 1, 8 * N), lambda step: (step, 0, 0))
+    block = (32, TILES, 8, 128)
     return pl.pallas_call(
         filter_kernel,
-        grid=(3,),
-        in_specs=[COLUMNS, waves, whole(wave), whole(to), whole(back), *[pl.BlockSpec(memory_space=pl.ANY) for _ in earlier]],
-        out_specs=pl.BlockSpec((32, 1, TILES, 8, 128), lambda step: (0, half, 0, step, 0)),
+        grid=(6,),
+        in_specs=[
+            pl.BlockSpec(block, lambda step: (0, 0, jnp.minimum(step, 2), 0)),
+            pl.BlockSpec(block, lambda step: (0, 0, jnp.maximum(step - 3, 0), 0)),
+            pl.BlockSpec((1, 1, 8 * N), lambda step: (step % 3, 0, 0)),
+            whole(wave),
+            whole(to),
+            whole(back),
+        ],
+        out_specs=pl.BlockSpec((32, 1, TILES, 8, 128), lambda step: (0, step // 3, 0, step % 3, 0)),
         out_shape=jax.ShapeDtypeStruct((32, 2, TILES, 24, 128), jnp.float32),
-        input_output_aliases={5: 0} if earlier else {},
-        compiler_params=PARAMS,
+        compiler_params=pltpu.CompilerParams(vmem_limit_bytes=32 * 1024 * 1024),
         cost_estimate=COST,
         name="filter",
-    )(columns, pair_wave, wave, to, back, *earlier)
+    )(first, last, pair_wave, wave, to, back)
 
 
 def wavenumber(index):
@@ -432,11 +448,10 @@
     halves.append(lax.all_gather(second, "z", axis=0, tiled=False))
     spectra = []
     for bands in halves:
-        spectra.append(exchange_plane(forward(slots, orbital, bands).reshape(32, 216, 128)))
-    columns = []
-    for half, arrived in enumerate(spectra):
-        columns = [filtered(arrived.reshape(32, TILES, 24, 128), pair_wave, wave, half, *columns)]
-    potentials = exchange_plane(columns[0].reshape(32, 432, 128))
+        blocks = forward(slots, orbital, bands)
+        blocks, pair_wave, wave = lax.optimization_barrier((blocks, pair_wave, wave))
+        spectra.append(exchange_plane(blocks.reshape(32, 216, 128)).reshape(32, TILES, 24, 128))
+    potentials = exchange_plane(filtered(*spectra, pair_wave, wave).reshape(32, 432, 128))
     total = inverse(potentials.reshape(4, 8, 2, TILES, 24, 128), halves)
     back = exchange_plane(exchange_z(total).reshape(32, 56, 128))
     return from_blocks(back)

time: 392 us -> 391 us (level)
  blocking collectives: 138 us -> 185 us
  waiting for transfers between devices: 136 us -> 98 us
  starting transfers between devices: 47.1 us -> 40.7 us
    all_to_all x2 -> x3, blocking collectives: 108 us -> 156 us  [exchange_plane(): return lax.all_to_all(blocks, PLANE, 0, 0, tiled=True)]
    all_to_all x5 -> x4, waiting for transfers between devices: 77.2 us -> 39.6 us  [exchange_plane(): return lax.all_to_all(blocks, PLANE, 0, 0, tiled=True)]
    all_to_all x5 -> x4, starting transfers between devices: 31.2 us -> 24.8 us  [exchange_plane(): return lax.all_to_all(blocks, PLANE, 0, 0, tiled=True)]
    pallas_call x2 -> x1, Pallas kernels: 14 us -> 10.5 us  [filtered(): pl.pallas_call(filter_kernel, grid=(6,), in_specs=[pl.BlockSpec(block, la...]
  transfers between devices with their start and end apart: 14 -> 13, of which waited for: 12 -> 11; matrix products, arithmetic and copies ran while one was open for 1% -> 0% of each run, Pallas kernels for 8% -> 6%
where the time goes in v6:
time: 391 us; the launch traced here: 390 us
  blocking collectives  185 us (47%)
  waiting for transfers between devices  98 us (25%)
  Pallas kernels  51.2 us (13%)
  starting transfers between devices  40.7 us (10%)
  between operations  13.7 us (4%)
    all_to_all x3, blocking collectives, exchange_plane(): return lax.all_to_all(blocks, PLANE, 0, 0, tiled=True)  156 us
    all_to_all x4, waiting for transfers between devices, exchange_plane(): return lax.all_to_all(blocks, PLANE, 0, 0, tiled=True)  39.6 us
    all_gather x1, waiting for transfers between devices, shards(): halves.append(lax.all_gather(second, 'z', axis=0, tiled=False))  33.8 us
    all_to_all x1, blocking collectives, exchange_z(): return lax.all_to_all(blocks, 'z', 0, 0, tiled=True)  29.4 us
    all_to_all x4, starting transfers between devices, exchange_plane(): return lax.all_to_all(blocks, PLANE, 0, 0, tiled=True)  24.8 us
    ppermute x7, waiting for transfers between devices, gather_orbital(): lax.ppermute(piece, 'z', [(z, (z + shift) % 8) for z in range(8)])  21.2 us
    ppermute x7, starting transfers between devices, gather_orbital(): lax.ppermute(piece, 'z', [(z, (z + shift) % 8) for z in range(8)])  15.8 us
    pallas_call x2, Pallas kernels, forward(): pl.pallas_call(forward_kernel, grid=(4,), in_specs=[pl.BlockSpec(memory_s...  15.2 us
  transfers between devices with their start and end apart: 13, of which 11 were waited for; matrix products, arithmetic and copies ran while one was open for 0% of the time, Pallas kernels for 6%

profile of v6, /device:TPU:1, one launch (start us, length us, event | category | flops | bytes accessed | tf_op | source)
XLA Modules:
  0.0 389.7 jit_solution(16264621071125402841)
XLA Ops:
  6.5 3.8 pack.5
  10.3 8.7 %all-to-all-start = ((f32[32,112,128]{2,1,0:T(8,128)}), f32[32,112,128]{2,1,0:T(8,128)S(1)}, u32[]{:S(2)}, u32[]{:S(2)}) async-start(f32[32,112,128]{2,1,0:T(8,128)} %pack.5), calls=%async_computation | async-start | bytes 3670016 | tf_op jit(solution)/shard_map/all_to_all | solution.py:418
  19.1 0.0 all-gather.5.cloned.1.call-start
  19.1 2.5 pack.4
  21.6 23.1 %all-to-all-done = f32[32,112,128]{2,1,0:T(8,128)S(1)} async-done(((f32[32,112,128]{2,1,0:T(8,128)}), f32[32,112,128]{2,1,0:T(8,128)S(1)}, u32[]{:S(2)}, u32[]{:S(2)}) %all-to-all-start) | async-done | bytes 1835040 | tf_op jit(solution)/shard_map/all_to_all | solution.py:418
  44.7 1.4 choose.2
  46.1 0.0 all-gather.5.cloned.1.call-update
  46.1 4.7 %all-to-all-start.1 = ((f32[32,56,128]{2,1,0:T(8,128)}), f32[32,56,128]{2,1,0:T(8,128)S(1)}, u32[]{:S(2)}, u32[]{:S(2)}) async-start(f32[32,56,128]{2,1,0:T(8,128)} %pack.4), calls=%async_computation.1 | async-start | bytes 1835008 | tf_op jit(solution)/shard_map/all_to_all | solution.py:418
  50.8 0.0 copy-start.17
  50.8 3.8 pack.3
  54.6 11.8 %all-to-all-done.1 = f32[32,56,128]{2,1,0:T(8,128)S(1)} async-done(((f32[32,56,128]{2,1,0:T(8,128)}), f32[32,56,128]{2,1,0:T(8,128)S(1)}, u32[]{:S(2)}, u32[]{:S(2)}) %all-to-all-start.1) | async-done | bytes 917536 | tf_op jit(solution)/shard_map/all_to_all | solution.py:418
  66.4 3.8 all-to-all-start.2
  70.3 0.0 all-gather.7.cloned.1.call-start
  70.4 0.7 slots.1
  71.1 7.0 %collective-permute-start = (f32[24,1152]{1,0:T(8,128)S(1)}, f32[24,1152]{1,0:T(8,128)S(1)}, u32[]{:S(2)}, u32[]{:S(2)}) collective-permute-start(f32[24,1152]{1,0:T(8,128)S(1)} %get-tuple-element.36), channel_id=1, source_target_pairs={{0,8},{2,10},{4,12},{6,14},{8,0},{10,2},{12,4},{14,6},{1,9},{3,11}... | collective-permute-start | bytes 331784 | tf_op jit(solution)/shard_map/ppermute | solution.py:432
  78.1 1.6 collective-permute-start.1
  79.8 2.8 collective-permute-start.2
  82.6 1.2 collective-permute-start.3
  83.8 2.4 collective-permute-start.4
  86.2 0.7 collective-permute-start.5
  86.9 9.3 %collective-permute-done.1.refs_2_ = f32[24,1152]{1,0:T(8,128)S(1)} collective-permute-done((f32[24,1152]{1,0:T(8,128)S(1)}, f32[24,1152]{1,0:T(8,128)S(1)}, u32[]{:S(2)}, u32[]{:S(2)}) %collective-permute-start.1) | collective-permute-done | bytes 110624 | tf_op jit(solution)/shard_map/ppermute | solution.py:432
  96.2 0.0 collective-permute-start.6
  96.2 1.2 collective-permute-done.2.refs_3_
  97.4 4.5 %collective-permute-done.3.refs_4_ = f32[24,1152]{1,0:T(8,128)S(1)} collective-permute-done((f32[24,1152]{1,0:T(8,128)S(1)}, f32[24,1152]{1,0:T(8,128)S(1)}, u32[]{:S(2)}, u32[]{:S(2)}) %collective-permute-start.3) | collective-permute-done | bytes 110624 | tf_op jit(solution)/shard_map/ppermute | solution.py:432
  101.9 0.3 collective-permute-done.4.refs_5_
  102.2 4.2 %collective-permute-done.5.refs_6_ = f32[24,1152]{1,0:T(8,128)S(1)} collective-permute-done((f32[24,1152]{1,0:T(8,128)S(1)}, f32[24,1152]{1,0:T(8,128)S(1)}, u32[]{:S(2)}, u32[]{:S(2)}) %collective-permute-start.5) | collective-permute-done | bytes 110624 | tf_op jit(solution)/shard_map/ppermute | solution.py:432
  106.4 1.7 collective-permute-done.6.refs_7_
  108.1 1.4 choose.3
  109.5 0.0 all-gather.7.cloned.1.call-update
  109.6 0.1 add_add_fusion
  109.7 0.1 reshape.88
  109.8 0.6 and_select_fusion.1.slots_ref
  110.4 3.3 all-gather.5.cloned.1.call-done
  113.8 7.6 %forward.2 = f32[4,8,9,24,128]{4,3,2,1,0:T(8,128)} custom-call(s32[8]{0:T(128)} %and_select_fusion.1.slots_ref, f32[24,1152]{1,0:T(8,128)} %copy-done.3, f32[24,1152]{1,0:T(8,128)} %copy-done.9, f32[24,1152]{1,0:T(8,128)} %copy-done.10, f32[24,1152]{1,0:T(8,128)} %copy-done.11, f32[24,1152]{1,0:T(8,128)} %copy-done.12, f32[24,1152]{1,0:T(8,128)} %copy-done.13, ...), custom_call_target="tpu_custom_call" | custom-call | flops 16000000000 | bytes 10000000 | tf_op jit(solution)/shard_map/forward/pallas_call | solution.py:335
  121.4 7.6 %all-to-all-start.3 = ((f32[32,216,128]{2,1,0:T(8,128)}), f32[32,216,128]{2,1,0:T(8,128)}, u32[]{:S(2)}, u32[]{:S(2)}) async-start(f32[32,216,128]{2,1,0:T(8,128)} %bitcast.31), calls=%async_computation.3 | async-start | bytes 7077888 | tf_op jit(solution)/shard_map/all_to_all | solution.py:418
  129.0 33.8 %all-gather.7.cloned.1.call-done = f32[32,24,1152]{2,1,0:T(8,128)} async-done(((f32[4,24,1152]{2,1,0:T(8,128)}), f32[32,24,1152]{2,1,0:T(8,128)}) %all-gather.7.cloned.1.call-update) | async-done | bytes 3538960 | tf_op jit(solution)/shard_map/all_gather | solution.py:448
  162.8 7.6 %forward.3 = f32[4,8,9,24,128]{4,3,2,1,0:T(8,128)} custom-call(s32[8]{0:T(128)} %and_select_fusion.1.slots_ref, f32[24,1152]{1,0:T(8,128)} %copy-done.3, f32[24,1152]{1,0:T(8,128)} %copy-done.9, f32[24,1152]{1,0:T(8,128)} %copy-done.10, f32[24,1152]{1,0:T(8,128)} %copy-done.11, f32[24,1152]{1,0:T(8,128)} %copy-done.12, f32[24,1152]{1,0:T(8,128)} %copy-done.13, ...), custom_call_target="tpu_custom_call" | custom-call | flops 16000000000 | bytes 10000000 | tf_op jit(solution)/shard_map/forward/pallas_call | solution.py:335
  170.4 4.7 %all-to-all-done.3 = f32[32,216,128]{2,1,0:T(8,128)} async-done(((f32[32,216,128]{2,1,0:T(8,128)}), f32[32,216,128]{2,1,0:T(8,128)}, u32[]{:S(2)}, u32[]{:S(2)}) %all-to-all-start.3) | async-done | bytes 3538976 | tf_op jit(solution)/shard_map/all_to_all | solution.py:418
  175.2 50.3 %all_to_all.40 = f32[32,216,128]{2,1,0:T(8,128)S(1)} all-to-all(f32[32,216,128]{2,1,0:T(8,128)} %bitcast.32), channel_id=1, replica_groups=mesh['x_lo'=2,'y'=4,'x_hi'=2,'z'=8,'core'=2] {'x_lo','y','x_hi','core'}, dimensions={0} | all-to-all | bytes 7077888 | tf_op jit(solution)/shard_map/all_to_all | solution.py:418
  225.4 10.5 %filter.1 = f32[32,2,9,24,128]{4,3,2,1,0:T(8,128)S(1)} custom-call(f32[32,9,24,128]{3,2,1,0:T(8,128)} %bitcast.5.first_ref, f32[32,9,24,128]{3,2,1,0:T(8,128)S(1)} %bitcast.23, f32[3,1,1536]{2,1,0:T(1,128)S(1)} %reshape.89.refs_0_, f32[192,1]{1,0:T(8,128)S(1)} %fusion.2.refs_1_, bf16[192,576]{1,0:T(8,128)(2,1)S(1)} %copy-done.8, bf16[192,576]{1,0:T(8,128)(2,1)S(1)} %copy-done.7), custom_call_target="tpu_custom_call" | custom-call | flops 16000000000 | bytes 10000000 | tf_op jit(solution)/shard_map/filter/pallas_call | solution.py:384
  236.0 0.0 copy-start.4
  236.0 0.0 copy-start.5
  236.0 0.0 copy-start.6
  236.0 85.5 %all_to_all.41 = f32[32,432,128]{2,1,0:T(8,128)S(1)} all-to-all(f32[32,432,128]{2,1,0:T(8,128)S(1)} %bitcast.20), channel_id=1, replica_groups=mesh['x_lo'=2,'y'=4,'x_hi'=2,'z'=8,'core'=2] {'x_lo','y','x_hi','core'}, dimensions={0} | all-to-all | bytes 14155776 | tf_op jit(solution)/shard_map/all_to_all | solution.py:418
  321.6 10.6 %inverse.1 = f32[8,224,128]{2,1,0:T(8,128)S(1)} custom-call(f32[4,8,2,9,24,128]{5,4,3,2,1,0:T(8,128)S(1)} %bitcast.21, f32[8,4,24,1152]{3,2,1,0:T(8,128)S(1)} %bitcast.25, f32[8,4,24,1152]{3,2,1,0:T(8,128)S(1)} %bitcast.27, bf16[768,256]{1,0:T(8,128)(2,1)S(1)} %copy-done.4, bf16[768,256]{1,0:T(8,128)(2,1)S(1)} %copy-done.5, bf16[192,576]{1,0:T(8,128)(2,1)S(1)} %copy-done.6), custom_call_target="tpu_custom_call" | custom-call | flops 16000000000 | bytes 10000000 | tf_op jit(solution)/shard_map/inverse/pallas_call | solution.py:360
  332.2 29.4 %all_to_all.42 = f32[8,224,128]{2,1,0:T(8,128)S(1)} all-to-all(f32[8,224,128]{2,1,0:T(8,128)S(1)} %inverse.1), channel_id=1, replica_groups=mesh['x_lo'=2,'y'=4,'x_hi'=2,'z'=8,'core'=2] {'z'}, dimensions={0} | all-to-all | bytes 1835008 | tf_op jit(solution)/shard_map/all_to_all | solution.py:422
  361.6 19.9 %all_to_all.43.blocks_ref = f32[32,56,128]{2,1,0:T(8,128)S(1)} all-to-all(f32[32,56,128]{2,1,0:T(8,128)S(1)} %bitcast.30), channel_id=1, replica_groups=mesh['x_lo'=2,'y'=4,'x_hi'=2,'z'=8,'core'=2] {'x_lo','y','x_hi','core'}, dimensions={0} | all-to-all | bytes 1835008 | tf_op jit(solution)/shard_map/all_to_all | solution.py:418
  381.6 1.3 unpack.1
  (43 shorter events, 0.2 us)
Async XLA Ops:
  10.3 34.3 %copy-start = (s32[2]{0:T(128)S(1)}, s32[2]{0:T(128)}, u32[]{:S(2)}) copy-start(s32[2]{0:T(128)} %owner_ref.3) | copy-start | bytes 28
  10.3 34.3 %all-to-all-start = ((f32[32,112,128]{2,1,0:T(8,128)}), f32[32,112,128]{2,1,0:T(8,128)S(1)}, u32[]{:S(2)}, u32[]{:S(2)}) async-start(f32[32,112,128]{2,1,0:T(8,128)} %pack.5), calls=%async_computation | async-start | bytes 3670016 | tf_op jit(solution)/shard_map/all_to_all | solution.py:418
  19.1 94.7 %all-gather.5.cloned.1.call-start = ((), (), s32[]{:S(2)}) async-start(), calls=%async_computation.8 | async-start | bytes 3981312 | tf_op jit(solution)/shard_map/all_gather | solution.py:442
  46.1 20.3 %all-to-all-start.1 = ((f32[32,56,128]{2,1,0:T(8,128)}), f32[32,56,128]{2,1,0:T(8,128)S(1)}, u32[]{:S(2)}, u32[]{:S(2)}) async-start(f32[32,56,128]{2,1,0:T(8,128)} %pack.4), calls=%async_computation.1 | async-start | bytes 1835008 | tf_op jit(solution)/shard_map/all_to_all | solution.py:418
  50.8 19.6 %copy-start.17 = (s32[8]{0:T(128)S(1)}, s32[8]{0:T(128)}, u32[]{:S(2)}) copy-start(s32[8]{0:T(128)} %constant.80.clone) | copy-start | bytes 100
  54.6 55.2 %copy-start.16 = (s32[8]{0:T(128)S(1)}, s32[8]{0:T(128)}, u32[]{:S(2)}) copy-start(s32[8]{0:T(128)} %constant.90) | copy-start | bytes 100
  66.4 41.7 %all-to-all-start.2 = ((f32[32,112,128]{2,1,0:T(8,128)}), f32[32,112,128]{2,1,0:T(8,128)S(1)}, u32[]{:S(2)}, u32[]{:S(2)}) async-start(f32[32,112,128]{2,1,0:T(8,128)} %pack.3), calls=%async_computation.2 | async-start | bytes 3670016 | tf_op jit(solution)/shard_map/all_to_all | solution.py:418
  70.3 92.6 %all-gather.7.cloned.1.call-start = ((), (), s32[]{:S(2)}) async-start(), calls=%async_computation.9 | async-start | bytes 3981312 | tf_op jit(solution)/shard_map/all_gather | solution.py:448
  71.1 42.6 %copy-start.3 = (f32[24,1152]{1,0:T(8,128)}, f32[24,1152]{1,0:T(8,128)S(1)}, u32[]{:S(2)}) copy-start(f32[24,1152]{1,0:T(8,128)S(1)} %get-tuple-element.43.refs_0_) | copy-start | bytes 331780
  71.1 15.1 %collective-permute-start = (f32[24,1152]{1,0:T(8,128)S(1)}, f32[24,1152]{1,0:T(8,128)S(1)}, u32[]{:S(2)}, u32[]{:S(2)}) collective-permute-start(f32[24,1152]{1,0:T(8,128)S(1)} %get-tuple-element.36), channel_id=1, source_target_pairs={{0,8},{2,10},{4,12},{6,14},{8,0},{10,2},{12,4},{14,6},{1,9},{3,11}... | collective-permute-start | bytes 331784 | tf_op jit(solution)/shard_map/ppermute | solution.py:432
  78.1 18.1 %collective-permute-start.1 = (f32[24,1152]{1,0:T(8,128)S(1)}, f32[24,1152]{1,0:T(8,128)S(1)}, u32[]{:S(2)}, u32[]{:S(2)}) collective-permute-start(f32[24,1152]{1,0:T(8,128)S(1)} %get-tuple-element.37), channel_id=1, source_target_pairs={{0,6},{2,8},{4,10},{6,12},{8,14},{10,0},{12,2},{14,4},{1,7},{3,9},... | collective-permute-start | bytes 331784 | tf_op jit(solution)/shard_map/ppermute | solution.py:432
  79.8 17.7 %collective-permute-start.2 = (f32[24,1152]{1,0:T(8,128)S(1)}, f32[24,1152]{1,0:T(8,128)S(1)}, u32[]{:S(2)}, u32[]{:S(2)}) collective-permute-start(f32[24,1152]{1,0:T(8,128)S(1)} %get-tuple-element.38), channel_id=1, source_target_pairs={{0,10},{2,12},{4,14},{6,0},{8,2},{10,4},{12,6},{14,8},{1,11},{3,13... | collective-permute-start | bytes 331784 | tf_op jit(solution)/shard_map/ppermute | solution.py:432
  82.6 19.3 %collective-permute-start.3 = (f32[24,1152]{1,0:T(8,128)S(1)}, f32[24,1152]{1,0:T(8,128)S(1)}, u32[]{:S(2)}, u32[]{:S(2)}) collective-permute-start(f32[24,1152]{1,0:T(8,128)S(1)} %get-tuple-element.39), channel_id=1, source_target_pairs={{0,4},{2,6},{4,8},{6,10},{8,12},{10,14},{12,0},{14,2},{1,5},{3,7},... | collective-permute-start | bytes 331784 | tf_op jit(solution)/shard_map/ppermute | solution.py:432
  83.8 18.4 %collective-permute-start.4 = (f32[24,1152]{1,0:T(8,128)S(1)}, f32[24,1152]{1,0:T(8,128)S(1)}, u32[]{:S(2)}, u32[]{:S(2)}) collective-permute-start(f32[24,1152]{1,0:T(8,128)S(1)} %get-tuple-element.40), channel_id=1, source_target_pairs={{0,12},{2,14},{4,0},{6,2},{8,4},{10,6},{12,8},{14,10},{1,13},{3,15... | collective-permute-start | bytes 331784 | tf_op jit(solution)/shard_map/ppermute | solution.py:432
  86.2 27.6 %copy-start.9 = (f32[24,1152]{1,0:T(8,128)}, f32[24,1152]{1,0:T(8,128)S(1)}, u32[]{:S(2)}) copy-start(f32[24,1152]{1,0:T(8,128)S(1)} %collective-permute-done.refs_1_) | copy-start | bytes 331780
  86.2 20.2 %collective-permute-start.5 = (f32[24,1152]{1,0:T(8,128)S(1)}, f32[24,1152]{1,0:T(8,128)S(1)}, u32[]{:S(2)}, u32[]{:S(2)}) collective-permute-start(f32[24,1152]{1,0:T(8,128)S(1)} %get-tuple-element.41), channel_id=1, source_target_pairs={{0,2},{2,4},{4,6},{6,8},{8,10},{10,12},{12,14},{14,0},{1,3},{3,5},... | collective-permute-start | bytes 331784 | tf_op jit(solution)/shard_map/ppermute | solution.py:432
  96.2 17.6 %copy-start.10 = (f32[24,1152]{1,0:T(8,128)}, f32[24,1152]{1,0:T(8,128)S(1)}, u32[]{:S(2)}) copy-start(f32[24,1152]{1,0:T(8,128)S(1)} %collective-permute-done.1.refs_2_) | copy-start | bytes 331780
  96.2 11.9 %collective-permute-start.6 = (f32[24,1152]{1,0:T(8,128)S(1)}, f32[24,1152]{1,0:T(8,128)S(1)}, u32[]{:S(2)}, u32[]{:S(2)}) collective-permute-start(f32[24,1152]{1,0:T(8,128)S(1)} %get-tuple-element.42), channel_id=1, source_target_pairs={{0,14},{2,0},{4,2},{6,4},{8,6},{10,8},{12,10},{14,12},{1,15},{3,1}... | collective-permute-start | bytes 331784 | tf_op jit(solution)/shard_map/ppermute | solution.py:432
  97.4 16.3 %copy-start.11 = (f32[24,1152]{1,0:T(8,128)}, f32[24,1152]{1,0:T(8,128)S(1)}, u32[]{:S(2)}) copy-start(f32[24,1152]{1,0:T(8,128)S(1)} %collective-permute-done.2.refs_3_) | copy-start | bytes 331780
  101.9 11.8 %copy-start.12 = (f32[24,1152]{1,0:T(8,128)}, f32[24,1152]{1,0:T(8,128)S(1)}, u32[]{:S(2)}) copy-start(f32[24,1152]{1,0:T(8,128)S(1)} %collective-permute-done.3.refs_4_) | copy-start | bytes 331780
  102.2 11.5 %copy-start.13 = (f32[24,1152]{1,0:T(8,128)}, f32[24,1152]{1,0:T(8,128)S(1)}, u32[]{:S(2)}) copy-start(f32[24,1152]{1,0:T(8,128)S(1)} %collective-permute-done.4.refs_5_) | copy-start | bytes 331780
  106.4 7.4 %copy-start.14 = (f32[24,1152]{1,0:T(8,128)}, f32[24,1152]{1,0:T(8,128)S(1)}, u32[]{:S(2)}) copy-start(f32[24,1152]{1,0:T(8,128)S(1)} %collective-permute-done.5.refs_6_) | copy-start | bytes 331780
  108.1 5.7 %copy-start.15 = (f32[24,1152]{1,0:T(8,128)}, f32[24,1152]{1,0:T(8,128)S(1)}, u32[]{:S(2)}) copy-start(f32[24,1152]{1,0:T(8,128)S(1)} %collective-permute-done.6.refs_7_) | copy-start | bytes 331780
  121.4 53.7 %all-to-all-start.3 = ((f32[32,216,128]{2,1,0:T(8,128)}), f32[32,216,128]{2,1,0:T(8,128)}, u32[]{:S(2)}, u32[]{:S(2)}) async-start(f32[32,216,128]{2,1,0:T(8,128)} %bitcast.31), calls=%async_computation.3 | async-start | bytes 7077888 | tf_op jit(solution)/shard_map/all_to_all | solution.py:418
  175.1 50.3 %copy-start.7 = (bf16[192,576]{1,0:T(8,128)(2,1)S(1)}, bf16[192,576]{1,0:T(8,128)(2,1)}, u32[]{:S(2)}) copy-start(bf16[192,576]{1,0:T(8,128)(2,1)} %constant.85.clone.refs_3_) | copy-start | bytes 663556
  175.2 50.3 %copy-start.8 = (bf16[192,576]{1,0:T(8,128)(2,1)S(1)}, bf16[192,576]{1,0:T(8,128)(2,1)}, u32[]{:S(2)}) copy-start(bf16[192,576]{1,0:T(8,128)(2,1)} %constant.84.clone.refs_2_) | copy-start | bytes 663556
  236.0 85.6 %copy-start.1 = (f32[32,24,1152]{2,1,0:T(8,128)S(1)}, f32[32,24,1152]{2,1,0:T(8,128)}, u32[]{:S(2)}) copy-start(f32[32,24,1152]{2,1,0:T(8,128)} %all-gather.5.cloned.1.call-done) | copy-start | bytes 10616836
  236.0 85.6 %copy-start.2 = (f32[32,24,1152]{2,1,0:T(8,128)S(1)}, f32[32,24,1152]{2,1,0:T(8,128)}, u32[]{:S(2)}) copy-start(f32[32,24,1152]{2,1,0:T(8,128)} %all-gather.7.cloned.1.call-done) | copy-start | bytes 10616836
  236.0 85.6 %copy-start.4 = (bf16[768,256]{1,0:T(8,128)(2,1)S(1)}, bf16[768,256]{1,0:T(8,128)(2,1)}, u32[]{:S(2)}) copy-start(bf16[768,256]{1,0:T(8,128)(2,1)} %constant.81.clone.refs_9_.refs_3_) | copy-start | bytes 1179652
  236.0 85.6 %copy-start.5 = (bf16[768,256]{1,0:T(8,128)(2,1)S(1)}, bf16[768,256]{1,0:T(8,128)(2,1)}, u32[]{:S(2)}) copy-start(bf16[768,256]{1,0:T(8,128)(2,1)} %constant.86.clone.refs_4_) | copy-start | bytes 1179652
  236.0 85.6 %copy-start.6 = (bf16[192,576]{1,0:T(8,128)(2,1)S(1)}, bf16[192,576]{1,0:T(8,128)(2,1)}, u32[]{:S(2)}) copy-start(bf16[192,576]{1,0:T(8,128)(2,1)} %constant.87.clone.refs_5_) | copy-start | bytes 663556
Sparse Core Ops, SparseCore 0:
  46.2 67.4 all-gather.4
  115.5 47.2 all-gather.6

commit v7 on v6

--- a/solution.py
+++ b/solution.py
@@ -1,4 +1,3 @@
-import functools
 import math
 
 import jax
@@ -14,7 +13,6 @@
 LANES = 6 * N
 TILES = LANES // 128
 PLANE = ("x_lo", "y", "x_hi", "core")
-PARTS = 1
 VMEM = 62 * 1024 * 1024
 
 
@@ -80,14 +78,16 @@
 def lane_transform(value, even_ref, odd_ref):
     high, low = split(value)
 
+    starts = range(0, value.shape[1], 384)
+
     def stacked(terms, offset):
-        return jnp.concatenate([terms[:, s + offset : s + offset + 256] for s in range(0, LANES, 384)], axis=0)
+        return jnp.concatenate([terms[:, s + offset : s + offset + 256] for s in starts], axis=0)
 
     first = right_product(stacked(high, 0), stacked(low, 0), even_ref)
     last = right_product(stacked(high, 128), stacked(low, 128), odd_ref)
     middle = first[:, 128:] + last[:, :128]
     tiles = []
-    for start in range(0, 3 * N, N):
+    for start in range(0, len(starts) * N, N):
         for part in (first[:, :128], middle, last[:, 128:]):
             tiles.append(part[start : start + N])
     return jnp.concatenate(tiles, axis=1)
@@ -146,37 +146,31 @@
         out_ref[0, :, tile] = spectrum[:, 128 * tile : 128 * tile + 128].reshape(8, 24, 128)
 
 
-def joined(refs):
-    return jnp.concatenate([ref[:, 0].reshape(N // PARTS, LANES) for ref in refs], axis=0)
-
-
-def inverse_kernel(*refs):
-    spectrum_refs, first_refs, last_refs = refs[:PARTS], refs[PARTS : 2 * PARTS], refs[2 * PARTS : 3 * PARTS]
-    even_ref, odd_ref, rows_ref, out_ref, total_ref = refs[3 * PARTS :]
+def inverse_kernel(spectrum_ref, first_ref, last_ref, even_ref, odd_ref, rows_ref, out_ref, total_ref):
     step = pl.program_id(0)
-    spectrum = []
-    for ref in spectrum_refs:
-        tiles = [ref[0, :, 0, tile].reshape(N // PARTS, 128) for tile in range(TILES)]
-        spectrum.append(jnp.concatenate(tiles, axis=1))
-    spectrum = jnp.concatenate(spectrum, axis=0)
-    potential = left_product(rows_ref, spectrum)
+    tiles = [spectrum_ref[pair, :, 0, tile].reshape(N, 128) for pair in range(2) for tile in range(TILES)]
+    potential = left_product(rows_ref, jnp.concatenate(tiles, axis=1))
     potential = lane_transform(potential, even_ref, odd_ref)
     prefactor = -1.0 / math.sqrt(N * 8)
-    potential = jnp.where(step % 4 < 2, prefactor, 2.0 * prefactor) * potential
+    weight = jnp.where(step % 2 == 0, prefactor, 2.0 * prefactor)
+
+    def term(band_ref):
+        one = band_ref[:, 0].reshape(N, LANES) * potential[:, :LANES]
+        return weight * (one + band_ref[:, 1].reshape(N, LANES) * potential[:, LANES:])
 
     @pl.when(step == 0)
     def _():
-        total_ref[...] = joined(first_refs) * potential
-
-    @pl.when((step > 0) & (step < 4))
-    def _():
-        total_ref[...] += joined(first_refs) * potential
-
-    @pl.when(step >= 4)
-    def _():
-        total_ref[...] += joined(last_refs) * potential
-
-    @pl.when(step == 7)
+        total_ref[...] = term(first_ref)
+
+    @pl.when(step == 1)
+    def _():
+        total_ref[...] += term(first_ref)
+
+    @pl.when(step >= 2)
+    def _():
+        total_ref[...] += term(last_ref)
+
+    @pl.when(step == 3)
     def _():
         for z in range(8):
             for source in range(4):
@@ -279,16 +273,6 @@
     )(planes)
 
 
-def in_parts(shape, dim, place):
-    block = shape[:dim] + (shape[dim] // PARTS,) + shape[dim + 1 :]
-
-    def part_place(part, step):
-        at = place(step)
-        return at[:dim] + (part,) + at[dim + 1 :]
-
-    return [pl.BlockSpec(block, functools.partial(part_place, part)) for part in range(PARTS)]
-
-
 def from_blocks(blocks):
     return pl.pallas_call(
         unpack_kernel,
@@ -359,11 +343,11 @@
     out = jax.ShapeDtypeStruct((8, 224, 128), jnp.float32)
     return pl.pallas_call(
         inverse_kernel,
-        grid=(8,),
+        grid=(4,),
         in_specs=[
-            *in_parts((1, 8, 1, TILES, 24, 128), 1, lambda step: (step % 4, 0, step // 4, 0, 0, 0)),
-            *in_parts((8, 1, 24, LANES), 0, lambda step: (0, jnp.minimum(step, 3), 0, 0)),
-            *in_parts((8, 1, 24, LANES), 0, lambda step: (0, jnp.maximum(step - 4, 0), 0, 0)),
+            pl.BlockSpec((2, 8, 1, TILES, 24, 128), lambda step: (step % 2, 0, step // 2, 0, 0, 0)),
+            pl.BlockSpec((8, 2, 24, LANES), lambda step: (0, jnp.minimum(step, 1), 0, 0)),
+            pl.BlockSpec((8, 2, 24, LANES), lambda step: (0, jnp.maximum(step - 2, 0), 0, 0)),
             whole(even),
             whole(odd),
             whole(rows),
@@ -374,7 +358,7 @@
         compiler_params=pltpu.CompilerParams(vmem_limit_bytes=32 * 1024 * 1024),
         cost_estimate=COST,
         name="inverse",
-    )(*[spectra] * PARTS, *[bands[0]] * PARTS, *[bands[1]] * PARTS, even, odd, rows)
+    )(spectra, *bands, even, odd, rows)
 
 
 def filtered(first, last, pair_wave, wave):

time: 391 us -> 389 us (level)
  no operation moved by 1% of the time
where the time goes in v7:
time: 389 us
  blocking collectives  185 us (48%)
  waiting for transfers between devices  98 us (25%)
  Pallas kernels  50.1 us (13%)
  starting transfers between devices  40.7 us (10%)
  between operations  13.7 us (4%)
    all_to_all x3, blocking collectives, exchange_plane(): return lax.all_to_all(blocks, PLANE, 0, 0, tiled=True)  156 us
    all_to_all x4, waiting for transfers between devices, exchange_plane(): return lax.all_to_all(blocks, PLANE, 0, 0, tiled=True)  39.6 us
    all_gather x1, waiting for transfers between devices, shards(): halves.append(lax.all_gather(second, 'z', axis=0, tiled=False))  33.8 us
    all_to_all x1, blocking collectives, exchange_z(): return lax.all_to_all(blocks, 'z', 0, 0, tiled=True)  29.4 us
    all_to_all x4, starting transfers between devices, exchange_plane(): return lax.all_to_all(blocks, PLANE, 0, 0, tiled=True)  24.8 us
    ppermute x7, waiting for transfers between devices, gather_orbital(): lax.ppermute(piece, 'z', [(z, (z + shift) % 8) for z in range(8)])  21.2 us
    ppermute x7, starting transfers between devices, gather_orbital(): lax.ppermute(piece, 'z', [(z, (z + shift) % 8) for z in range(8)])  15.8 us
    pallas_call x2, Pallas kernels, forward(): pl.pallas_call(forward_kernel, grid=(4,), in_specs=[pl.BlockSpec(memory_s...  15.2 us
  transfers between devices with their start and end apart: 13, of which 11 were waited for; matrix products, arithmetic and copies ran while one was open for 0% of the time, Pallas kernels for 6%

profile of v7, /device:TPU:1, one launch (start us, length us, event | category | flops | bytes accessed | tf_op | source)
XLA Modules:
  0.0 388.6 jit_solution(2201827869579054307)
XLA Ops:
  6.5 3.8 pack.5
  10.3 8.7 %all-to-all-start = ((f32[32,112,128]{2,1,0:T(8,128)}), f32[32,112,128]{2,1,0:T(8,128)S(1)}, u32[]{:S(2)}, u32[]{:S(2)}) async-start(f32[32,112,128]{2,1,0:T(8,128)} %pack.5), calls=%async_computation | async-start | bytes 3670016 | tf_op jit(solution)/shard_map/all_to_all | solution.py:402
  19.1 0.0 all-gather.5.cloned.1.call-start
  19.1 2.5 pack.4
  21.6 23.1 %all-to-all-done = f32[32,112,128]{2,1,0:T(8,128)S(1)} async-done(((f32[32,112,128]{2,1,0:T(8,128)}), f32[32,112,128]{2,1,0:T(8,128)S(1)}, u32[]{:S(2)}, u32[]{:S(2)}) %all-to-all-start) | async-done | bytes 1835040 | tf_op jit(solution)/shard_map/all_to_all | solution.py:402
  44.7 1.4 choose.2
  46.1 0.0 all-gather.5.cloned.1.call-update
  46.1 4.7 %all-to-all-start.1 = ((f32[32,56,128]{2,1,0:T(8,128)}), f32[32,56,128]{2,1,0:T(8,128)S(1)}, u32[]{:S(2)}, u32[]{:S(2)}) async-start(f32[32,56,128]{2,1,0:T(8,128)} %pack.4), calls=%async_computation.1 | async-start | bytes 1835008 | tf_op jit(solution)/shard_map/all_to_all | solution.py:402
  50.8 0.0 copy-start.17
  50.8 3.8 pack.3
  54.6 11.8 %all-to-all-done.1 = f32[32,56,128]{2,1,0:T(8,128)S(1)} async-done(((f32[32,56,128]{2,1,0:T(8,128)}), f32[32,56,128]{2,1,0:T(8,128)S(1)}, u32[]{:S(2)}, u32[]{:S(2)}) %all-to-all-start.1) | async-done | bytes 917536 | tf_op jit(solution)/shard_map/all_to_all | solution.py:402
  66.4 3.8 all-to-all-start.2
  70.3 0.0 all-gather.7.cloned.1.call-start
  70.4 0.7 slots.1
  71.1 7.0 %collective-permute-start = (f32[24,1152]{1,0:T(8,128)S(1)}, f32[24,1152]{1,0:T(8,128)S(1)}, u32[]{:S(2)}, u32[]{:S(2)}) collective-permute-start(f32[24,1152]{1,0:T(8,128)S(1)} %get-tuple-element.36), channel_id=1, source_target_pairs={{0,8},{2,10},{4,12},{6,14},{8,0},{10,2},{12,4},{14,6},{1,9},{3,11}... | collective-permute-start | bytes 331784 | tf_op jit(solution)/shard_map/ppermute | solution.py:416
  78.1 1.6 collective-permute-start.1
  79.8 2.8 collective-permute-start.2
  82.6 1.2 collective-permute-start.3
  83.8 2.4 collective-permute-start.4
  86.2 0.7 collective-permute-start.5
  86.9 9.3 %collective-permute-done.1.refs_2_ = f32[24,1152]{1,0:T(8,128)S(1)} collective-permute-done((f32[24,1152]{1,0:T(8,128)S(1)}, f32[24,1152]{1,0:T(8,128)S(1)}, u32[]{:S(2)}, u32[]{:S(2)}) %collective-permute-start.1) | collective-permute-done | bytes 110624 | tf_op jit(solution)/shard_map/ppermute | solution.py:416
  96.2 0.0 collective-permute-start.6
  96.2 1.2 collective-permute-done.2.refs_3_
  97.4 4.5 %collective-permute-done.3.refs_4_ = f32[24,1152]{1,0:T(8,128)S(1)} collective-permute-done((f32[24,1152]{1,0:T(8,128)S(1)}, f32[24,1152]{1,0:T(8,128)S(1)}, u32[]{:S(2)}, u32[]{:S(2)}) %collective-permute-start.3) | collective-permute-done | bytes 110624 | tf_op jit(solution)/shard_map/ppermute | solution.py:416
  101.9 0.3 collective-permute-done.4.refs_5_
  102.2 4.2 %collective-permute-done.5.refs_6_ = f32[24,1152]{1,0:T(8,128)S(1)} collective-permute-done((f32[24,1152]{1,0:T(8,128)S(1)}, f32[24,1152]{1,0:T(8,128)S(1)}, u32[]{:S(2)}, u32[]{:S(2)}) %collective-permute-start.5) | collective-permute-done | bytes 110624 | tf_op jit(solution)/shard_map/ppermute | solution.py:416
  106.4 1.7 collective-permute-done.6.refs_7_
  108.1 1.4 choose.3
  109.5 0.0 all-gather.7.cloned.1.call-update
  109.6 0.1 add_add_fusion
  109.7 0.1 reshape.88
  109.8 0.6 and_select_fusion.1.slots_ref
  110.4 3.3 all-gather.5.cloned.1.call-done
  113.8 7.6 %forward.2 = f32[4,8,9,24,128]{4,3,2,1,0:T(8,128)} custom-call(s32[8]{0:T(128)} %and_select_fusion.1.slots_ref, f32[24,1152]{1,0:T(8,128)} %copy-done.3, f32[24,1152]{1,0:T(8,128)} %copy-done.9, f32[24,1152]{1,0:T(8,128)} %copy-done.10, f32[24,1152]{1,0:T(8,128)} %copy-done.11, f32[24,1152]{1,0:T(8,128)} %copy-done.12, f32[24,1152]{1,0:T(8,128)} %copy-done.13, ...), custom_call_target="tpu_custom_call" | custom-call | flops 16000000000 | bytes 10000000 | tf_op jit(solution)/shard_map/forward/pallas_call | solution.py:319
  121.4 7.6 %all-to-all-start.3 = ((f32[32,216,128]{2,1,0:T(8,128)}), f32[32,216,128]{2,1,0:T(8,128)}, u32[]{:S(2)}, u32[]{:S(2)}) async-start(f32[32,216,128]{2,1,0:T(8,128)} %bitcast.31), calls=%async_computation.3 | async-start | bytes 7077888 | tf_op jit(solution)/shard_map/all_to_all | solution.py:402
  129.0 33.8 %all-gather.7.cloned.1.call-done = f32[32,24,1152]{2,1,0:T(8,128)} async-done(((f32[4,24,1152]{2,1,0:T(8,128)}), f32[32,24,1152]{2,1,0:T(8,128)}) %all-gather.7.cloned.1.call-update) | async-done | bytes 3538960 | tf_op jit(solution)/shard_map/all_gather | solution.py:432
  162.8 7.6 %forward.3 = f32[4,8,9,24,128]{4,3,2,1,0:T(8,128)} custom-call(s32[8]{0:T(128)} %and_select_fusion.1.slots_ref, f32[24,1152]{1,0:T(8,128)} %copy-done.3, f32[24,1152]{1,0:T(8,128)} %copy-done.9, f32[24,1152]{1,0:T(8,128)} %copy-done.10, f32[24,1152]{1,0:T(8,128)} %copy-done.11, f32[24,1152]{1,0:T(8,128)} %copy-done.12, f32[24,1152]{1,0:T(8,128)} %copy-done.13, ...), custom_call_target="tpu_custom_call" | custom-call | flops 16000000000 | bytes 10000000 | tf_op jit(solution)/shard_map/forward/pallas_call | solution.py:319
  170.4 4.7 %all-to-all-done.3 = f32[32,216,128]{2,1,0:T(8,128)} async-done(((f32[32,216,128]{2,1,0:T(8,128)}), f32[32,216,128]{2,1,0:T(8,128)}, u32[]{:S(2)}, u32[]{:S(2)}) %all-to-all-start.3) | async-done | bytes 3538976 | tf_op jit(solution)/shard_map/all_to_all | solution.py:402
  175.2 50.3 %all_to_all.40 = f32[32,216,128]{2,1,0:T(8,128)S(1)} all-to-all(f32[32,216,128]{2,1,0:T(8,128)} %bitcast.32), channel_id=1, replica_groups=mesh['x_lo'=2,'y'=4,'x_hi'=2,'z'=8,'core'=2] {'x_lo','y','x_hi','core'}, dimensions={0} | all-to-all | bytes 7077888 | tf_op jit(solution)/shard_map/all_to_all | solution.py:402
  225.4 10.5 %filter.1 = f32[32,2,9,24,128]{4,3,2,1,0:T(8,128)S(1)} custom-call(f32[32,9,24,128]{3,2,1,0:T(8,128)} %bitcast.5.first_ref, f32[32,9,24,128]{3,2,1,0:T(8,128)S(1)} %bitcast.23, f32[3,1,1536]{2,1,0:T(1,128)S(1)} %reshape.89.refs_0_, f32[192,1]{1,0:T(8,128)S(1)} %fusion.2.refs_1_, bf16[192,576]{1,0:T(8,128)(2,1)S(1)} %copy-done.8, bf16[192,576]{1,0:T(8,128)(2,1)S(1)} %copy-done.7), custom_call_target="tpu_custom_call" | custom-call | flops 16000000000 | bytes 10000000 | tf_op jit(solution)/shard_map/filter/pallas_call | solution.py:368
  236.0 0.0 copy-start.4
  236.0 0.0 copy-start.5
  236.0 0.0 copy-start.6
  236.0 85.5 %all_to_all.41 = f32[32,432,128]{2,1,0:T(8,128)S(1)} all-to-all(f32[32,432,128]{2,1,0:T(8,128)S(1)} %bitcast.20), channel_id=1, replica_groups=mesh['x_lo'=2,'y'=4,'x_hi'=2,'z'=8,'core'=2] {'x_lo','y','x_hi','core'}, dimensions={0} | all-to-all | bytes 14155776 | tf_op jit(solution)/shard_map/all_to_all | solution.py:402
  321.6 9.4 %inverse.1 = f32[8,224,128]{2,1,0:T(8,128)S(1)} custom-call(f32[4,8,2,9,24,128]{5,4,3,2,1,0:T(8,128)S(1)} %bitcast.21, f32[8,4,24,1152]{3,2,1,0:T(8,128)S(1)} %bitcast.25, f32[8,4,24,1152]{3,2,1,0:T(8,128)S(1)} %bitcast.27, bf16[768,256]{1,0:T(8,128)(2,1)S(1)} %copy-done.4, bf16[768,256]{1,0:T(8,128)(2,1)S(1)} %copy-done.5, bf16[192,576]{1,0:T(8,128)(2,1)S(1)} %copy-done.6), custom_call_target="tpu_custom_call" | custom-call | flops 16000000000 | bytes 10000000 | tf_op jit(solution)/shard_map/inverse/pallas_call | solution.py:344
  331.1 29.4 %all_to_all.42 = f32[8,224,128]{2,1,0:T(8,128)S(1)} all-to-all(f32[8,224,128]{2,1,0:T(8,128)S(1)} %inverse.1), channel_id=1, replica_groups=mesh['x_lo'=2,'y'=4,'x_hi'=2,'z'=8,'core'=2] {'z'}, dimensions={0} | all-to-all | bytes 1835008 | tf_op jit(solution)/shard_map/all_to_all | solution.py:406
  360.5 20.0 %all_to_all.43.blocks_ref = f32[32,56,128]{2,1,0:T(8,128)S(1)} all-to-all(f32[32,56,128]{2,1,0:T(8,128)S(1)} %bitcast.30), channel_id=1, replica_groups=mesh['x_lo'=2,'y'=4,'x_hi'=2,'z'=8,'core'=2] {'x_lo','y','x_hi','core'}, dimensions={0} | all-to-all | bytes 1835008 | tf_op jit(solution)/shard_map/all_to_all | solution.py:402
  380.4 1.3 unpack.1
  (43 shorter events, 0.2 us)
Async XLA Ops:
  10.3 34.3 %copy-start = (s32[2]{0:T(128)S(1)}, s32[2]{0:T(128)}, u32[]{:S(2)}) copy-start(s32[2]{0:T(128)} %owner_ref.3) | copy-start | bytes 28
  10.3 34.3 %all-to-all-start = ((f32[32,112,128]{2,1,0:T(8,128)}), f32[32,112,128]{2,1,0:T(8,128)S(1)}, u32[]{:S(2)}, u32[]{:S(2)}) async-start(f32[32,112,128]{2,1,0:T(8,128)} %pack.5), calls=%async_computation | async-start | bytes 3670016 | tf_op jit(solution)/shard_map/all_to_all | solution.py:402
  19.1 94.7 %all-gather.5.cloned.1.call-start = ((), (), s32[]{:S(2)}) async-start(), calls=%async_computation.8 | async-start | bytes 3981312 | tf_op jit(solution)/shard_map/all_gather | solution.py:426
  46.1 20.3 %all-to-all-start.1 = ((f32[32,56,128]{2,1,0:T(8,128)}), f32[32,56,128]{2,1,0:T(8,128)S(1)}, u32[]{:S(2)}, u32[]{:S(2)}) async-start(f32[32,56,128]{2,1,0:T(8,128)} %pack.4), calls=%async_computation.1 | async-start | bytes 1835008 | tf_op jit(solution)/shard_map/all_to_all | solution.py:402
  50.8 19.6 %copy-start.17 = (s32[8]{0:T(128)S(1)}, s32[8]{0:T(128)}, u32[]{:S(2)}) copy-start(s32[8]{0:T(128)} %constant.80.clone) | copy-start | bytes 100
  54.6 55.2 %copy-start.16 = (s32[8]{0:T(128)S(1)}, s32[8]{0:T(128)}, u32[]{:S(2)}) copy-start(s32[8]{0:T(128)} %constant.90) | copy-start | bytes 100
  66.4 41.7 %all-to-all-start.2 = ((f32[32,112,128]{2,1,0:T(8,128)}), f32[32,112,128]{2,1,0:T(8,128)S(1)}, u32[]{:S(2)}, u32[]{:S(2)}) async-start(f32[32,112,128]{2,1,0:T(8,128)} %pack.3), calls=%async_computation.2 | async-start | bytes 3670016 | tf_op jit(solution)/shard_map/all_to_all | solution.py:402
  70.3 92.6 %all-gather.7.cloned.1.call-start = ((), (), s32[]{:S(2)}) async-start(), calls=%async_computation.9 | async-start | bytes 3981312 | tf_op jit(solution)/shard_map/all_gather | solution.py:432
  71.1 42.6 %copy-start.3 = (f32[24,1152]{1,0:T(8,128)}, f32[24,1152]{1,0:T(8,128)S(1)}, u32[]{:S(2)}) copy-start(f32[24,1152]{1,0:T(8,128)S(1)} %get-tuple-element.43.refs_0_) | copy-start | bytes 331780
  71.1 15.1 %collective-permute-start = (f32[24,1152]{1,0:T(8,128)S(1)}, f32[24,1152]{1,0:T(8,128)S(1)}, u32[]{:S(2)}, u32[]{:S(2)}) collective-permute-start(f32[24,1152]{1,0:T(8,128)S(1)} %get-tuple-element.36), channel_id=1, source_target_pairs={{0,8},{2,10},{4,12},{6,14},{8,0},{10,2},{12,4},{14,6},{1,9},{3,11}... | collective-permute-start | bytes 331784 | tf_op jit(solution)/shard_map/ppermute | solution.py:416
  78.1 18.1 %collective-permute-start.1 = (f32[24,1152]{1,0:T(8,128)S(1)}, f32[24,1152]{1,0:T(8,128)S(1)}, u32[]{:S(2)}, u32[]{:S(2)}) collective-permute-start(f32[24,1152]{1,0:T(8,128)S(1)} %get-tuple-element.37), channel_id=1, source_target_pairs={{0,6},{2,8},{4,10},{6,12},{8,14},{10,0},{12,2},{14,4},{1,7},{3,9},... | collective-permute-start | bytes 331784 | tf_op jit(solution)/shard_map/ppermute | solution.py:416
  79.8 17.7 %collective-permute-start.2 = (f32[24,1152]{1,0:T(8,128)S(1)}, f32[24,1152]{1,0:T(8,128)S(1)}, u32[]{:S(2)}, u32[]{:S(2)}) collective-permute-start(f32[24,1152]{1,0:T(8,128)S(1)} %get-tuple-element.38), channel_id=1, source_target_pairs={{0,10},{2,12},{4,14},{6,0},{8,2},{10,4},{12,6},{14,8},{1,11},{3,13... | collective-permute-start | bytes 331784 | tf_op jit(solution)/shard_map/ppermute | solution.py:416
  82.6 19.3 %collective-permute-start.3 = (f32[24,1152]{1,0:T(8,128)S(1)}, f32[24,1152]{1,0:T(8,128)S(1)}, u32[]{:S(2)}, u32[]{:S(2)}) collective-permute-start(f32[24,1152]{1,0:T(8,128)S(1)} %get-tuple-element.39), channel_id=1, source_target_pairs={{0,4},{2,6},{4,8},{6,10},{8,12},{10,14},{12,0},{14,2},{1,5},{3,7},... | collective-permute-start | bytes 331784 | tf_op jit(solution)/shard_map/ppermute | solution.py:416
  83.8 18.4 %collective-permute-start.4 = (f32[24,1152]{1,0:T(8,128)S(1)}, f32[24,1152]{1,0:T(8,128)S(1)}, u32[]{:S(2)}, u32[]{:S(2)}) collective-permute-start(f32[24,1152]{1,0:T(8,128)S(1)} %get-tuple-element.40), channel_id=1, source_target_pairs={{0,12},{2,14},{4,0},{6,2},{8,4},{10,6},{12,8},{14,10},{1,13},{3,15... | collective-permute-start | bytes 331784 | tf_op jit(solution)/shard_map/ppermute | solution.py:416
  86.2 27.6 %copy-start.9 = (f32[24,1152]{1,0:T(8,128)}, f32[24,1152]{1,0:T(8,128)S(1)}, u32[]{:S(2)}) copy-start(f32[24,1152]{1,0:T(8,128)S(1)} %collective-permute-done.refs_1_) | copy-start | bytes 331780
  86.2 20.2 %collective-permute-start.5 = (f32[24,1152]{1,0:T(8,128)S(1)}, f32[24,1152]{1,0:T(8,128)S(1)}, u32[]{:S(2)}, u32[]{:S(2)}) collective-permute-start(f32[24,1152]{1,0:T(8,128)S(1)} %get-tuple-element.41), channel_id=1, source_target_pairs={{0,2},{2,4},{4,6},{6,8},{8,10},{10,12},{12,14},{14,0},{1,3},{3,5},... | collective-permute-start | bytes 331784 | tf_op jit(solution)/shard_map/ppermute | solution.py:416
  96.2 17.6 %copy-start.10 = (f32[24,1152]{1,0:T(8,128)}, f32[24,1152]{1,0:T(8,128)S(1)}, u32[]{:S(2)}) copy-start(f32[24,1152]{1,0:T(8,128)S(1)} %collective-permute-done.1.refs_2_) | copy-start | bytes 331780
  96.2 11.9 %collective-permute-start.6 = (f32[24,1152]{1,0:T(8,128)S(1)}, f32[24,1152]{1,0:T(8,128)S(1)}, u32[]{:S(2)}, u32[]{:S(2)}) collective-permute-start(f32[24,1152]{1,0:T(8,128)S(1)} %get-tuple-element.42), channel_id=1, source_target_pairs={{0,14},{2,0},{4,2},{6,4},{8,6},{10,8},{12,10},{14,12},{1,15},{3,1}... | collective-permute-start | bytes 331784 | tf_op jit(solution)/shard_map/ppermute | solution.py:416
  97.4 16.3 %copy-start.11 = (f32[24,1152]{1,0:T(8,128)}, f32[24,1152]{1,0:T(8,128)S(1)}, u32[]{:S(2)}) copy-start(f32[24,1152]{1,0:T(8,128)S(1)} %collective-permute-done.2.refs_3_) | copy-start | bytes 331780
  101.9 11.8 %copy-start.12 = (f32[24,1152]{1,0:T(8,128)}, f32[24,1152]{1,0:T(8,128)S(1)}, u32[]{:S(2)}) copy-start(f32[24,1152]{1,0:T(8,128)S(1)} %collective-permute-done.3.refs_4_) | copy-start | bytes 331780
  102.2 11.5 %copy-start.13 = (f32[24,1152]{1,0:T(8,128)}, f32[24,1152]{1,0:T(8,128)S(1)}, u32[]{:S(2)}) copy-start(f32[24,1152]{1,0:T(8,128)S(1)} %collective-permute-done.4.refs_5_) | copy-start | bytes 331780
  106.4 7.4 %copy-start.14 = (f32[24,1152]{1,0:T(8,128)}, f32[24,1152]{1,0:T(8,128)S(1)}, u32[]{:S(2)}) copy-start(f32[24,1152]{1,0:T(8,128)S(1)} %collective-permute-done.5.refs_6_) | copy-start | bytes 331780
  108.1 5.7 %copy-start.15 = (f32[24,1152]{1,0:T(8,128)}, f32[24,1152]{1,0:T(8,128)S(1)}, u32[]{:S(2)}) copy-start(f32[24,1152]{1,0:T(8,128)S(1)} %collective-permute-done.6.refs_7_) | copy-start | bytes 331780
  121.4 53.7 %all-to-all-start.3 = ((f32[32,216,128]{2,1,0:T(8,128)}), f32[32,216,128]{2,1,0:T(8,128)}, u32[]{:S(2)}, u32[]{:S(2)}) async-start(f32[32,216,128]{2,1,0:T(8,128)} %bitcast.31), calls=%async_computation.3 | async-start | bytes 7077888 | tf_op jit(solution)/shard_map/all_to_all | solution.py:402
  175.1 50.3 %copy-start.7 = (bf16[192,576]{1,0:T(8,128)(2,1)S(1)}, bf16[192,576]{1,0:T(8,128)(2,1)}, u32[]{:S(2)}) copy-start(bf16[192,576]{1,0:T(8,128)(2,1)} %constant.85.clone.refs_3_) | copy-start | bytes 663556
  175.2 50.3 %copy-start.8 = (bf16[192,576]{1,0:T(8,128)(2,1)S(1)}, bf16[192,576]{1,0:T(8,128)(2,1)}, u32[]{:S(2)}) copy-start(bf16[192,576]{1,0:T(8,128)(2,1)} %constant.84.clone.refs_2_) | copy-start | bytes 663556
  236.0 85.6 %copy-start.1 = (f32[32,24,1152]{2,1,0:T(8,128)S(1)}, f32[32,24,1152]{2,1,0:T(8,128)}, u32[]{:S(2)}) copy-start(f32[32,24,1152]{2,1,0:T(8,128)} %all-gather.5.cloned.1.call-done) | copy-start | bytes 10616836
  236.0 85.6 %copy-start.2 = (f32[32,24,1152]{2,1,0:T(8,128)S(1)}, f32[32,24,1152]{2,1,0:T(8,128)}, u32[]{:S(2)}) copy-start(f32[32,24,1152]{2,1,0:T(8,128)} %all-gather.7.cloned.1.call-done) | copy-start | bytes 10616836
  236.0 85.6 %copy-start.4 = (bf16[768,256]{1,0:T(8,128)(2,1)S(1)}, bf16[768,256]{1,0:T(8,128)(2,1)}, u32[]{:S(2)}) copy-start(bf16[768,256]{1,0:T(8,128)(2,1)} %constant.81.clone.refs_9_.even_ref) | copy-start | bytes 1179652
  236.0 85.6 %copy-start.5 = (bf16[768,256]{1,0:T(8,128)(2,1)S(1)}, bf16[768,256]{1,0:T(8,128)(2,1)}, u32[]{:S(2)}) copy-start(bf16[768,256]{1,0:T(8,128)(2,1)} %constant.86.clone.odd_ref) | copy-start | bytes 1179652
  236.0 85.6 %copy-start.6 = (bf16[192,576]{1,0:T(8,128)(2,1)S(1)}, bf16[192,576]{1,0:T(8,128)(2,1)}, u32[]{:S(2)}) copy-start(bf16[192,576]{1,0:T(8,128)(2,1)} %constant.87.clone.rows_ref) | copy-start | bytes 663556
Sparse Core Ops, SparseCore 0:
  46.2 67.4 all-gather.4
  115.5 47.2 all-gather.6

commit v8 on v7

--- a/solution.py
+++ b/solution.py
@@ -197,7 +197,7 @@
         out_ref[0, a, :, 128:] = right[:, :64]
 
 
-def filter_block(columns_ref, pair_ref, wave_ref, to_ref, from_ref, out_ref):
+def filter_block(columns_ref, to_ref, from_ref, out_ref, coulomb_ref):
     source = columns_ref.reshape(32 * TILES * 8, 128)
     target = out_ref.reshape(32 * TILES * 8, 128)
     lower = lax.broadcasted_iota(jnp.int32, (32, 128), 1) < 64
@@ -218,7 +218,7 @@
         blocks.append(jnp.concatenate(parts, axis=0))
     columns = jnp.concatenate(blocks, axis=1)
     spectrum = left_product(to_ref, columns)
-    spectrum = spectrum * ((4.0 * math.pi / float(N) ** 3) / (wave_ref[...] + pair_ref[0]))
+    spectrum = spectrum * coulomb_ref[...]
     columns = left_product(from_ref, spectrum)
     for k in range(8):
         for i in range(6):
@@ -233,14 +233,16 @@
             target[rows(3 * h + 1, k + 1), :] = jnp.where(lower, pltpu.roll(one, 64, 1), two)
 
 
-def filter_kernel(first_ref, last_ref, *refs):
-    step = pl.program_id(0)
-
-    @pl.when(step < 3)
-    def _():
+def filter_kernel(first_ref, last_ref, pair_ref, wave_ref, *refs):
+    coulomb_ref = refs[-1]
+    half = pl.program_id(0) % 2
+
+    @pl.when(half == 0)
+    def _():
+        coulomb_ref[...] = (4.0 * math.pi / float(N) ** 3) / (wave_ref[...] + pair_ref[0])
         filter_block(first_ref, *refs)
 
-    @pl.when(step >= 3)
+    @pl.when(half == 1)
     def _():
         filter_block(last_ref, *refs)
 
@@ -369,15 +371,16 @@
         filter_kernel,
         grid=(6,),
         in_specs=[
-            pl.BlockSpec(block, lambda step: (0, 0, jnp.minimum(step, 2), 0)),
-            pl.BlockSpec(block, lambda step: (0, 0, jnp.maximum(step - 3, 0), 0)),
-            pl.BlockSpec((1, 1, 8 * N), lambda step: (step % 3, 0, 0)),
+            pl.BlockSpec(block, lambda step: (0, 0, step // 2, 0)),
+            pl.BlockSpec(block, lambda step: (0, 0, step // 2, 0)),
+            pl.BlockSpec((1, 1, 8 * N), lambda step: (step // 2, 0, 0)),
             whole(wave),
             whole(to),
             whole(back),
         ],
-        out_specs=pl.BlockSpec((32, 1, TILES, 8, 128), lambda step: (0, step // 3, 0, step % 3, 0)),
+        out_specs=pl.BlockSpec((32, 1, TILES, 8, 128), lambda step: (0, step % 2, 0, step // 2, 0)),
         out_shape=jax.ShapeDtypeStruct((32, 2, TILES, 24, 128), jnp.float32),
+        scratch_shapes=[pltpu.VMEM((N, 8 * N), jnp.float32)],
         compiler_params=pltpu.CompilerParams(vmem_limit_bytes=32 * 1024 * 1024),
         cost_estimate=COST,
         name="filter",

time: 389 us -> 389 us (level)
  no operation moved by 1% of the time
where the time goes in v8:
time: 389 us; the launch traced here: 388 us
  blocking collectives  185 us (48%)
  waiting for transfers between devices  98 us (25%)
  Pallas kernels  50 us (13%)
  starting transfers between devices  40.7 us (10%)
  between operations  13.7 us (4%)
    all_to_all x3, blocking collectives, exchange_plane(): return lax.all_to_all(blocks, PLANE, 0, 0, tiled=True)  156 us
    all_to_all x4, waiting for transfers between devices, exchange_plane(): return lax.all_to_all(blocks, PLANE, 0, 0, tiled=True)  39.6 us
    all_gather x1, waiting for transfers between devices, shards(): halves.append(lax.all_gather(second, 'z', axis=0, tiled=False))  33.8 us
    all_to_all x1, blocking collectives, exchange_z(): return lax.all_to_all(blocks, 'z', 0, 0, tiled=True)  29.4 us
    all_to_all x4, starting transfers between devices, exchange_plane(): return lax.all_to_all(blocks, PLANE, 0, 0, tiled=True)  24.8 us
    ppermute x7, waiting for transfers between devices, gather_orbital(): lax.ppermute(piece, 'z', [(z, (z + shift) % 8) for z in range(8)])  21.2 us
    ppermute x7, starting transfers between devices, gather_orbital(): lax.ppermute(piece, 'z', [(z, (z + shift) % 8) for z in range(8)])  15.8 us
    pallas_call x2, Pallas kernels, forward(): pl.pallas_call(forward_kernel, grid=(4,), in_specs=[pl.BlockSpec(memory_s...  15.2 us
  transfers between devices with their start and end apart: 13, of which 11 were waited for; matrix products, arithmetic and copies ran while one was open for 0% of the time, Pallas kernels for 6%

profile of v8, /device:TPU:1, one launch (start us, length us, event | category | flops | bytes accessed | tf_op | source)
XLA Modules:
  0.0 388.4 jit_solution(12535880852365016229)
XLA Ops:
  6.5 3.8 pack.5
  10.3 8.7 %all-to-all-start = ((f32[32,112,128]{2,1,0:T(8,128)}), f32[32,112,128]{2,1,0:T(8,128)S(1)}, u32[]{:S(2)}, u32[]{:S(2)}) async-start(f32[32,112,128]{2,1,0:T(8,128)} %pack.5), calls=%async_computation | async-start | bytes 3670016 | tf_op jit(solution)/shard_map/all_to_all | solution.py:405
  19.1 0.0 all-gather.5.cloned.1.call-start
  19.1 2.5 pack.4
  21.6 23.1 %all-to-all-done = f32[32,112,128]{2,1,0:T(8,128)S(1)} async-done(((f32[32,112,128]{2,1,0:T(8,128)}), f32[32,112,128]{2,1,0:T(8,128)S(1)}, u32[]{:S(2)}, u32[]{:S(2)}) %all-to-all-start) | async-done | bytes 1835040 | tf_op jit(solution)/shard_map/all_to_all | solution.py:405
  44.7 1.4 choose.2
  46.1 0.0 all-gather.5.cloned.1.call-update
  46.1 4.7 %all-to-all-start.1 = ((f32[32,56,128]{2,1,0:T(8,128)}), f32[32,56,128]{2,1,0:T(8,128)S(1)}, u32[]{:S(2)}, u32[]{:S(2)}) async-start(f32[32,56,128]{2,1,0:T(8,128)} %pack.4), calls=%async_computation.1 | async-start | bytes 1835008 | tf_op jit(solution)/shard_map/all_to_all | solution.py:405
  50.8 0.0 copy-start.17
  50.8 3.8 pack.3
  54.6 11.8 %all-to-all-done.1 = f32[32,56,128]{2,1,0:T(8,128)S(1)} async-done(((f32[32,56,128]{2,1,0:T(8,128)}), f32[32,56,128]{2,1,0:T(8,128)S(1)}, u32[]{:S(2)}, u32[]{:S(2)}) %all-to-all-start.1) | async-done | bytes 917536 | tf_op jit(solution)/shard_map/all_to_all | solution.py:405
  66.4 3.8 all-to-all-start.2
  70.3 0.0 all-gather.7.cloned.1.call-start
  70.4 0.7 slots.1
  71.1 7.0 %collective-permute-start = (f32[24,1152]{1,0:T(8,128)S(1)}, f32[24,1152]{1,0:T(8,128)S(1)}, u32[]{:S(2)}, u32[]{:S(2)}) collective-permute-start(f32[24,1152]{1,0:T(8,128)S(1)} %get-tuple-element.36), channel_id=1, source_target_pairs={{0,8},{2,10},{4,12},{6,14},{8,0},{10,2},{12,4},{14,6},{1,9},{3,11}... | collective-permute-start | bytes 331784 | tf_op jit(solution)/shard_map/ppermute | solution.py:419
  78.1 1.6 collective-permute-start.1
  79.8 2.8 collective-permute-start.2
  82.6 1.2 collective-permute-start.3
  83.8 2.4 collective-permute-start.4
  86.2 0.7 collective-permute-start.5
  86.9 9.3 %collective-permute-done.1.refs_2_ = f32[24,1152]{1,0:T(8,128)S(1)} collective-permute-done((f32[24,1152]{1,0:T(8,128)S(1)}, f32[24,1152]{1,0:T(8,128)S(1)}, u32[]{:S(2)}, u32[]{:S(2)}) %collective-permute-start.1) | collective-permute-done | bytes 110624 | tf_op jit(solution)/shard_map/ppermute | solution.py:419
  96.2 0.0 collective-permute-start.6
  96.2 1.2 collective-permute-done.2.refs_3_
  97.4 4.5 %collective-permute-done.3.refs_4_ = f32[24,1152]{1,0:T(8,128)S(1)} collective-permute-done((f32[24,1152]{1,0:T(8,128)S(1)}, f32[24,1152]{1,0:T(8,128)S(1)}, u32[]{:S(2)}, u32[]{:S(2)}) %collective-permute-start.3) | collective-permute-done | bytes 110624 | tf_op jit(solution)/shard_map/ppermute | solution.py:419
  101.9 0.3 collective-permute-done.4.refs_5_
  102.2 4.2 %collective-permute-done.5.refs_6_ = f32[24,1152]{1,0:T(8,128)S(1)} collective-permute-done((f32[24,1152]{1,0:T(8,128)S(1)}, f32[24,1152]{1,0:T(8,128)S(1)}, u32[]{:S(2)}, u32[]{:S(2)}) %collective-permute-start.5) | collective-permute-done | bytes 110624 | tf_op jit(solution)/shard_map/ppermute | solution.py:419
  106.4 1.7 collective-permute-done.6.refs_7_
  108.1 1.4 choose.3
  109.5 0.0 all-gather.7.cloned.1.call-update
  109.6 0.1 add_add_fusion
  109.7 0.1 reshape.88
  109.8 0.6 and_select_fusion.1.slots_ref
  110.4 3.3 all-gather.5.cloned.1.call-done
  113.8 7.6 %forward.2 = f32[4,8,9,24,128]{4,3,2,1,0:T(8,128)} custom-call(s32[8]{0:T(128)} %and_select_fusion.1.slots_ref, f32[24,1152]{1,0:T(8,128)} %copy-done.3, f32[24,1152]{1,0:T(8,128)} %copy-done.9, f32[24,1152]{1,0:T(8,128)} %copy-done.10, f32[24,1152]{1,0:T(8,128)} %copy-done.11, f32[24,1152]{1,0:T(8,128)} %copy-done.12, f32[24,1152]{1,0:T(8,128)} %copy-done.13, ...), custom_call_target="tpu_custom_call" | custom-call | flops 16000000000 | bytes 10000000 | tf_op jit(solution)/shard_map/forward/pallas_call | solution.py:321
  121.4 7.6 %all-to-all-start.3 = ((f32[32,216,128]{2,1,0:T(8,128)}), f32[32,216,128]{2,1,0:T(8,128)}, u32[]{:S(2)}, u32[]{:S(2)}) async-start(f32[32,216,128]{2,1,0:T(8,128)} %bitcast.31), calls=%async_computation.3 | async-start | bytes 7077888 | tf_op jit(solution)/shard_map/all_to_all | solution.py:405
  129.0 33.8 %all-gather.7.cloned.1.call-done = f32[32,24,1152]{2,1,0:T(8,128)} async-done(((f32[4,24,1152]{2,1,0:T(8,128)}), f32[32,24,1152]{2,1,0:T(8,128)}) %all-gather.7.cloned.1.call-update) | async-done | bytes 3538960 | tf_op jit(solution)/shard_map/all_gather | solution.py:435
  162.8 7.6 %forward.3 = f32[4,8,9,24,128]{4,3,2,1,0:T(8,128)} custom-call(s32[8]{0:T(128)} %and_select_fusion.1.slots_ref, f32[24,1152]{1,0:T(8,128)} %copy-done.3, f32[24,1152]{1,0:T(8,128)} %copy-done.9, f32[24,1152]{1,0:T(8,128)} %copy-done.10, f32[24,1152]{1,0:T(8,128)} %copy-done.11, f32[24,1152]{1,0:T(8,128)} %copy-done.12, f32[24,1152]{1,0:T(8,128)} %copy-done.13, ...), custom_call_target="tpu_custom_call" | custom-call | flops 16000000000 | bytes 10000000 | tf_op jit(solution)/shard_map/forward/pallas_call | solution.py:321
  170.4 4.7 %all-to-all-done.3 = f32[32,216,128]{2,1,0:T(8,128)} async-done(((f32[32,216,128]{2,1,0:T(8,128)}), f32[32,216,128]{2,1,0:T(8,128)}, u32[]{:S(2)}, u32[]{:S(2)}) %all-to-all-start.3) | async-done | bytes 3538976 | tf_op jit(solution)/shard_map/all_to_all | solution.py:405
  175.2 50.3 %all_to_all.40 = f32[32,216,128]{2,1,0:T(8,128)S(1)} all-to-all(f32[32,216,128]{2,1,0:T(8,128)} %bitcast.32), channel_id=1, replica_groups=mesh['x_lo'=2,'y'=4,'x_hi'=2,'z'=8,'core'=2] {'x_lo','y','x_hi','core'}, dimensions={0} | all-to-all | bytes 7077888 | tf_op jit(solution)/shard_map/all_to_all | solution.py:405
  225.4 10.4 %filter.1 = f32[32,2,9,24,128]{4,3,2,1,0:T(8,128)S(1)} custom-call(f32[32,9,24,128]{3,2,1,0:T(8,128)} %bitcast.5.first_ref, f32[32,9,24,128]{3,2,1,0:T(8,128)S(1)} %bitcast.23, f32[3,1,1536]{2,1,0:T(1,128)S(1)} %reshape.89.pair_ref, f32[192,1]{1,0:T(8,128)S(1)} %fusion.2.wave_ref, bf16[192,576]{1,0:T(8,128)(2,1)S(1)} %copy-done.8, bf16[192,576]{1,0:T(8,128)(2,1)S(1)} %copy-done.7), custom_call_target="tpu_custom_call" | custom-call | flops 16000000000 | bytes 10000000 | tf_op jit(solution)/shard_map/filter/pallas_call | solution.py:370
  235.9 0.0 copy-start.4
  235.9 0.0 copy-start.5
  235.9 0.0 copy-start.6
  235.9 85.5 %all_to_all.41 = f32[32,432,128]{2,1,0:T(8,128)S(1)} all-to-all(f32[32,432,128]{2,1,0:T(8,128)S(1)} %bitcast.20), channel_id=1, replica_groups=mesh['x_lo'=2,'y'=4,'x_hi'=2,'z'=8,'core'=2] {'x_lo','y','x_hi','core'}, dimensions={0} | all-to-all | bytes 14155776 | tf_op jit(solution)/shard_map/all_to_all | solution.py:405
  321.5 9.4 %inverse.1 = f32[8,224,128]{2,1,0:T(8,128)S(1)} custom-call(f32[4,8,2,9,24,128]{5,4,3,2,1,0:T(8,128)S(1)} %bitcast.21, f32[8,4,24,1152]{3,2,1,0:T(8,128)S(1)} %bitcast.25, f32[8,4,24,1152]{3,2,1,0:T(8,128)S(1)} %bitcast.27, bf16[768,256]{1,0:T(8,128)(2,1)S(1)} %copy-done.4, bf16[768,256]{1,0:T(8,128)(2,1)S(1)} %copy-done.5, bf16[192,576]{1,0:T(8,128)(2,1)S(1)} %copy-done.6), custom_call_target="tpu_custom_call" | custom-call | flops 16000000000 | bytes 10000000 | tf_op jit(solution)/shard_map/inverse/pallas_call | solution.py:346
  330.9 29.4 %all_to_all.42 = f32[8,224,128]{2,1,0:T(8,128)S(1)} all-to-all(f32[8,224,128]{2,1,0:T(8,128)S(1)} %inverse.1), channel_id=1, replica_groups=mesh['x_lo'=2,'y'=4,'x_hi'=2,'z'=8,'core'=2] {'z'}, dimensions={0} | all-to-all | bytes 1835008 | tf_op jit(solution)/shard_map/all_to_all | solution.py:409
  360.3 20.0 %all_to_all.43.blocks_ref = f32[32,56,128]{2,1,0:T(8,128)S(1)} all-to-all(f32[32,56,128]{2,1,0:T(8,128)S(1)} %bitcast.30), channel_id=1, replica_groups=mesh['x_lo'=2,'y'=4,'x_hi'=2,'z'=8,'core'=2] {'x_lo','y','x_hi','core'}, dimensions={0} | all-to-all | bytes 1835008 | tf_op jit(solution)/shard_map/all_to_all | solution.py:405
  380.3 1.3 unpack.1
  (43 shorter events, 0.2 us)
Async XLA Ops:
  10.3 34.3 %copy-start = (s32[2]{0:T(128)S(1)}, s32[2]{0:T(128)}, u32[]{:S(2)}) copy-start(s32[2]{0:T(128)} %owner_ref.3) | copy-start | bytes 28
  10.3 34.3 %all-to-all-start = ((f32[32,112,128]{2,1,0:T(8,128)}), f32[32,112,128]{2,1,0:T(8,128)S(1)}, u32[]{:S(2)}, u32[]{:S(2)}) async-start(f32[32,112,128]{2,1,0:T(8,128)} %pack.5), calls=%async_computation | async-start | bytes 3670016 | tf_op jit(solution)/shard_map/all_to_all | solution.py:405
  19.1 94.7 %all-gather.5.cloned.1.call-start = ((), (), s32[]{:S(2)}) async-start(), calls=%async_computation.8 | async-start | bytes 3981312 | tf_op jit(solution)/shard_map/all_gather | solution.py:429
  46.1 20.3 %all-to-all-start.1 = ((f32[32,56,128]{2,1,0:T(8,128)}), f32[32,56,128]{2,1,0:T(8,128)S(1)}, u32[]{:S(2)}, u32[]{:S(2)}) async-start(f32[32,56,128]{2,1,0:T(8,128)} %pack.4), calls=%async_computation.1 | async-start | bytes 1835008 | tf_op jit(solution)/shard_map/all_to_all | solution.py:405
  50.8 19.6 %copy-start.17 = (s32[8]{0:T(128)S(1)}, s32[8]{0:T(128)}, u32[]{:S(2)}) copy-start(s32[8]{0:T(128)} %constant.80.clone) | copy-start | bytes 100
  54.6 55.2 %copy-start.16 = (s32[8]{0:T(128)S(1)}, s32[8]{0:T(128)}, u32[]{:S(2)}) copy-start(s32[8]{0:T(128)} %constant.90) | copy-start | bytes 100
  66.4 41.7 %all-to-all-start.2 = ((f32[32,112,128]{2,1,0:T(8,128)}), f32[32,112,128]{2,1,0:T(8,128)S(1)}, u32[]{:S(2)}, u32[]{:S(2)}) async-start(f32[32,112,128]{2,1,0:T(8,128)} %pack.3), calls=%async_computation.2 | async-start | bytes 3670016 | tf_op jit(solution)/shard_map/all_to_all | solution.py:405
  70.3 92.6 %all-gather.7.cloned.1.call-start = ((), (), s32[]{:S(2)}) async-start(), calls=%async_computation.9 | async-start | bytes 3981312 | tf_op jit(solution)/shard_map/all_gather | solution.py:435
  71.1 42.6 %copy-start.3 = (f32[24,1152]{1,0:T(8,128)}, f32[24,1152]{1,0:T(8,128)S(1)}, u32[]{:S(2)}) copy-start(f32[24,1152]{1,0:T(8,128)S(1)} %get-tuple-element.43.refs_0_) | copy-start | bytes 331780
  71.1 15.1 %collective-permute-start = (f32[24,1152]{1,0:T(8,128)S(1)}, f32[24,1152]{1,0:T(8,128)S(1)}, u32[]{:S(2)}, u32[]{:S(2)}) collective-permute-start(f32[24,1152]{1,0:T(8,128)S(1)} %get-tuple-element.36), channel_id=1, source_target_pairs={{0,8},{2,10},{4,12},{6,14},{8,0},{10,2},{12,4},{14,6},{1,9},{3,11}... | collective-permute-start | bytes 331784 | tf_op jit(solution)/shard_map/ppermute | solution.py:419
  78.1 18.1 %collective-permute-start.1 = (f32[24,1152]{1,0:T(8,128)S(1)}, f32[24,1152]{1,0:T(8,128)S(1)}, u32[]{:S(2)}, u32[]{:S(2)}) collective-permute-start(f32[24,1152]{1,0:T(8,128)S(1)} %get-tuple-element.37), channel_id=1, source_target_pairs={{0,6},{2,8},{4,10},{6,12},{8,14},{10,0},{12,2},{14,4},{1,7},{3,9},... | collective-permute-start | bytes 331784 | tf_op jit(solution)/shard_map/ppermute | solution.py:419
  79.8 17.7 %collective-permute-start.2 = (f32[24,1152]{1,0:T(8,128)S(1)}, f32[24,1152]{1,0:T(8,128)S(1)}, u32[]{:S(2)}, u32[]{:S(2)}) collective-permute-start(f32[24,1152]{1,0:T(8,128)S(1)} %get-tuple-element.38), channel_id=1, source_target_pairs={{0,10},{2,12},{4,14},{6,0},{8,2},{10,4},{12,6},{14,8},{1,11},{3,13... | collective-permute-start | bytes 331784 | tf_op jit(solution)/shard_map/ppermute | solution.py:419
  82.6 19.3 %collective-permute-start.3 = (f32[24,1152]{1,0:T(8,128)S(1)}, f32[24,1152]{1,0:T(8,128)S(1)}, u32[]{:S(2)}, u32[]{:S(2)}) collective-permute-start(f32[24,1152]{1,0:T(8,128)S(1)} %get-tuple-element.39), channel_id=1, source_target_pairs={{0,4},{2,6},{4,8},{6,10},{8,12},{10,14},{12,0},{14,2},{1,5},{3,7},... | collective-permute-start | bytes 331784 | tf_op jit(solution)/shard_map/ppermute | solution.py:419
  83.8 18.4 %collective-permute-start.4 = (f32[24,1152]{1,0:T(8,128)S(1)}, f32[24,1152]{1,0:T(8,128)S(1)}, u32[]{:S(2)}, u32[]{:S(2)}) collective-permute-start(f32[24,1152]{1,0:T(8,128)S(1)} %get-tuple-element.40), channel_id=1, source_target_pairs={{0,12},{2,14},{4,0},{6,2},{8,4},{10,6},{12,8},{14,10},{1,13},{3,15... | collective-permute-start | bytes 331784 | tf_op jit(solution)/shard_map/ppermute | solution.py:419
  86.2 27.6 %copy-start.9 = (f32[24,1152]{1,0:T(8,128)}, f32[24,1152]{1,0:T(8,128)S(1)}, u32[]{:S(2)}) copy-start(f32[24,1152]{1,0:T(8,128)S(1)} %collective-permute-done.refs_1_) | copy-start | bytes 331780
  86.2 20.2 %collective-permute-start.5 = (f32[24,1152]{1,0:T(8,128)S(1)}, f32[24,1152]{1,0:T(8,128)S(1)}, u32[]{:S(2)}, u32[]{:S(2)}) collective-permute-start(f32[24,1152]{1,0:T(8,128)S(1)} %get-tuple-element.41), channel_id=1, source_target_pairs={{0,2},{2,4},{4,6},{6,8},{8,10},{10,12},{12,14},{14,0},{1,3},{3,5},... | collective-permute-start | bytes 331784 | tf_op jit(solution)/shard_map/ppermute | solution.py:419
  96.2 17.6 %copy-start.10 = (f32[24,1152]{1,0:T(8,128)}, f32[24,1152]{1,0:T(8,128)S(1)}, u32[]{:S(2)}) copy-start(f32[24,1152]{1,0:T(8,128)S(1)} %collective-permute-done.1.refs_2_) | copy-start | bytes 331780
  96.2 11.9 %collective-permute-start.6 = (f32[24,1152]{1,0:T(8,128)S(1)}, f32[24,1152]{1,0:T(8,128)S(1)}, u32[]{:S(2)}, u32[]{:S(2)}) collective-permute-start(f32[24,1152]{1,0:T(8,128)S(1)} %get-tuple-element.42), channel_id=1, source_target_pairs={{0,14},{2,0},{4,2},{6,4},{8,6},{10,8},{12,10},{14,12},{1,15},{3,1}... | collective-permute-start | bytes 331784 | tf_op jit(solution)/shard_map/ppermute | solution.py:419
  97.4 16.3 %copy-start.11 = (f32[24,1152]{1,0:T(8,128)}, f32[24,1152]{1,0:T(8,128)S(1)}, u32[]{:S(2)}) copy-start(f32[24,1152]{1,0:T(8,128)S(1)} %collective-permute-done.2.refs_3_) | copy-start | bytes 331780
  101.9 11.8 %copy-start.12 = (f32[24,1152]{1,0:T(8,128)}, f32[24,1152]{1,0:T(8,128)S(1)}, u32[]{:S(2)}) copy-start(f32[24,1152]{1,0:T(8,128)S(1)} %collective-permute-done.3.refs_4_) | copy-start | bytes 331780
  102.2 11.5 %copy-start.13 = (f32[24,1152]{1,0:T(8,128)}, f32[24,1152]{1,0:T(8,128)S(1)}, u32[]{:S(2)}) copy-start(f32[24,1152]{1,0:T(8,128)S(1)} %collective-permute-done.4.refs_5_) | copy-start | bytes 331780
  106.4 7.4 %copy-start.14 = (f32[24,1152]{1,0:T(8,128)}, f32[24,1152]{1,0:T(8,128)S(1)}, u32[]{:S(2)}) copy-start(f32[24,1152]{1,0:T(8,128)S(1)} %collective-permute-done.5.refs_6_) | copy-start | bytes 331780
  108.1 5.7 %copy-start.15 = (f32[24,1152]{1,0:T(8,128)}, f32[24,1152]{1,0:T(8,128)S(1)}, u32[]{:S(2)}) copy-start(f32[24,1152]{1,0:T(8,128)S(1)} %collective-permute-done.6.refs_7_) | copy-start | bytes 331780
  121.4 53.7 %all-to-all-start.3 = ((f32[32,216,128]{2,1,0:T(8,128)}), f32[32,216,128]{2,1,0:T(8,128)}, u32[]{:S(2)}, u32[]{:S(2)}) async-start(f32[32,216,128]{2,1,0:T(8,128)} %bitcast.31), calls=%async_computation.3 | async-start | bytes 7077888 | tf_op jit(solution)/shard_map/all_to_all | solution.py:405
  175.1 50.3 %copy-start.7 = (bf16[192,576]{1,0:T(8,128)(2,1)S(1)}, bf16[192,576]{1,0:T(8,128)(2,1)}, u32[]{:S(2)}) copy-start(bf16[192,576]{1,0:T(8,128)(2,1)} %constant.85.clone.refs_1_) | copy-start | bytes 663556
  175.2 50.3 %copy-start.8 = (bf16[192,576]{1,0:T(8,128)(2,1)S(1)}, bf16[192,576]{1,0:T(8,128)(2,1)}, u32[]{:S(2)}) copy-start(bf16[192,576]{1,0:T(8,128)(2,1)} %constant.84.clone.refs_0_) | copy-start | bytes 663556
  235.8 85.6 %copy-start.1 = (f32[32,24,1152]{2,1,0:T(8,128)S(1)}, f32[32,24,1152]{2,1,0:T(8,128)}, u32[]{:S(2)}) copy-start(f32[32,24,1152]{2,1,0:T(8,128)} %all-gather.5.cloned.1.call-done) | copy-start | bytes 10616836
  235.8 85.6 %copy-start.2 = (f32[32,24,1152]{2,1,0:T(8,128)S(1)}, f32[32,24,1152]{2,1,0:T(8,128)}, u32[]{:S(2)}) copy-start(f32[32,24,1152]{2,1,0:T(8,128)} %all-gather.7.cloned.1.call-done) | copy-start | bytes 10616836
  235.9 85.6 %copy-start.4 = (bf16[768,256]{1,0:T(8,128)(2,1)S(1)}, bf16[768,256]{1,0:T(8,128)(2,1)}, u32[]{:S(2)}) copy-start(bf16[768,256]{1,0:T(8,128)(2,1)} %constant.81.clone.refs_9_.even_ref) | copy-start | bytes 1179652
  235.9 85.6 %copy-start.5 = (bf16[768,256]{1,0:T(8,128)(2,1)S(1)}, bf16[768,256]{1,0:T(8,128)(2,1)}, u32[]{:S(2)}) copy-start(bf16[768,256]{1,0:T(8,128)(2,1)} %constant.86.clone.odd_ref) | copy-start | bytes 1179652
  235.9 85.6 %copy-start.6 = (bf16[192,576]{1,0:T(8,128)(2,1)S(1)}, bf16[192,576]{1,0:T(8,128)(2,1)}, u32[]{:S(2)}) copy-start(bf16[192,576]{1,0:T(8,128)(2,1)} %constant.87.clone.rows_ref) | copy-start | bytes 663556
Sparse Core Ops, SparseCore 0:
  46.2 67.4 all-gather.4
  115.5 47.2 all-gather.6

commit v9 on v7

--- a/solution.py
+++ b/solution.py
@@ -139,11 +139,14 @@
         for slot, piece_ref in enumerate(piece_refs):
             orbital_ref[slots_ref[slot]] = piece_ref[...]
 
-    pair = orbital_ref[...].reshape(N, LANES) * band_ref[:, 0].reshape(N, LANES)
-    spectrum = lane_transform(pair, even_ref, odd_ref)
+    orbital = orbital_ref[...].reshape(N, LANES)
+    pairs = [orbital * band_ref[:, pair].reshape(N, LANES) for pair in range(2)]
+    spectrum = lane_transform(jnp.concatenate(pairs, axis=1), even_ref, odd_ref)
     spectrum = left_product(rows_ref, spectrum)
-    for tile in range(TILES):
-        out_ref[0, :, tile] = spectrum[:, 128 * tile : 128 * tile + 128].reshape(8, 24, 128)
+    for pair in range(2):
+        for tile in range(TILES):
+            start = LANES * pair + 128 * tile
+            out_ref[pair, :, tile] = spectrum[:, start : start + 128].reshape(8, 24, 128)
 
 
 def inverse_kernel(spectrum_ref, first_ref, last_ref, even_ref, odd_ref, rows_ref, out_ref, total_ref):
@@ -251,8 +254,8 @@
 
 PARAMS = pltpu.CompilerParams(vmem_limit_bytes=VMEM)
 COST = pl.CostEstimate(flops=16 * 10**9, bytes_accessed=10**7, transcendentals=0)
-BANDS = pl.BlockSpec((8, 1, 24, LANES), lambda step: (0, step, 0, 0))
-SPECTRA = pl.BlockSpec((1, 8, TILES, 24, 128), lambda step: (step, 0, 0, 0, 0))
+BANDS = pl.BlockSpec((8, 2, 24, LANES), lambda step: (0, step, 0, 0))
+SPECTRA = pl.BlockSpec((2, 8, TILES, 24, 128), lambda step: (step, 0, 0, 0, 0))
 
 
 MOVES = pltpu.CompilerParams(vmem_limit_bytes=16 * 1024 * 1024)
@@ -318,7 +321,7 @@
     rows = stacked_terms(cas_matrix()[:, held_order()])
     return pl.pallas_call(
         forward_kernel,
-        grid=(4,),
+        grid=(2,),
         in_specs=[
             pl.BlockSpec(memory_space=pltpu.SMEM),
             *[whole(piece) for piece in pieces],

time: 389 us -> 389 us (level)
  no operation moved by 1% of the time
where the time goes in v9:
time: 389 us; the launch traced here: 388 us
  blocking collectives  185 us (48%)
  waiting for transfers between devices  98.6 us (25%)
  Pallas kernels  48.9 us (13%)
  starting transfers between devices  40.7 us (10%)
  between operations  13.7 us (4%)
    all_to_all x3, blocking collectives, exchange_plane(): return lax.all_to_all(blocks, PLANE, 0, 0, tiled=True)  156 us
    all_to_all x4, waiting for transfers between devices, exchange_plane(): return lax.all_to_all(blocks, PLANE, 0, 0, tiled=True)  39.6 us
    all_gather x1, waiting for transfers between devices, shards(): halves.append(lax.all_gather(second, 'z', axis=0, tiled=False))  34.4 us
    all_to_all x1, blocking collectives, exchange_z(): return lax.all_to_all(blocks, 'z', 0, 0, tiled=True)  29.4 us
    all_to_all x4, starting transfers between devices, exchange_plane(): return lax.all_to_all(blocks, PLANE, 0, 0, tiled=True)  24.8 us
    ppermute x7, waiting for transfers between devices, gather_orbital(): lax.ppermute(piece, 'z', [(z, (z + shift) % 8) for z in range(8)])  21.2 us
    ppermute x7, starting transfers between devices, gather_orbital(): lax.ppermute(piece, 'z', [(z, (z + shift) % 8) for z in range(8)])  15.8 us
    pallas_call x2, Pallas kernels, forward(): pl.pallas_call(forward_kernel, grid=(2,), in_specs=[pl.BlockSpec(memory_s...  14 us
  transfers between devices with their start and end apart: 13, of which 11 were waited for; matrix products, arithmetic and copies ran while one was open for 0% of the time, Pallas kernels for 6%

profile of v9, /device:TPU:1, one launch (start us, length us, event | category | flops | bytes accessed | tf_op | source)
XLA Modules:
  0.0 387.9 jit_solution(10455112874749715134)
XLA Ops:
  6.5 3.8 pack.5
  10.3 8.7 %all-to-all-start = ((f32[32,112,128]{2,1,0:T(8,128)}), f32[32,112,128]{2,1,0:T(8,128)S(1)}, u32[]{:S(2)}, u32[]{:S(2)}) async-start(f32[32,112,128]{2,1,0:T(8,128)} %pack.5), calls=%async_computation | async-start | bytes 3670016 | tf_op jit(solution)/shard_map/all_to_all | solution.py:405
  19.1 0.0 all-gather.5.cloned.1.call-start
  19.1 2.5 pack.4
  21.6 23.1 %all-to-all-done = f32[32,112,128]{2,1,0:T(8,128)S(1)} async-done(((f32[32,112,128]{2,1,0:T(8,128)}), f32[32,112,128]{2,1,0:T(8,128)S(1)}, u32[]{:S(2)}, u32[]{:S(2)}) %all-to-all-start) | async-done | bytes 1835040 | tf_op jit(solution)/shard_map/all_to_all | solution.py:405
  44.7 1.4 choose.2
  46.1 0.0 all-gather.5.cloned.1.call-update
  46.1 4.7 %all-to-all-start.1 = ((f32[32,56,128]{2,1,0:T(8,128)}), f32[32,56,128]{2,1,0:T(8,128)S(1)}, u32[]{:S(2)}, u32[]{:S(2)}) async-start(f32[32,56,128]{2,1,0:T(8,128)} %pack.4), calls=%async_computation.1 | async-start | bytes 1835008 | tf_op jit(solution)/shard_map/all_to_all | solution.py:405
  50.8 0.0 copy-start.17
  50.8 3.8 pack.3
  54.6 11.8 %all-to-all-done.1 = f32[32,56,128]{2,1,0:T(8,128)S(1)} async-done(((f32[32,56,128]{2,1,0:T(8,128)}), f32[32,56,128]{2,1,0:T(8,128)S(1)}, u32[]{:S(2)}, u32[]{:S(2)}) %all-to-all-start.1) | async-done | bytes 917536 | tf_op jit(solution)/shard_map/all_to_all | solution.py:405
  66.4 3.8 all-to-all-start.2
  70.3 0.0 all-gather.7.cloned.1.call-start
  70.4 0.7 slots.1
  71.1 7.0 %collective-permute-start = (f32[24,1152]{1,0:T(8,128)S(1)}, f32[24,1152]{1,0:T(8,128)S(1)}, u32[]{:S(2)}, u32[]{:S(2)}) collective-permute-start(f32[24,1152]{1,0:T(8,128)S(1)} %get-tuple-element.36), channel_id=1, source_target_pairs={{0,8},{2,10},{4,12},{6,14},{8,0},{10,2},{12,4},{14,6},{1,9},{3,11}... | collective-permute-start | bytes 331784 | tf_op jit(solution)/shard_map/ppermute | solution.py:419
  78.1 1.6 collective-permute-start.1
  79.8 2.8 collective-permute-start.2
  82.6 1.2 collective-permute-start.3
  83.8 2.4 collective-permute-start.4
  86.2 0.7 collective-permute-start.5
  86.9 9.3 %collective-permute-done.1.refs_2_ = f32[24,1152]{1,0:T(8,128)S(1)} collective-permute-done((f32[24,1152]{1,0:T(8,128)S(1)}, f32[24,1152]{1,0:T(8,128)S(1)}, u32[]{:S(2)}, u32[]{:S(2)}) %collective-permute-start.1) | collective-permute-done | bytes 110624 | tf_op jit(solution)/shard_map/ppermute | solution.py:419
  96.2 0.0 collective-permute-start.6
  96.2 1.2 collective-permute-done.2.refs_3_
  97.4 4.5 %collective-permute-done.3.refs_4_ = f32[24,1152]{1,0:T(8,128)S(1)} collective-permute-done((f32[24,1152]{1,0:T(8,128)S(1)}, f32[24,1152]{1,0:T(8,128)S(1)}, u32[]{:S(2)}, u32[]{:S(2)}) %collective-permute-start.3) | collective-permute-done | bytes 110624 | tf_op jit(solution)/shard_map/ppermute | solution.py:419
  101.9 0.3 collective-permute-done.4.refs_5_
  102.2 4.2 %collective-permute-done.5.refs_6_ = f32[24,1152]{1,0:T(8,128)S(1)} collective-permute-done((f32[24,1152]{1,0:T(8,128)S(1)}, f32[24,1152]{1,0:T(8,128)S(1)}, u32[]{:S(2)}, u32[]{:S(2)}) %collective-permute-start.5) | collective-permute-done | bytes 110624 | tf_op jit(solution)/shard_map/ppermute | solution.py:419
  106.4 1.7 collective-permute-done.6.refs_7_
  108.1 1.4 choose.3
  109.5 0.0 all-gather.7.cloned.1.call-update
  109.6 0.1 add_add_fusion
  109.7 0.1 reshape.88
  109.8 0.6 and_select_fusion.1.slots_ref
  110.4 3.3 all-gather.5.cloned.1.call-done
  113.8 7.0 %forward.2 = f32[4,8,9,24,128]{4,3,2,1,0:T(8,128)} custom-call(s32[8]{0:T(128)} %and_select_fusion.1.slots_ref, f32[24,1152]{1,0:T(8,128)} %copy-done.3, f32[24,1152]{1,0:T(8,128)} %copy-done.9, f32[24,1152]{1,0:T(8,128)} %copy-done.10, f32[24,1152]{1,0:T(8,128)} %copy-done.11, f32[24,1152]{1,0:T(8,128)} %copy-done.12, f32[24,1152]{1,0:T(8,128)} %copy-done.13, ...), custom_call_target="tpu_custom_call" | custom-call | flops 16000000000 | bytes 10000000 | tf_op jit(solution)/shard_map/forward/pallas_call | solution.py:322
  120.8 7.6 %all-to-all-start.3 = ((f32[32,216,128]{2,1,0:T(8,128)}), f32[32,216,128]{2,1,0:T(8,128)}, u32[]{:S(2)}, u32[]{:S(2)}) async-start(f32[32,216,128]{2,1,0:T(8,128)} %bitcast.31), calls=%async_computation.3 | async-start | bytes 7077888 | tf_op jit(solution)/shard_map/all_to_all | solution.py:405
  128.4 34.4 %all-gather.7.cloned.1.call-done = f32[32,24,1152]{2,1,0:T(8,128)} async-done(((f32[4,24,1152]{2,1,0:T(8,128)}), f32[32,24,1152]{2,1,0:T(8,128)}) %all-gather.7.cloned.1.call-update) | async-done | bytes 3538960 | tf_op jit(solution)/shard_map/all_gather | solution.py:435
  162.8 7.0 %forward.3 = f32[4,8,9,24,128]{4,3,2,1,0:T(8,128)} custom-call(s32[8]{0:T(128)} %and_select_fusion.1.slots_ref, f32[24,1152]{1,0:T(8,128)} %copy-done.3, f32[24,1152]{1,0:T(8,128)} %copy-done.9, f32[24,1152]{1,0:T(8,128)} %copy-done.10, f32[24,1152]{1,0:T(8,128)} %copy-done.11, f32[24,1152]{1,0:T(8,128)} %copy-done.12, f32[24,1152]{1,0:T(8,128)} %copy-done.13, ...), custom_call_target="tpu_custom_call" | custom-call | flops 16000000000 | bytes 10000000 | tf_op jit(solution)/shard_map/forward/pallas_call | solution.py:322
  169.8 4.7 %all-to-all-done.3 = f32[32,216,128]{2,1,0:T(8,128)} async-done(((f32[32,216,128]{2,1,0:T(8,128)}), f32[32,216,128]{2,1,0:T(8,128)}, u32[]{:S(2)}, u32[]{:S(2)}) %all-to-all-start.3) | async-done | bytes 3538976 | tf_op jit(solution)/shard_map/all_to_all | solution.py:405
  174.5 50.3 %all_to_all.40 = f32[32,216,128]{2,1,0:T(8,128)S(1)} all-to-all(f32[32,216,128]{2,1,0:T(8,128)} %bitcast.32), channel_id=1, replica_groups=mesh['x_lo'=2,'y'=4,'x_hi'=2,'z'=8,'core'=2] {'x_lo','y','x_hi','core'}, dimensions={0} | all-to-all | bytes 7077888 | tf_op jit(solution)/shard_map/all_to_all | solution.py:405
  224.8 10.5 %filter.1 = f32[32,2,9,24,128]{4,3,2,1,0:T(8,128)S(1)} custom-call(f32[32,9,24,128]{3,2,1,0:T(8,128)} %bitcast.5.first_ref, f32[32,9,24,128]{3,2,1,0:T(8,128)S(1)} %bitcast.23, f32[3,1,1536]{2,1,0:T(1,128)S(1)} %reshape.89.refs_0_, f32[192,1]{1,0:T(8,128)S(1)} %fusion.2.refs_1_, bf16[192,576]{1,0:T(8,128)(2,1)S(1)} %copy-done.8, bf16[192,576]{1,0:T(8,128)(2,1)S(1)} %copy-done.7), custom_call_target="tpu_custom_call" | custom-call | flops 16000000000 | bytes 10000000 | tf_op jit(solution)/shard_map/filter/pallas_call | solution.py:371
  235.4 0.0 copy-start.4
  235.4 0.0 copy-start.5
  235.4 0.0 copy-start.6
  235.4 85.5 %all_to_all.41 = f32[32,432,128]{2,1,0:T(8,128)S(1)} all-to-all(f32[32,432,128]{2,1,0:T(8,128)S(1)} %bitcast.20), channel_id=1, replica_groups=mesh['x_lo'=2,'y'=4,'x_hi'=2,'z'=8,'core'=2] {'x_lo','y','x_hi','core'}, dimensions={0} | all-to-all | bytes 14155776 | tf_op jit(solution)/shard_map/all_to_all | solution.py:405
  321.0 9.4 %inverse.1 = f32[8,224,128]{2,1,0:T(8,128)S(1)} custom-call(f32[4,8,2,9,24,128]{5,4,3,2,1,0:T(8,128)S(1)} %bitcast.21, f32[8,4,24,1152]{3,2,1,0:T(8,128)S(1)} %bitcast.25, f32[8,4,24,1152]{3,2,1,0:T(8,128)S(1)} %bitcast.27, bf16[768,256]{1,0:T(8,128)(2,1)S(1)} %copy-done.4, bf16[768,256]{1,0:T(8,128)(2,1)S(1)} %copy-done.5, bf16[192,576]{1,0:T(8,128)(2,1)S(1)} %copy-done.6), custom_call_target="tpu_custom_call" | custom-call | flops 16000000000 | bytes 10000000 | tf_op jit(solution)/shard_map/inverse/pallas_call | solution.py:347
  330.4 29.4 %all_to_all.42 = f32[8,224,128]{2,1,0:T(8,128)S(1)} all-to-all(f32[8,224,128]{2,1,0:T(8,128)S(1)} %inverse.1), channel_id=1, replica_groups=mesh['x_lo'=2,'y'=4,'x_hi'=2,'z'=8,'core'=2] {'z'}, dimensions={0} | all-to-all | bytes 1835008 | tf_op jit(solution)/shard_map/all_to_all | solution.py:409
  359.8 20.0 %all_to_all.43.blocks_ref = f32[32,56,128]{2,1,0:T(8,128)S(1)} all-to-all(f32[32,56,128]{2,1,0:T(8,128)S(1)} %bitcast.30), channel_id=1, replica_groups=mesh['x_lo'=2,'y'=4,'x_hi'=2,'z'=8,'core'=2] {'x_lo','y','x_hi','core'}, dimensions={0} | all-to-all | bytes 1835008 | tf_op jit(solution)/shard_map/all_to_all | solution.py:405
  379.8 1.3 unpack.1
  (43 shorter events, 0.2 us)
Async XLA Ops:
  10.3 34.3 %copy-start = (s32[2]{0:T(128)S(1)}, s32[2]{0:T(128)}, u32[]{:S(2)}) copy-start(s32[2]{0:T(128)} %owner_ref.3) | copy-start | bytes 28
  10.3 34.3 %all-to-all-start = ((f32[32,112,128]{2,1,0:T(8,128)}), f32[32,112,128]{2,1,0:T(8,128)S(1)}, u32[]{:S(2)}, u32[]{:S(2)}) async-start(f32[32,112,128]{2,1,0:T(8,128)} %pack.5), calls=%async_computation | async-start | bytes 3670016 | tf_op jit(solution)/shard_map/all_to_all | solution.py:405
  19.1 94.7 %all-gather.5.cloned.1.call-start = ((), (), s32[]{:S(2)}) async-start(), calls=%async_computation.8 | async-start | bytes 3981312 | tf_op jit(solution)/shard_map/all_gather | solution.py:429
  46.1 20.3 %all-to-all-start.1 = ((f32[32,56,128]{2,1,0:T(8,128)}), f32[32,56,128]{2,1,0:T(8,128)S(1)}, u32[]{:S(2)}, u32[]{:S(2)}) async-start(f32[32,56,128]{2,1,0:T(8,128)} %pack.4), calls=%async_computation.1 | async-start | bytes 1835008 | tf_op jit(solution)/shard_map/all_to_all | solution.py:405
  50.8 19.6 %copy-start.17 = (s32[8]{0:T(128)S(1)}, s32[8]{0:T(128)}, u32[]{:S(2)}) copy-start(s32[8]{0:T(128)} %constant.80.clone) | copy-start | bytes 100
  54.6 55.2 %copy-start.16 = (s32[8]{0:T(128)S(1)}, s32[8]{0:T(128)}, u32[]{:S(2)}) copy-start(s32[8]{0:T(128)} %constant.90) | copy-start | bytes 100
  66.4 41.7 %all-to-all-start.2 = ((f32[32,112,128]{2,1,0:T(8,128)}), f32[32,112,128]{2,1,0:T(8,128)S(1)}, u32[]{:S(2)}, u32[]{:S(2)}) async-start(f32[32,112,128]{2,1,0:T(8,128)} %pack.3), calls=%async_computation.2 | async-start | bytes 3670016 | tf_op jit(solution)/shard_map/all_to_all | solution.py:405
  70.3 92.6 %all-gather.7.cloned.1.call-start = ((), (), s32[]{:S(2)}) async-start(), calls=%async_computation.9 | async-start | bytes 3981312 | tf_op jit(solution)/shard_map/all_gather | solution.py:435
  71.1 42.6 %copy-start.3 = (f32[24,1152]{1,0:T(8,128)}, f32[24,1152]{1,0:T(8,128)S(1)}, u32[]{:S(2)}) copy-start(f32[24,1152]{1,0:T(8,128)S(1)} %get-tuple-element.43.refs_0_) | copy-start | bytes 331780
  71.1 15.1 %collective-permute-start = (f32[24,1152]{1,0:T(8,128)S(1)}, f32[24,1152]{1,0:T(8,128)S(1)}, u32[]{:S(2)}, u32[]{:S(2)}) collective-permute-start(f32[24,1152]{1,0:T(8,128)S(1)} %get-tuple-element.36), channel_id=1, source_target_pairs={{0,8},{2,10},{4,12},{6,14},{8,0},{10,2},{12,4},{14,6},{1,9},{3,11}... | collective-permute-start | bytes 331784 | tf_op jit(solution)/shard_map/ppermute | solution.py:419
  78.1 18.1 %collective-permute-start.1 = (f32[24,1152]{1,0:T(8,128)S(1)}, f32[24,1152]{1,0:T(8,128)S(1)}, u32[]{:S(2)}, u32[]{:S(2)}) collective-permute-start(f32[24,1152]{1,0:T(8,128)S(1)} %get-tuple-element.37), channel_id=1, source_target_pairs={{0,6},{2,8},{4,10},{6,12},{8,14},{10,0},{12,2},{14,4},{1,7},{3,9},... | collective-permute-start | bytes 331784 | tf_op jit(solution)/shard_map/ppermute | solution.py:419
  79.8 17.7 %collective-permute-start.2 = (f32[24,1152]{1,0:T(8,128)S(1)}, f32[24,1152]{1,0:T(8,128)S(1)}, u32[]{:S(2)}, u32[]{:S(2)}) collective-permute-start(f32[24,1152]{1,0:T(8,128)S(1)} %get-tuple-element.38), channel_id=1, source_target_pairs={{0,10},{2,12},{4,14},{6,0},{8,2},{10,4},{12,6},{14,8},{1,11},{3,13... | collective-permute-start | bytes 331784 | tf_op jit(solution)/shard_map/ppermute | solution.py:419
  82.6 19.3 %collective-permute-start.3 = (f32[24,1152]{1,0:T(8,128)S(1)}, f32[24,1152]{1,0:T(8,128)S(1)}, u32[]{:S(2)}, u32[]{:S(2)}) collective-permute-start(f32[24,1152]{1,0:T(8,128)S(1)} %get-tuple-element.39), channel_id=1, source_target_pairs={{0,4},{2,6},{4,8},{6,10},{8,12},{10,14},{12,0},{14,2},{1,5},{3,7},... | collective-permute-start | bytes 331784 | tf_op jit(solution)/shard_map/ppermute | solution.py:419
  83.8 18.4 %collective-permute-start.4 = (f32[24,1152]{1,0:T(8,128)S(1)}, f32[24,1152]{1,0:T(8,128)S(1)}, u32[]{:S(2)}, u32[]{:S(2)}) collective-permute-start(f32[24,1152]{1,0:T(8,128)S(1)} %get-tuple-element.40), channel_id=1, source_target_pairs={{0,12},{2,14},{4,0},{6,2},{8,4},{10,6},{12,8},{14,10},{1,13},{3,15... | collective-permute-start | bytes 331784 | tf_op jit(solution)/shard_map/ppermute | solution.py:419
  86.2 27.6 %copy-start.9 = (f32[24,1152]{1,0:T(8,128)}, f32[24,1152]{1,0:T(8,128)S(1)}, u32[]{:S(2)}) copy-start(f32[24,1152]{1,0:T(8,128)S(1)} %collective-permute-done.refs_1_) | copy-start | bytes 331780
  86.2 20.2 %collective-permute-start.5 = (f32[24,1152]{1,0:T(8,128)S(1)}, f32[24,1152]{1,0:T(8,128)S(1)}, u32[]{:S(2)}, u32[]{:S(2)}) collective-permute-start(f32[24,1152]{1,0:T(8,128)S(1)} %get-tuple-element.41), channel_id=1, source_target_pairs={{0,2},{2,4},{4,6},{6,8},{8,10},{10,12},{12,14},{14,0},{1,3},{3,5},... | collective-permute-start | bytes 331784 | tf_op jit(solution)/shard_map/ppermute | solution.py:419
  96.2 17.6 %copy-start.10 = (f32[24,1152]{1,0:T(8,128)}, f32[24,1152]{1,0:T(8,128)S(1)}, u32[]{:S(2)}) copy-start(f32[24,1152]{1,0:T(8,128)S(1)} %collective-permute-done.1.refs_2_) | copy-start | bytes 331780
  96.2 11.9 %collective-permute-start.6 = (f32[24,1152]{1,0:T(8,128)S(1)}, f32[24,1152]{1,0:T(8,128)S(1)}, u32[]{:S(2)}, u32[]{:S(2)}) collective-permute-start(f32[24,1152]{1,0:T(8,128)S(1)} %get-tuple-element.42), channel_id=1, source_target_pairs={{0,14},{2,0},{4,2},{6,4},{8,6},{10,8},{12,10},{14,12},{1,15},{3,1}... | collective-permute-start | bytes 331784 | tf_op jit(solution)/shard_map/ppermute | solution.py:419
  97.4 16.3 %copy-start.11 = (f32[24,1152]{1,0:T(8,128)}, f32[24,1152]{1,0:T(8,128)S(1)}, u32[]{:S(2)}) copy-start(f32[24,1152]{1,0:T(8,128)S(1)} %collective-permute-done.2.refs_3_) | copy-start | bytes 331780
  101.9 11.8 %copy-start.12 = (f32[24,1152]{1,0:T(8,128)}, f32[24,1152]{1,0:T(8,128)S(1)}, u32[]{:S(2)}) copy-start(f32[24,1152]{1,0:T(8,128)S(1)} %collective-permute-done.3.refs_4_) | copy-start | bytes 331780
  102.2 11.5 %copy-start.13 = (f32[24,1152]{1,0:T(8,128)}, f32[24,1152]{1,0:T(8,128)S(1)}, u32[]{:S(2)}) copy-start(f32[24,1152]{1,0:T(8,128)S(1)} %collective-permute-done.4.refs_5_) | copy-start | bytes 331780
  106.4 7.4 %copy-start.14 = (f32[24,1152]{1,0:T(8,128)}, f32[24,1152]{1,0:T(8,128)S(1)}, u32[]{:S(2)}) copy-start(f32[24,1152]{1,0:T(8,128)S(1)} %collective-permute-done.5.refs_6_) | copy-start | bytes 331780
  108.1 5.7 %copy-start.15 = (f32[24,1152]{1,0:T(8,128)}, f32[24,1152]{1,0:T(8,128)S(1)}, u32[]{:S(2)}) copy-start(f32[24,1152]{1,0:T(8,128)S(1)} %collective-permute-done.6.refs_7_) | copy-start | bytes 331780
  120.8 53.7 %all-to-all-start.3 = ((f32[32,216,128]{2,1,0:T(8,128)}), f32[32,216,128]{2,1,0:T(8,128)}, u32[]{:S(2)}, u32[]{:S(2)}) async-start(f32[32,216,128]{2,1,0:T(8,128)} %bitcast.31), calls=%async_computation.3 | async-start | bytes 7077888 | tf_op jit(solution)/shard_map/all_to_all | solution.py:405
  174.5 50.3 %copy-start.7 = (bf16[192,576]{1,0:T(8,128)(2,1)S(1)}, bf16[192,576]{1,0:T(8,128)(2,1)}, u32[]{:S(2)}) copy-start(bf16[192,576]{1,0:T(8,128)(2,1)} %constant.85.clone.refs_3_) | copy-start | bytes 663556
  174.5 50.3 %copy-start.8 = (bf16[192,576]{1,0:T(8,128)(2,1)S(1)}, bf16[192,576]{1,0:T(8,128)(2,1)}, u32[]{:S(2)}) copy-start(bf16[192,576]{1,0:T(8,128)(2,1)} %constant.84.clone.refs_2_) | copy-start | bytes 663556
  235.3 85.6 %copy-start.1 = (f32[32,24,1152]{2,1,0:T(8,128)S(1)}, f32[32,24,1152]{2,1,0:T(8,128)}, u32[]{:S(2)}) copy-start(f32[32,24,1152]{2,1,0:T(8,128)} %all-gather.5.cloned.1.call-done) | copy-start | bytes 10616836
  235.4 85.6 %copy-start.2 = (f32[32,24,1152]{2,1,0:T(8,128)S(1)}, f32[32,24,1152]{2,1,0:T(8,128)}, u32[]{:S(2)}) copy-start(f32[32,24,1152]{2,1,0:T(8,128)} %all-gather.7.cloned.1.call-done) | copy-start | bytes 10616836
  235.4 85.6 %copy-start.4 = (bf16[768,256]{1,0:T(8,128)(2,1)S(1)}, bf16[768,256]{1,0:T(8,128)(2,1)}, u32[]{:S(2)}) copy-start(bf16[768,256]{1,0:T(8,128)(2,1)} %constant.81.clone.refs_9_.even_ref) | copy-start | bytes 1179652
  235.4 85.6 %copy-start.5 = (bf16[768,256]{1,0:T(8,128)(2,1)S(1)}, bf16[768,256]{1,0:T(8,128)(2,1)}, u32[]{:S(2)}) copy-start(bf16[768,256]{1,0:T(8,128)(2,1)} %constant.86.clone.odd_ref) | copy-start | bytes 1179652
  235.4 85.6 %copy-start.6 = (bf16[192,576]{1,0:T(8,128)(2,1)S(1)}, bf16[192,576]{1,0:T(8,128)(2,1)}, u32[]{:S(2)}) copy-start(bf16[192,576]{1,0:T(8,128)(2,1)} %constant.87.clone.rows_ref) | copy-start | bytes 663556
Sparse Core Ops, SparseCore 0:
  46.2 67.4 all-gather.4
  115.5 47.2 all-gather.6
